TPU v7x, 32 devices: a whole 2x2x4 slice. The times are simulated.
32 devices in a mesh: groups: 2 (over x), row: 16 (over z, y, core).
Axes of the slice: x: 2, y: 2, z: 4, core: 2. Of those that a mesh axis runs over, the one named last changes fastest.
Arguments:
- features: bfloat16 [128, 64, 512], P(('groups', 'row')), parts along dimension 0, may hold values from -6 to 6
- cotangent: bfloat16 [128, 64, 512], P(('groups', 'row')), parts along dimension 0, may hold values from -6 to 6
- depth_weight: bfloat16 [49, 512], P(None, 'row'), may hold values from -0.875 to 0.875
- depth_bias: bfloat16 [512], P('row'), may hold values from -3 to 3
- norm_gain: bfloat16 [512], P('row'), may hold values from 0.25 to 1.75
- norm_shift: bfloat16 [512], P('row'), may hold values from -3 to 3
- up_weight: bfloat16 [512, 2048], P('row'), may hold values from -0.25 to 0.25
- up_bias: bfloat16 [2048], P('row'), may hold values from -3 to 3
- down_weight: bfloat16 [2048, 512], P('row'), may hold values from -0.125 to 0.125
- down_bias: bfloat16 [512], P('row'), may hold values from -3 to 3
Outputs:
- block_out: bfloat16 [128, 64, 512], P(('groups', 'row')), parts along dimension 0
- grad_features: bfloat16 [128, 64, 512], P(('groups', 'row')), parts along dimension 0
- grad_up_weight: float32 [1024, 2048], P(('groups', 'row')), parts along dimension 0
- grad_down_weight: float32 [4096, 512], P(('groups', 'row')), parts along dimension 0
- grad_depth_weight: float32 [98, 512], P('groups', 'row'), parts along dimension 0
- grad_depth_bias: float32 [1024], P(('groups', 'row')), parts along dimension 0
- grad_norm_gain: float32 [1024], P(('groups', 'row')), parts along dimension 0
- grad_norm_shift: float32 [1024], P(('groups', 'row')), parts along dimension 0
- grad_up_bias: float32 [4096], P(('groups', 'row')), parts along dimension 0
- grad_down_bias: float32 [1024], P(('groups', 'row')), parts along dimension 0
There are 2 independent parts, one for each index of `groups`. A program takes and returns all parts, laid end to end along the dimension named above; an argument that names none is the same for every part. Nothing has to cross between parts.
All inputs are finite; a program needn't handle non-finite values.
Results may differ from a plain program's by a relative error of at most 0.0055.
Values may be sent and summed in bfloat16 or wider, within the bound.
No kernel may reach another device: no remote copies, remote signals or barrier semaphores. Data moves between devices by JAX's collectives and lax.ppermute only.
A program may use at most 64 MiB of HBM per device.

v0:
```python
import math

import jax
import jax.numpy as jnp
from jax import lax
from jax.sharding import PartitionSpec as P

eps = 1e-06


def with_halo(block, sides, width):
    for axis, dim in sides:
        count = lax.axis_size(axis)
        forward = [(i, i + 1) for i in range(count - 1)]
        backward = [(target, source) for source, target in forward]
        low = lax.ppermute(
            lax.slice_in_dim(block, block.shape[dim] - width, None, axis=dim), axis, forward
        )
        high = lax.ppermute(lax.slice_in_dim(block, 0, width, axis=dim), axis, backward)
        block = jnp.concatenate([low, block, high], axis=dim)
    return block


def gelu_value(value):
    return 0.5 * value * (1.0 + lax.erf(value * (1.0 / math.sqrt(2.0))))


def gelu_slope(value):
    cumulative = 0.5 * (1.0 + lax.erf(value * (1.0 / math.sqrt(2.0))))
    density = jnp.exp(-0.5 * value * value) * (1.0 / math.sqrt(2.0 * math.pi))
    return cumulative + value * density


def depth_conv(padded, kernel, height, width):
    total = jnp.zeros((height, width, kernel.shape[1]), jnp.float32)
    for first in range(7):
        for second in range(7):
            total = (
                total
                + padded[first : first + height, second : second + width, :]
                * kernel[first * 7 + second]
            )
    return total


def depth_conv_back(padded, kernel, height, width):
    total = jnp.zeros((height, width, kernel.shape[1]), jnp.float32)
    for first in range(7):
        for second in range(7):
            total = (
                total
                + padded[6 - first : 6 - first + height, 6 - second : 6 - second + width, :]
                * kernel[first * 7 + second]
            )
    return total


def per_device(
    features,
    cotangent,
    depth_weight,
    depth_bias,
    norm_gain,
    norm_shift,
    up_weight,
    up_bias,
    down_weight,
    down_bias,
):
    height, width, chans = features.shape
    devices = lax.axis_size("row")
    cells = height * width
    scale = 1.0 / math.sqrt(cells * devices)
    kernel, conv_bias, gain, shift, bias_down, bias_up = (
        lax.all_gather(depth_weight, "row", axis=1, tiled=True),
        lax.all_gather(depth_bias, "row", axis=0, tiled=True),
        lax.all_gather(norm_gain, "row", axis=0, tiled=True),
        lax.all_gather(norm_shift, "row", axis=0, tiled=True),
        lax.all_gather(down_bias, "row", axis=0, tiled=True),
        lax.all_gather(up_bias, "row", axis=0, tiled=True),
    )
    kernel = kernel.astype(jnp.float32)
    gain = gain.astype(jnp.float32)
    rimmed = with_halo(features, (("row", 0),), 3)
    padded = jnp.pad(rimmed.astype(jnp.float32), ((0, 0), (3, 3), (0, 0)))
    conv = depth_conv(padded, kernel, height, width) + conv_bias.astype(jnp.float32)
    mean_val = jnp.mean(conv, axis=2, keepdims=True)
    centered = conv - mean_val
    var_val = jnp.mean(centered * centered, axis=2, keepdims=True)
    inv = lax.rsqrt(var_val + eps)
    normed = centered * inv
    normal_out = (normed * gain + shift.astype(jnp.float32)).astype(jnp.bfloat16)
    flat_norm = normal_out.reshape(cells, chans)
    flat_cot = cotangent.reshape(cells, chans)
    columns = flat_norm
    hidden = jnp.dot(
        columns,
        lax.all_gather(up_weight, "row", axis=0, tiled=True),
        preferred_element_type=jnp.float32,
    ) + bias_up.astype(jnp.float32)
    act = gelu_value(hidden).astype(jnp.bfloat16)
    columns = act
    mixed = jnp.dot(
        columns,
        lax.all_gather(down_weight, "row", axis=0, tiled=True),
        preferred_element_type=jnp.float32,
    )
    block_out = (
        features.astype(jnp.float32)
        + (mixed + bias_down.astype(jnp.float32)).reshape(height, width, chans)
    ).astype(jnp.bfloat16)
    down_full = (
        lax.dot_general(act, flat_cot, (((0,), (0,)), ((), ())), preferred_element_type=jnp.float32)
        * scale
    )
    grad_down_weight = lax.psum_scatter(down_full, "row", scatter_dimension=0, tiled=True)
    dact = lax.dot_general(
        flat_cot,
        lax.all_gather(down_weight, "row", axis=0, tiled=True),
        (((1,), (1,)), ((), ())),
        preferred_element_type=jnp.float32,
    )
    dhidden = (dact * gelu_slope(hidden)).astype(jnp.bfloat16)
    columns = flat_norm
    grad_up_weight = lax.psum_scatter(
        lax.dot_general(
            columns, dhidden, (((0,), (0,)), ((), ())), preferred_element_type=jnp.float32
        )
        * scale,
        "row",
        scatter_dimension=0,
        tiled=True,
    )
    dnorm = lax.dot_general(
        dhidden,
        lax.all_gather(up_weight, "row", axis=0, tiled=True),
        (((1,), (1,)), ((), ())),
        preferred_element_type=jnp.float32,
    )
    dnorm = dnorm.reshape(height, width, chans)
    down_bias_term = jnp.sum(flat_cot.astype(jnp.float32), axis=0) * scale
    up_bias_term = jnp.sum(dhidden.astype(jnp.float32), axis=0) * scale
    gain_term = jnp.sum(dnorm * normed, axis=(0, 1)) * scale
    shift_term = jnp.sum(dnorm, axis=(0, 1)) * scale
    grad_down_bias, grad_up_bias, grad_norm_gain, grad_norm_shift = (
        lax.psum_scatter(down_bias_term, "row", scatter_dimension=0, tiled=True),
        lax.psum_scatter(up_bias_term, "row", scatter_dimension=0, tiled=True),
        lax.psum_scatter(gain_term, "row", scatter_dimension=0, tiled=True),
        lax.psum_scatter(shift_term, "row", scatter_dimension=0, tiled=True),
    )
    scaled = dnorm * gain
    dconv = inv * (
        scaled
        - jnp.mean(scaled, axis=2, keepdims=True)
        - normed * jnp.mean(scaled * normed, axis=2, keepdims=True)
    )
    dconv = dconv.astype(jnp.bfloat16)
    dconv_wide = dconv.astype(jnp.float32)
    back_rim = with_halo(dconv, (("row", 0),), 3)
    back_pad = jnp.pad(back_rim.astype(jnp.float32), ((0, 0), (3, 3), (0, 0)))
    grad_features = (
        cotangent.astype(jnp.float32) + depth_conv_back(back_pad, kernel, height, width)
    ).astype(jnp.bfloat16)
    taps = []
    for first in range(7):
        for second in range(7):
            taps.append(
                jnp.sum(
                    dconv_wide * padded[first : first + height, second : second + width, :],
                    axis=(0, 1),
                )
            )
    kernel_term = jnp.stack(taps, axis=0) * scale
    conv_bias_term = jnp.sum(dconv_wide, axis=(0, 1)) * scale
    grad_depth_weight, grad_depth_bias = (
        lax.psum_scatter(kernel_term, "row", scatter_dimension=1, tiled=True),
        lax.psum_scatter(conv_bias_term, "row", scatter_dimension=0, tiled=True),
    )
    return (
        block_out,
        grad_features,
        grad_up_weight,
        grad_down_weight,
        grad_depth_weight,
        grad_depth_bias,
        grad_norm_gain,
        grad_norm_shift,
        grad_up_bias,
        grad_down_bias,
    )


def solution(mesh):
    placed = (
        P(("groups", "row"), None, None),
        P(("groups", "row"), None, None),
        P(None, "row"),
        P("row"),
        P("row"),
        P("row"),
        P("row", None),
        P("row"),
        P("row", None),
        P("row"),
    )
    return jax.shard_map(
        per_device,
        mesh=mesh,
        in_specs=placed,
        out_specs=(
            P(("groups", "row"), None, None),
            P(("groups", "row"), None, None),
            P(("groups", "row"), None),
            P(("groups", "row"), None),
            P("groups", "row"),
            P(("groups", "row")),
            P(("groups", "row")),
            P(("groups", "row")),
            P(("groups", "row")),
            P(("groups", "row")),
        ),
        check_vma=False,
    )
```

profile of v0, /device:TPU:0, one launch (start us, length us, event | category | flops | bytes accessed | tf_op | source)
XLA Modules:
  0.0 335.8 jit_solution(5923359344454385601)
XLA Ops:
  7.2 0.7 all-gather.4.cloned.1.call-update
  8.0 0.7 all-gather.6.cloned.1.call-update
  8.7 1.1 fusion.148
  9.8 2.4 collective-permute-start
  12.1 1.3 collective-permute-start.1
  13.4 25.6 %all_gather.26 = bf16[49,512]{0,1:T(8,128)(2,1)S(1)} all-gather(bf16[49,32]{0,1:T(8,128)(2,1)} %param.12), channel_id=1, replica_groups=mesh['groups'=2,'row'=16] {'row'}, dimensions={1}, use_global_device_ids=true | all-gather | bytes 53312 | tf_op jit(solution)/shard_map/all_gather | solution.py:75
  39.1 2.6 slice_reduce_fusion.48
  41.8 1.6 slice_reduce_fusion.46
  43.4 0.6 fusion.149
  44.7 0.2 dynamic-update-slice
  44.9 0.2 dynamic-update-slice.1
  45.2 0.2 dynamic-update-slice.2
  45.4 0.2 dynamic-update-slice.3
  45.7 30.4 %all-reduce.12 = (bf16[512]{0:T(512)(128)(2,1)S(1)}, bf16[512]{0:T(512)(128)(2,1)S(1)}, bf16[512]{0:T(512)(128)(2,1)S(1)}, bf16[512]{0:T(512)(128)(2,1)}) all-reduce(bf16[512]{0:T(512)(128)(2,1)S(1)} %dynamic-update-slice, bf16[512]{0:T(512)(128)(2,1)S(1)} %dynamic-update-slice.2, ...), channel_id=1, replica_groups=mesh['groups'=2,'row'=16] {'row'}, use_global_device_ids=true, to_apply=%add.2 | all-reduce | flops 2048 | bytes 8192
  76.1 17.3 %all-gather = bf16[16,1,128]{2,1,0:T(2,128)(2,1)S(1)} all-gather(bf16[1,1,128]{2,1,0:T(2,128)(2,1)S(1)} %bitcast.131), channel_id=1, replica_groups=mesh['groups'=2,'row'=16] {'row'}, dimensions={0}, use_global_device_ids=true | all-gather | bytes 4352 | tf_op jit(solution)/shard_map/all_gather | solution.py:80
  93.4 2.7 slice_reduce_fusion.47
  96.4 4.7 %fusion.146 = (f32[4,64]{1,0:T(4,128)S(1)}, f32[4,64,512]{2,1,0:T(8,128)S(1)}) fusion(f32[512]{0:T(512)S(1)} %convert_element_type.62, f32[512]{0:T(512)S(1)} %get-tuple-element.85, f32[512]{0:T(512)S(1)} %get-tuple-element.86, f32[512]{0:T(512)S(1)} %get-tuple-element.87, f32[512]{0:T(512)S(1)} %get-tuple-element.88, ...), kind=kLoop, calls=%fused_computation.368 | loop fusion | flops 12975872 | bytes 5608448 | tf_op jit(solution)/shard_map/reduce_sum | solution.py:87
  101.4 0.2 multiply_reduce_fusion.3
  101.6 0.2 add_convert_fusion.1
  101.8 3.8 %multiply_convert_fusion = (bf16[256,2048]{1,0:T(8,128)(2,1)S(1)}, f32[256,2048]{1,0:T(8,128)}) fusion(f32[2048]{0:T(1024)S(1)} %bitcast.81, bf16[256,512]{1,0:T(8,128)(2,1)S(1)} %bitcast.75, bf16[512,2048]{1,0:T(8,128)(2,1)} %all-gather.4.cloned.1.call-done), kind=kOutput, calls=%fused_computation.61 | convolution fusion | flops 540016640 | bytes 5513216 | tf_op jit(solution)/shard_map/dot_general | solution.py:96
  105.6 4.2 %convert_reduce_fusion.1 = (f32[2048]{0:T(1024)}, bf16[256,2048]{1,0:T(8,128)(2,1)S(1)}) fusion(f32[256,2048]{1,0:T(8,128)} %get-tuple-element.152, bf16[256,512]{1,0:T(8,128)(2,1)} %bitcast.77, bf16[2048,512]{1,0:T(8,128)(2,1)} %all-gather.6.cloned.1.call-done), kind=kOutput, calls=%fused_computation.60 | convolution fusion | flops 543160320 | bytes 5513216 | tf_op jit(solution)/shard_map/dot_general | solution.py:117
  109.8 1.3 fusion.145
  111.2 0.8 copy-done
  112.0 0.8 multiply_reduce_fusion
  112.8 0.6 broadcast_multiply_fusion.6
  113.4 0.7 div.17
  114.0 3.2 fusion.143
  117.2 1.4 fusion.142
  118.7 1.0 fusion.144
  119.9 2.3 stack.199
  122.2 0.9 copy.22
  123.1 0.3 reduce-scatter.6.cloned.1.call-start
  123.4 3.9 %convolution_multiply_fusion.1 = f32[512,2048]{1,0:T(8,128)} fusion(bf16[256,512]{1,0:T(8,128)(2,1)S(1)} %bitcast.76, bf16[256,2048]{1,0:T(8,128)(2,1)} %copy-done.6), kind=kOutput, calls=%fused_computation.51 | convolution fusion | flops 537919488 | bytes 5505024 | tf_op jit(solution)/shard_map/dot_general | solution.py:126
  127.4 0.9 copy-done.4
  128.2 2.7 convolution_multiply_fusion
  132.5 59.3 %all-reduce.11 = (f32[512]{0:T(512)S(1)}, f32[512]{0:T(512)S(1)}, f32[512]{0:T(512)S(1)}, f32[2048]{0:T(1024)S(1)}, f32[512]{0:T(512)S(1)}) all-reduce(f32[512]{0:T(512)S(1)} %broadcast_multiply_fusion.5, f32[512]{0:T(512)S(1)} %get-tuple-element.157, ...), channel_id=5, replica_groups=mesh['groups'=2,'row'=16] {'row'}, use_global_device_ids=true, to_apply=%region_57.58.clone | all-reduce | flops 4096 | bytes 32768
  191.8 0.6 dynamic-slice.13
  192.4 0.6 dynamic-slice.9
  193.0 0.6 dynamic-slice.7
  193.6 0.6 dynamic-slice.5
  194.2 1.3 collective-permute-start.2
  195.5 1.3 collective-permute-start.3
  196.8 0.6 dynamic-slice.11
  197.4 2.4 convolution_add_fusion.1
  200.0 0.8 add_convert_fusion
  201.0 4.7 %fusion.5 = bf16[4,64,512]{2,1,0:T(8,128)(2,1)} fusion(bf16[4,64,512]{2,1,0:T(8,128)(2,1)S(1)} %copy-done.4, f32[10,64,512]{2,1,0:T(8,128)S(1)} %maximum_convert_fusion.1, f32[512]{0:T(512)S(1)} %get-tuple-element.85, f32[512]{0:T(512)S(1)} %get-tuple-element.86, f32[512]{0:T(512)S(1)} %get-tuple-element.87, f32[512]{0:T(512)S(1)} %get-tuple-element.88, ...), kind=kLoop, calls=%fused_computation.152 | loop fusion | flops 13107200 | bytes 5605376 | tf_op jit(solution)/shard_map/convert_element_type | solution.py:163
  205.7 47.4 %reduce-scatter.6.cloned.1.call-done = f32[32,2048]{1,0:T(8,128)} async-done(((f32[512,2048]{1,0:T(8,128)}), f32[32,2048]{1,0:T(8,128)}) %reduce-scatter.6.cloned.1.call-update) | async-done | bytes 262160 | tf_op jit(solution)/shard_map/reduce_scatter | solution.py:125
  253.1 76.1 %reduce-scatter.8.cloned.1.call-done = f32[128,512]{1,0:T(8,128)} async-done(((f32[2048,512]{1,0:T(8,128)}), f32[128,512]{1,0:T(8,128)}) %reduce-scatter.8.cloned.1.call-update) | async-done | bytes 262160 | tf_op jit(solution)/shard_map/reduce_scatter | solution.py:116
  (174 shorter events, 0.9 us)
Async XLA Ops:
  7.2 94.6 %all-gather.4.cloned.1.call-start = ((), (), s32[]{:S(2)}) async-start(), calls=%async_computation.3 | async-start | bytes 2228224 | tf_op jit(solution)/shard_map/all_gather | solution.py:98
  7.9 97.7 %all-gather.6.cloned.1.call-start = ((), (), s32[]{:S(2)}) async-start(), calls=%async_computation.4 | async-start | bytes 2228224 | tf_op jit(solution)/shard_map/all_gather | solution.py:105
  8.7 197.0 %reduce-scatter.10.cloned.1.call-start = ((), (), s32[]{:S(2)}) async-start(), calls=%async_computation.7 | async-start | bytes 278528
  9.8 86.5 %collective-permute-start = (bf16[3,64,512]{2,1,0:T(8,128)(2,1)S(1)}, bf16[3,64,512]{2,1,0:T(8,128)(2,1)S(1)}, u32[]{:S(2)}, u32[]{:S(2)}) collective-permute-start(bf16[3,64,512]{2,1,0:T(8,128)(2,1)S(1)} %get-tuple-element.147), channel_id=1, source_target_pairs={{0,1},{1,2},{2,3},{3,4},{4,5},{5,6},{6,7},{7,8},{8,9},{9,10},{10,1... | collective-permute-start | bytes 589832 | tf_op jit(solution)/shard_map/ppermute | solution.py:16
  12.1 84.2 %collective-permute-start.1 = (bf16[3,64,512]{2,1,0:T(8,128)(2,1)S(1)}, bf16[3,64,512]{2,1,0:T(8,128)(2,1)S(1)}, u32[]{:S(2)}, u32[]{:S(2)}) collective-permute-start(bf16[3,64,512]{2,1,0:T(8,128)(2,1)S(1)} %get-tuple-element.148), channel_id=1, source_target_pairs={{1,0},{2,1},{3,2},{4,3},{5,4},{6,5},{7,6},{8,7},{9,8},{10,9},{11,1... | collective-permute-start | bytes 589832 | tf_op jit(solution)/shard_map/ppermute | solution.py:19
  41.7 1.7 copy-start.62
  41.7 2.9 copy-start.66
  41.7 3.2 copy-start.67
  41.7 3.4 %copy-start.68 = (bf16[32]{0:T(256)(128)(2,1)S(1)}, bf16[32]{0:T(256)(128)(2,1)}, u32[]{:S(2)}) copy-start(bf16[32]{0:T(256)(128)(2,1)} %param.15) | copy-start | bytes 196
  41.8 3.7 %copy-start.69 = (bf16[32]{0:T(256)(128)(2,1)S(1)}, bf16[32]{0:T(256)(128)(2,1)}, u32[]{:S(2)}) copy-start(bf16[32]{0:T(256)(128)(2,1)} %param.19) | copy-start | bytes 196
  41.8 34.3 %copy-start.65 = (bf16[128]{0:T(256)(128)(2,1)S(1)}, bf16[128]{0:T(256)(128)(2,1)}, u32[]{:S(2)}) copy-start(bf16[128]{0:T(256)(128)(2,1)} %param.17) | copy-start | bytes 772
  93.4 2.9 copy-start.1
  96.1 5.0 %copy-start.7 = (f32[512]{0:T(512)}, f32[512]{0:T(512)S(1)}, u32[]{:S(2)}) copy-start(f32[512]{0:T(512)S(1)} %get-tuple-element.104) | copy-start | bytes 6148
  96.1 5.0 %copy-start.9 = (f32[512]{0:T(512)}, f32[512]{0:T(512)S(1)}, u32[]{:S(2)}) copy-start(f32[512]{0:T(512)S(1)} %get-tuple-element.105) | copy-start | bytes 6148
  96.1 5.0 %copy-start.11 = (f32[512]{0:T(512)}, f32[512]{0:T(512)S(1)}, u32[]{:S(2)}) copy-start(f32[512]{0:T(512)S(1)} %get-tuple-element.106) | copy-start | bytes 6148
  96.2 5.0 %copy-start.13 = (f32[512]{0:T(512)}, f32[512]{0:T(512)S(1)}, u32[]{:S(2)}) copy-start(f32[512]{0:T(512)S(1)} %get-tuple-element.107) | copy-start | bytes 6148
  96.2 5.0 %copy-start.15 = (f32[512]{0:T(512)}, f32[512]{0:T(512)S(1)}, u32[]{:S(2)}) copy-start(f32[512]{0:T(512)S(1)} %get-tuple-element.108) | copy-start | bytes 6148
  96.2 5.0 %copy-start.17 = (f32[512]{0:T(512)}, f32[512]{0:T(512)S(1)}, u32[]{:S(2)}) copy-start(f32[512]{0:T(512)S(1)} %get-tuple-element.109) | copy-start | bytes 6148
  96.2 5.0 %copy-start.19 = (f32[512]{0:T(512)}, f32[512]{0:T(512)S(1)}, u32[]{:S(2)}) copy-start(f32[512]{0:T(512)S(1)} %get-tuple-element.110) | copy-start | bytes 6148
  96.2 5.0 %copy-start.21 = (f32[512]{0:T(512)}, f32[512]{0:T(512)S(1)}, u32[]{:S(2)}) copy-start(f32[512]{0:T(512)S(1)} %get-tuple-element.111) | copy-start | bytes 6148
  96.2 5.0 %copy-start.23 = (f32[512]{0:T(512)}, f32[512]{0:T(512)S(1)}, u32[]{:S(2)}) copy-start(f32[512]{0:T(512)S(1)} %get-tuple-element.112) | copy-start | bytes 6148
  96.2 5.0 %copy-start.25 = (f32[512]{0:T(512)}, f32[512]{0:T(512)S(1)}, u32[]{:S(2)}) copy-start(f32[512]{0:T(512)S(1)} %get-tuple-element.113) | copy-start | bytes 6148
  96.2 5.0 %copy-start.27 = (f32[512]{0:T(512)}, f32[512]{0:T(512)S(1)}, u32[]{:S(2)}) copy-start(f32[512]{0:T(512)S(1)} %get-tuple-element.114) | copy-start | bytes 6148
  96.2 5.0 %copy-start.29 = (f32[512]{0:T(512)}, f32[512]{0:T(512)S(1)}, u32[]{:S(2)}) copy-start(f32[512]{0:T(512)S(1)} %get-tuple-element.115) | copy-start | bytes 6148
  96.2 5.0 %copy-start.31 = (f32[512]{0:T(512)}, f32[512]{0:T(512)S(1)}, u32[]{:S(2)}) copy-start(f32[512]{0:T(512)S(1)} %get-tuple-element.116) | copy-start | bytes 6148
  96.3 5.0 %copy-start.33 = (f32[512]{0:T(512)}, f32[512]{0:T(512)S(1)}, u32[]{:S(2)}) copy-start(f32[512]{0:T(512)S(1)} %get-tuple-element.117) | copy-start | bytes 6148
  96.3 5.0 %copy-start.35 = (f32[512]{0:T(512)}, f32[512]{0:T(512)S(1)}, u32[]{:S(2)}) copy-start(f32[512]{0:T(512)S(1)} %get-tuple-element.118) | copy-start | bytes 6148
  96.3 5.0 %copy-start.37 = (f32[512]{0:T(512)}, f32[512]{0:T(512)S(1)}, u32[]{:S(2)}) copy-start(f32[512]{0:T(512)S(1)} %get-tuple-element.119) | copy-start | bytes 6148
  96.3 5.0 %copy-start.39 = (f32[512]{0:T(512)}, f32[512]{0:T(512)S(1)}, u32[]{:S(2)}) copy-start(f32[512]{0:T(512)S(1)} %get-tuple-element.120) | copy-start | bytes 6148
  96.3 5.0 %copy-start.41 = (f32[512]{0:T(512)}, f32[512]{0:T(512)S(1)}, u32[]{:S(2)}) copy-start(f32[512]{0:T(512)S(1)} %get-tuple-element.121) | copy-start | bytes 6148
  101.7 3.9 %copy-start.2 = (bf16[4,64,512]{2,1,0:T(8,128)(2,1)}, bf16[4,64,512]{2,1,0:T(8,128)(2,1)S(1)}, u32[]{:S(2)}) copy-start(bf16[4,64,512]{2,1,0:T(8,128)(2,1)S(1)} %add_convert_fusion.1) | copy-start | bytes 786436
  105.6 4.2 %copy-start.5 = (bf16[512,2048]{1,0:T(8,128)(2,1)S(1)}, bf16[512,2048]{1,0:T(8,128)(2,1)}, u32[]{:S(2)}) copy-start(bf16[512,2048]{1,0:T(8,128)(2,1)} %all-gather.4.cloned.1.call-done) | copy-start | bytes 6291460
  109.8 2.9 copy-start.6
  118.6 1.2 copy-start.48
  118.6 1.2 copy-start.49
  118.6 1.2 copy-start.50
  118.6 1.2 copy-start.51
  118.6 1.2 copy-start.52
  118.7 4.7 %copy-start.3 = (bf16[4,64,512]{2,1,0:T(8,128)(2,1)S(1)}, bf16[4,64,512]{2,1,0:T(8,128)(2,1)}, u32[]{:S(2)}) copy-start(bf16[4,64,512]{2,1,0:T(8,128)(2,1)} %copy-done.2) | copy-start | bytes 786436
  123.1 130.0 %reduce-scatter.6.cloned.1.call-start = ((), (), s32[]{:S(2)}) async-start(), calls=%async_computation.5 | async-start | bytes 4456448 | tf_op jit(solution)/shard_map/reduce_scatter | solution.py:125
  127.3 201.9 %reduce-scatter.8.cloned.1.call-start = ((), (), s32[]{:S(2)}) async-start(), calls=%async_computation.6 | async-start | bytes 4456448 | tf_op jit(solution)/shard_map/reduce_scatter | solution.py:116
  131.0 1.3 copy-start.64
  131.0 1.4 copy-start.61
  131.0 1.5 copy-start.59
  131.0 1.5 copy-start.63
  131.0 1.5 copy-start.60
  194.2 6.6 %collective-permute-start.2 = (bf16[3,64,512]{2,1,0:T(8,128)(2,1)S(1)}, bf16[3,64,512]{2,1,0:T(8,128)(2,1)S(1)}, u32[]{:S(2)}, u32[]{:S(2)}) collective-permute-start(bf16[3,64,512]{2,1,0:T(8,128)(2,1)S(1)} %get-tuple-element.145), channel_id=1, source_target_pairs={{0,1},{1,2},{2,3},{3,4},{4,5},{5,6},{6,7},{7,8},{8,9},{9,10},{10,1... | collective-permute-start | bytes 589832 | tf_op jit(solution)/shard_map/ppermute | solution.py:16
  195.5 5.3 %collective-permute-start.3 = (bf16[3,64,512]{2,1,0:T(8,128)(2,1)S(1)}, bf16[3,64,512]{2,1,0:T(8,128)(2,1)S(1)}, u32[]{:S(2)}, u32[]{:S(2)}) collective-permute-start(bf16[3,64,512]{2,1,0:T(8,128)(2,1)S(1)} %get-tuple-element.146), channel_id=1, source_target_pairs={{1,0},{2,1},{3,2},{4,3},{5,4},{6,5},{7,6},{8,7},{9,8},{10,9},{11,1... | collective-permute-start | bytes 589832 | tf_op jit(solution)/shard_map/ppermute | solution.py:19
  (31 other events, 34.3 us)
Sparse Core Ops, SparseCore 0:
  10.2 44.1 all-gather.3
  56.5 40.2 all-gather.5
  123.2 54.0 reduce-scatter.9
  181.6 71.4 reduce-scatter.5
  257.9 71.3 reduce-scatter.7
where the time goes:
time: 336 us
  blocking collectives  133 us (40%)
  waiting for transfers between devices  125 us (37%)
  matrix products  18.4 us (5%)
  local copies, waits for them, and re-layouts  18.3 us (5%)
  other arithmetic  17.8 us (5%)
  between operations  16.9 us (5%)
  starting transfers between devices  6.67 us (2%)
    unnamed x2, blocking collectives  89.8 us
    reduce_scatter x1, waiting for transfers between devices, per_device(): lax.psum_scatter(down_full, 'row', scatter_dimension=0, tiled=True)  76.1 us
    reduce_scatter x1, waiting for transfers between devices, per_device(): lax.psum_scatter(lax.dot_general(columns, dhidden, (((0,), (0,)), ((), ()...  47.4 us
    all_gather x1, blocking collectives, per_device(): lax.all_gather(depth_weight, 'row', axis=1, tiled=True)  25.6 us
    all_gather x1, blocking collectives, per_device(): lax.all_gather(up_bias, 'row', axis=0, tiled=True)  17.3 us
    unnamed x155, local copies, waits for them, and re-layouts  7.34 us
    slice x3, local copies, waits for them, and re-layouts, depth_conv(): kernel[first * 7 + second]  6.92 us
  transfers between devices with their start and end apart: 9, of which 2 were waited for; matrix products, arithmetic and copies ran while one was open for 11% of the time, Pallas kernels for 0%

commit v1 on v0

v1 whole, which is shorter than its diff:
```python
import functools
import math

import jax
import jax.numpy as jnp
from jax import lax
from jax.experimental import pallas as pl
from jax.experimental.pallas import tpu as pltpu
from jax.sharding import PartitionSpec as P

eps = 1e-06
lanes = 128
taps = 49
f32 = jnp.float32
bf16 = jnp.bfloat16
row_bias, row_gain, row_shift, row_down, row_up = 49, 50, 51, 52, 53


def round_up(value, unit):
    return (value + unit - 1) // unit * unit


def call(kernel, outs, args, scratch=(), mib=24, flops=1_000_000, moved=1_000_000):
    return pl.pallas_call(
        kernel,
        out_shape=[jax.ShapeDtypeStruct(shape, dtype) for shape, dtype in outs],
        in_specs=[pl.BlockSpec(memory_space=pltpu.VMEM)] * len(args),
        out_specs=[pl.BlockSpec(memory_space=pltpu.VMEM)] * len(outs),
        scratch_shapes=list(scratch),
        compiler_params=pltpu.CompilerParams(vmem_limit_bytes=mib * 1024 * 1024),
        cost_estimate=pl.CostEstimate(flops=flops, bytes_accessed=moved, transcendentals=0),
    )(*args)


def place(quads):
    index = lax.axis_index("row")
    return index // quads, lax.rem(index, quads)


def one_hot(rows, columns, offset):
    down = lax.broadcasted_iota(jnp.int32, (rows, columns), 0)
    across = lax.broadcasted_iota(jnp.int32, (rows, columns), 1)
    return (across == down + offset).astype(f32)


def pack_kernel(quads, layers, rows, dw, db, gain, shift, down, upb, up, *rest):
    packs, held = rest[:-1], rest[-1]
    layer, member = place(quads)
    own = dw.shape[1]
    width = packs[0].shape[1]
    part = upb.shape[1]
    held[...] = jnp.zeros_like(held)
    held[0:taps, :] = dw[...].astype(f32)
    held[row_bias : row_bias + 1, :] = db[...].astype(f32)
    held[row_gain : row_gain + 1, :] = gain[...].astype(f32)
    held[row_shift : row_shift + 1, :] = shift[...].astype(f32)
    held[row_down : row_down + 1, :] = down[...].astype(f32)
    spread = one_hot(own, width, lax.axis_index("row") * own).astype(bf16)
    small = jnp.dot(held[...].astype(bf16), spread, preferred_element_type=f32)
    along = one_hot(part, width, layer * part).astype(bf16)
    bias = jnp.dot(
        jnp.broadcast_to(upb[...], (8, part)).astype(bf16), along, preferred_element_type=f32
    )
    at = lax.broadcasted_iota(jnp.int32, (rows, width), 0)
    small = small + jnp.where(at == row_up + member, bias[0:1, :], 0.0)
    small = small.astype(bf16)
    wide = [up[:, i * part : (i + 1) * part] for i in range(layers * quads)]
    for other, pack in enumerate(packs):
        partner = jnp.bitwise_xor(member, other)
        pack[0:rows, :] = small
        if pack.shape[0] != rows + own or width != layers * part:
            pack[rows:, :] = jnp.zeros((pack.shape[0] - rows, width), bf16)
        for z in range(layers):
            piece = wide[z * quads]
            for s in range(1, quads):
                piece = jnp.where(partner == s, wide[z * quads + s], piece)
            pack[rows : rows + own, z * part : (z + 1) * part] = piece


def unpack_kernel(quads, rows, own, *refs):
    packs, (small, up) = refs[:-2], refs[-2:]
    _, member = place(quads)
    total = packs[0][0:rows, :].astype(f32)
    for pack in packs[1:]:
        total = total + pack[0:rows, :].astype(f32)
    small[...] = total.astype(bf16)
    for other, pack in enumerate(packs):
        block = pack[rows:, :].astype(f32)[0:own, 0 : up.shape[2]]
        up[jnp.bitwise_xor(member, other)] = block.astype(bf16)


def fill(padded, blocks, width):
    height = blocks[1].shape[0]
    rows, columns, chans = padded.shape
    zero = jnp.zeros((rows, 8, chans), f32)
    padded[:, 0:8, :] = zero
    padded[:, 8 + width :, :] = jnp.zeros((rows, columns - 8 - width, chans), f32)
    padded[0:3, 8 : 8 + width, :] = blocks[0][height - 3 :, :, :].astype(f32)
    padded[3 : 3 + height, 8 : 8 + width, :] = blocks[1][...].astype(f32)
    padded[3 + height :, 8 : 8 + width, :] = blocks[2][0:3, :, :].astype(f32)


def slide(padded, weights, height, width, at, flip):
    sums = [jnp.zeros((width, lanes), f32) for _ in range(height)]
    for second in range(7):
        for row in range(height + 6):
            piece = padded[row, 5 + second : 5 + second + width, at]
            for out in range(height):
                first = row - out
                if 0 <= first < 7:
                    tap = first * 7 + second
                    tap = taps - 1 - tap if flip else tap
                    sums[out] = sums[out] + piece * weights[tap : tap + 1, at]
    return sums


def conv_kernel(features, low, high, *refs):
    smalls, (normal, normed, inv, params, padded, conv) = refs[:-6], refs[-6:]
    height, width, chans = features.shape
    total = smalls[0][...].astype(f32)
    for small in smalls[1:]:
        total = total + small[...].astype(f32)
    params[...] = total
    fill(padded, (low, features, high), width)

    def chunk(i, carry):
        at = pl.ds(pl.multiple_of(i * lanes, lanes), lanes)
        sums = slide(padded, params, height, width, at, False)
        for out in range(height):
            conv[out * width : (out + 1) * width, at] = (
                sums[out] + params[row_bias : row_bias + 1, at]
            )
        return carry

    lax.fori_loop(0, chans // lanes, chunk, 0)

    def norm(i, carry):
        at = pl.ds(pl.multiple_of(i * width, width), width)
        value = conv[at, :]
        centered = value - jnp.mean(value, axis=1, keepdims=True)
        var = jnp.mean(centered * centered, axis=1, keepdims=True)
        scale = lax.rsqrt(var + eps)
        value = centered * scale
        normed[at, :] = value
        inv[at, :] = jnp.broadcast_to(scale, (width, lanes))
        normal[at, :] = (
            value * params[row_gain : row_gain + 1, 0:chans]
            + params[row_shift : row_shift + 1, 0:chans]
        ).astype(bf16)
        return carry

    lax.fori_loop(0, height, norm, 0)


def back_kernel(dconv, low, high, cotangent, params, out, padded):
    height, width, chans = dconv.shape
    fill(padded, (low, dconv, high), width)

    def chunk(i, carry):
        at = pl.ds(pl.multiple_of(i * lanes, lanes), lanes)
        sums = slide(padded, params, height, width, at, True)
        for row in range(height):
            out[row, :, at] = (cotangent[row, :, at].astype(f32) + sums[row]).astype(bf16)
        return carry

    lax.fori_loop(0, chans // lanes, chunk, 0)


def taps_kernel(
    quads, layers, scale, dconv, features, low, high, cotangent, norms, upb, *refs
):
    outs, (padded, grads) = refs[:-2], refs[-2:]
    height, width, chans = dconv.shape
    layer, member = place(quads)
    fill(padded, (low, features, high), width)
    grads[...] = jnp.zeros_like(grads)

    def fold(value):
        return jnp.sum(value.reshape(width // 8, 8, lanes), axis=0)

    def chunk(i, carry):
        at = pl.ds(pl.multiple_of(i * lanes, lanes), lanes)
        own = [dconv[row, :, at].astype(f32) for row in range(height)]
        for second in range(7):
            sums = [jnp.zeros((8, lanes), f32) for _ in range(7)]
            for row in range(height + 6):
                piece = padded[row, 5 + second : 5 + second + width, at]
                for out in range(height):
                    first = row - out
                    if 0 <= first < 7:
                        sums[first] = sums[first] + fold(own[out] * piece)
            for first in range(7):
                tap = first * 7 + second
                grads[tap : tap + 1, at] = (
                    jnp.sum(sums[first], axis=0, keepdims=True) * scale
                )
        total = fold(own[0])
        for row in range(1, height):
            total = total + fold(own[row])
        grads[row_bias : row_bias + 1, at] = jnp.sum(total, axis=0, keepdims=True) * scale
        total = fold(cotangent[0, :, at].astype(f32))
        for row in range(1, height):
            total = total + fold(cotangent[row, :, at].astype(f32))
        grads[row_down : row_down + 1, at] = jnp.sum(total, axis=0, keepdims=True) * scale
        grads[row_gain : row_gain + 1, at] = norms[0:1, at] * scale
        grads[row_shift : row_shift + 1, at] = norms[1:2, at] * scale
        return carry

    lax.fori_loop(0, chans // lanes, chunk, 0)
    part = upb.shape[1] // layers
    for z in range(layers):
        bias = upb[0:1, z * part : (z + 1) * part] * scale
        for s in range(quads):
            grads[row_up + s : row_up + s + 1, z * lanes : z * lanes + part] = jnp.where(
                member == s, bias, 0.0
            )
    for step, out in enumerate(outs):
        to = lax.rem(layer + step, layers)
        out[...] = grads[:, pl.ds(pl.multiple_of(to * lanes, lanes), lanes)]


def mlp_kernel(quads, layers, scale, params, *refs):
    normals, refs = refs[:quads], refs[quads:]
    cots, refs = refs[:quads], refs[quads:]
    ups, refs = refs[:layers], refs[layers:]
    downs, refs = refs[:layers], refs[layers:]
    grad_ups, refs = refs[:layers], refs[layers:]
    dnorms, refs = refs[:quads], refs[quads:]
    act, upb, down, up, total = refs
    layer, member = place(quads)
    cells, chans = normals[0].shape
    hidden_units = act.shape[1]
    part = hidden_units // layers
    for step in range(layers):
        source = lax.rem(layer - step + layers, layers)
        up[pl.ds(pl.multiple_of(source * lanes, lanes), lanes), :] = ups[step][...]
        down[pl.ds(pl.multiple_of(source * part, part), part), :] = downs[step][...]
    bias = params[row_up : row_up + 1, 0:hidden_units]
    for s in range(1, quads):
        bias = jnp.where(member == s, params[row_up + s : row_up + s + 1, 0:hidden_units], bias)
    bias_sum = jnp.zeros((1, hidden_units), f32)
    for i in range(quads):
        hidden = jnp.dot(normals[i][...], up[...], preferred_element_type=f32) + bias
        dact = lax.dot_general(
            cots[i][...], down[...], (((1,), (1,)), ((), ())), preferred_element_type=f32
        )
        cumulative = 0.5 * (1.0 + lax.erf(hidden * (1.0 / math.sqrt(2.0))))
        density = jnp.exp(-0.5 * hidden * hidden) * (1.0 / math.sqrt(2.0 * math.pi))
        act[i * cells : (i + 1) * cells, :] = (hidden * cumulative).astype(bf16)
        dhidden = (dact * (cumulative + hidden * density)).astype(bf16)
        bias_sum = bias_sum + jnp.sum(dhidden.astype(f32), axis=0, keepdims=True)
        dnorm = lax.dot_general(
            dhidden, up[...], (((1,), (1,)), ((), ())), preferred_element_type=f32
        )
        dnorms[i][...] = dnorm.astype(dnorms[i].dtype)
        grad = lax.dot_general(
            normals[i][...], dhidden, (((0,), (0,)), ((), ())), preferred_element_type=f32
        )
        total[...] = grad if i == 0 else total[...] + grad
    upb[...] = jnp.broadcast_to(bias_sum, upb.shape)
    for step, out in enumerate(grad_ups):
        to = lax.rem(layer + step, layers)
        piece = total[pl.ds(pl.multiple_of(to * lanes, lanes), lanes), :] * scale
        out[...] = piece.astype(out.dtype)


def out_kernel(quads, layers, scale, act, down, *refs):
    cots, refs = refs[:quads], refs[quads:]
    grad_downs, refs = refs[:layers], refs[layers:]
    mixed, total = refs[:quads], refs[quads]
    layer, _ = place(quads)
    cells = cots[0].shape[0]
    part = down.shape[0] // layers
    for i in range(quads):
        block = act[i * cells : (i + 1) * cells, :]
        grad = lax.dot_general(
            block, cots[i][...], (((0,), (0,)), ((), ())), preferred_element_type=f32
        )
        total[...] = grad if i == 0 else total[...] + grad
    for step, out in enumerate(grad_downs):
        to = lax.rem(layer + step, layers)
        piece = total[pl.ds(pl.multiple_of(to * part, part), part), :] * scale
        out[...] = piece.astype(out.dtype)
    for i in range(quads):
        block = act[i * cells : (i + 1) * cells, :]
        mixed[i][...] = jnp.dot(block, down[...], preferred_element_type=f32).astype(
            mixed[i].dtype
        )


def norm_back_kernel(normed, inv, params, *refs):
    parts, (dconv, norms) = refs[:-2], refs[-2:]
    height, width, chans = dconv.shape
    gain_sum = jnp.zeros((1, chans), f32)
    shift_sum = jnp.zeros((1, chans), f32)
    for row in range(height):
        at = slice(row * width, (row + 1) * width)
        dnorm = parts[0][at, :].astype(f32)
        for part in parts[1:]:
            dnorm = dnorm + part[at, :].astype(f32)
        value = normed[at, :]
        gain_sum = gain_sum + jnp.sum(dnorm * value, axis=0, keepdims=True)
        shift_sum = shift_sum + jnp.sum(dnorm, axis=0, keepdims=True)
        scaled = dnorm * params[row_gain : row_gain + 1, 0:chans]
        mean = jnp.mean(scaled, axis=1, keepdims=True)
        cross = jnp.mean(scaled * value, axis=1, keepdims=True)
        dconv[row, :, :] = (inv[at, 0:1] * (scaled - mean - value * cross)).astype(bf16)
    norms[0:1, :] = gain_sum
    norms[1:2, :] = shift_sum


def up_split_kernel(quads, *refs):
    parts, outs = refs[:-quads], refs[-quads:]
    _, member = place(quads)
    own = outs[0].shape[0]
    total = parts[0]
    for other, out in enumerate(outs):
        row = pl.multiple_of(jnp.bitwise_xor(member, other) * own, own)
        piece = total[pl.ds(row, own), :].astype(f32)
        for part in parts[1:]:
            piece = piece + part[pl.ds(row, own), :].astype(f32)
        out[...] = piece


def up_join_kernel(quads, layers, *refs):
    pieces, out = refs[:-1], refs[-1]
    _, member = place(quads)
    part = out.shape[1] // (quads * layers)
    for s in range(quads):
        held = pieces[s][...]
        for m in range(1, quads):
            held = jnp.where(member == m, pieces[s ^ m][...], held)
        for z in range(layers):
            at = (z * quads + s) * part
            out[:, at : at + part] = held[:, z * part : (z + 1) * part]


def small_kernel(quads, part_up, *refs):
    parts, outs = refs[:-6], refs[-6:]
    _, member = place(quads)
    total = parts[0][...]
    for part in parts[1:]:
        total = total + part[...]
    own = outs[0].shape[1]
    down = lax.broadcasted_iota(jnp.int32, (lanes, own), 0)
    across = lax.broadcasted_iota(jnp.int32, (lanes, own), 1)
    pick = (down == across + member * own).astype(f32)
    mine = jnp.dot(total, pick, preferred_element_type=f32, precision=lax.Precision.HIGHEST)
    outs[0][...] = mine[0:taps, :]
    for row, out in zip((row_bias, row_gain, row_shift, row_down), outs[1:5]):
        out[...] = mine[row : row + 1, :]
    at = lax.broadcasted_iota(jnp.int32, total.shape, 0)
    chosen = jnp.where(at == row_up + member, total, 0.0)
    outs[5][...] = jnp.sum(chosen, axis=0, keepdims=True)[:, 0:part_up]


def per_device(
    features,
    cotangent,
    depth_weight,
    depth_bias,
    norm_gain,
    norm_shift,
    up_weight,
    up_bias,
    down_weight,
    down_bias,
):
    height, width, chans = features.shape
    devices = lax.axis_size("row")
    own, hidden_units = up_weight.shape
    part = down_weight.shape[0]
    layers = chans // lanes
    quads = devices // layers
    share = layers * part
    cells = height * width
    scale = 1.0 / math.sqrt(cells * devices)
    rows = round_up(row_up + quads, 16)
    pack_width = max(chans, share)

    def swap(value, other):
        return lax.ppermute(value, "row", [(i, i ^ other) for i in range(devices)])

    def turn(value, step):
        pairs = [
            (i, (i // quads + step) % layers * quads + i % quads) for i in range(devices)
        ]
        return lax.ppermute(value, "row", pairs)

    def around(value):
        return [value] + [turn(value, step) for step in range(1, layers)]

    def shift(value, step):
        pairs = [(i, i + step) for i in range(devices) if 0 <= i + step < devices]
        return lax.ppermute(value, "row", pairs)

    bits = []
    while 1 << len(bits) < quads:
        bits.append(1 << len(bits))

    def gather(value):
        held = {0: value}
        for bit in reversed(bits):
            held.update({i ^ bit: swap(block, bit) for i, block in list(held.items())})
        return [held[i] for i in range(quads)]

    def scatter(blocks):
        terms = []
        held = {i: [block] for i, block in enumerate(blocks)}
        for bit in bits:
            for i in [i for i in held if i & bit]:
                value = held.pop(i)
                value = functools.reduce(lambda a, b: a.astype(f32) + b.astype(f32), value)
                held[i ^ bit].append(swap(value.astype(bf16), bit))
        return held[0]

    downs = around(down_weight)
    shapes = [((rows + round_up(own, 16), pack_width), bf16)] * quads
    packs = call(
        functools.partial(pack_kernel, quads, layers, rows),
        shapes,
        (
            depth_weight,
            depth_bias.reshape(1, own),
            norm_gain.reshape(1, own),
            norm_shift.reshape(1, own),
            down_bias.reshape(1, own),
            up_bias.reshape(1, part),
            up_weight,
        ),
        [pltpu.VMEM((rows, own), f32)],
    )
    packs = [pack if i == 0 else swap(pack, i) for i, pack in enumerate(packs)]
    small, up = call(
        functools.partial(unpack_kernel, quads, rows, own),
        [((rows, pack_width), bf16), ((quads, own, share), bf16)],
        packs,
    )
    smalls = around(small)
    low, high = shift(features, 1), shift(features, -1)
    ups = around(up.reshape(quads * own, share))
    cots = gather(cotangent.reshape(cells, chans))

    rim = (height + 6, width + 16, chans)
    normal, normed, inv, params = call(
        conv_kernel,
        [
            ((cells, chans), bf16),
            ((cells, chans), f32),
            ((cells, lanes), f32),
            ((rows, pack_width), f32),
        ],
        (features, low, high, *smalls),
        [pltpu.VMEM(rim, f32), pltpu.VMEM((cells, chans), f32)],
        flops=20_000_000,
    )
    normals = gather(normal)

    outs = call(
        functools.partial(mlp_kernel, quads, layers, scale),
        [((lanes, share), f32)]
        + [((lanes, share), bf16)] * (layers - 1)
        + [((cells, chans), f32)]
        + [((cells, chans), bf16)] * (quads - 1)
        + [((quads * cells, share), bf16), ((8, share), f32), ((share, chans), bf16)],
        (params, *normals, *cots, *ups, *downs),
        [pltpu.VMEM((chans, share), bf16), pltpu.VMEM((chans, share), f32)],
        mib=40,
        flops=4_000_000_000,
    )
    grad_ups, dnorms = outs[:layers], outs[layers : layers + quads]
    act, upb, down_full = outs[layers + quads :]
    dnorms = scatter(dnorms)
    grad_ups = [grad_ups[0]] + [turn(grad_ups[i], i) for i in range(1, layers)]
    outs = call(
        functools.partial(out_kernel, quads, layers, scale),
        [((part, chans), f32)]
        + [((part, chans), bf16)] * (layers - 1)
        + [((cells, chans), f32)]
        + [((cells, chans), bf16)] * (quads - 1),
        (act, down_full, *cots),
        [pltpu.VMEM((share, chans), f32)],
        mib=40,
        flops=2_000_000_000,
    )
    grad_downs, mixed = outs[:layers], outs[layers:]
    grad_downs = [grad_downs[0]] + [turn(grad_downs[i], i) for i in range(1, layers)]
    mixed = scatter(mixed)

    dconv, norms = call(
        norm_back_kernel,
        [((height, width, chans), bf16), ((8, chans), f32)],
        (normed, inv, params, *dnorms),
    )
    low_back, high_back = shift(dconv, 1), shift(dconv, -1)
    grads = call(
        functools.partial(taps_kernel, quads, layers, scale),
        [((rows, lanes), f32)] * layers,
        (dconv, features, low, high, cotangent, norms, upb),
        [pltpu.VMEM(rim, f32), pltpu.VMEM((rows, chans), f32)],
        flops=20_000_000,
    )
    grads = [grads[0]] + [turn(grads[i], i) for i in range(1, layers)]
    total = functools.reduce(lambda a, b: a + b, grads)
    for bit in bits[:-1]:
        total = total + swap(total, bit)
    (grad_features,) = call(
        back_kernel,
        [((height, width, chans), bf16)],
        (dconv, low_back, high_back, cotangent, params),
        [pltpu.VMEM(rim, f32)],
        flops=20_000_000,
    )
    small_outs = call(
        functools.partial(small_kernel, quads, part),
        [((taps, own), f32)] + [((1, own), f32)] * 4 + [((1, part), f32)],
        (total, swap(total, bits[-1])),
    )
    grad_depth_weight = small_outs[0]
    grad_depth_bias, grad_norm_gain, grad_norm_shift, grad_down_bias, grad_up_bias = (
        value.reshape(-1) for value in small_outs[1:]
    )

    pieces = call(
        functools.partial(up_split_kernel, quads), [((own, share), f32)] * quads, grad_ups
    )
    pieces = [pieces[0]] + [swap(pieces[i], i) for i in range(1, quads)]
    (grad_up_weight,) = call(
        functools.partial(up_join_kernel, quads, layers), [((own, hidden_units), f32)], pieces
    )
    grad_down_weight = functools.reduce(lambda a, b: a + b.astype(f32), grad_downs)
    mixed = functools.reduce(lambda a, b: a.astype(f32) + b.astype(f32), mixed)
    block_out = (
        features.astype(f32)
        + (mixed + params[row_down, 0:chans]).reshape(height, width, chans)
    ).astype(bf16)
    return (
        block_out,
        grad_features,
        grad_up_weight,
        grad_down_weight,
        grad_depth_weight,
        grad_depth_bias,
        grad_norm_gain,
        grad_norm_shift,
        grad_up_bias,
        grad_down_bias,
    )


def solution(mesh):
    placed = (
        P(("groups", "row"), None, None),
        P(("groups", "row"), None, None),
        P(None, "row"),
        P("row"),
        P("row"),
        P("row"),
        P("row", None),
        P("row"),
        P("row", None),
        P("row"),
    )
    return jax.shard_map(
        per_device,
        mesh=mesh,
        in_specs=placed,
        out_specs=(
            P(("groups", "row"), None, None),
            P(("groups", "row"), None, None),
            P(("groups", "row"), None),
            P(("groups", "row"), None),
            P("groups", "row"),
            P(("groups", "row")),
            P(("groups", "row")),
            P(("groups", "row")),
            P(("groups", "row")),
            P(("groups", "row")),
        ),
        check_vma=False,
    )
```

time: 336 us -> 118 us (0.35)
  blocking collectives: 133 us -> 0 us
  waiting for transfers between devices: 125 us -> 43 us
  starting transfers between devices: 6.67 us -> 49.2 us
  Pallas kernels: 0 us -> 20 us
  matrix products: 18.4 us -> 0 us
  other arithmetic: 17.8 us -> 1.79 us
  between operations: 16.9 us -> 0.93 us
  local copies, waits for them, and re-layouts: 18.3 us -> 3.08 us
    reduce_scatter x2 -> x0, waiting for transfers between devices: 124 us -> none  [the longest x1 76.1 us: per_device(): lax.psum_scatter(down_full, 'row', scatter_dimension=0, tiled=True)]
    unnamed x2 -> x0, blocking collectives: 89.8 us -> none
    ppermute x4 -> x42, waiting for transfers between devices: 0.01 us -> 43 us  [the longest x18 33.4 us: turn(): return lax.ppermute(value, 'row', pairs)]
    ppermute x4 -> x42, starting transfers between devices: 6.25 us -> 49.2 us  [the longest x18 24.8 us: turn(): return lax.ppermute(value, 'row', pairs)]
    all_gather x2 -> x0, blocking collectives: 42.9 us -> none  [the longest x1 25.6 us: per_device(): lax.all_gather(depth_weight, 'row', axis=1, tiled=True)]
    pallas_call x0 -> x11, Pallas kernels: none -> 20 us  [call(): pl.pallas_call(kernel, out_shape=[jax.ShapeDtypeStruct(shape, dtype) for...]
    dot_general x6 -> x0, matrix products: 18.4 us -> none  [the longest x1 4.23 us: per_device(): lax.dot_general(flat_cot, lax.all_gather(down_weight, 'row', axis=0, tile...]
    reduce_sum x7 -> x0, other arithmetic: 11.4 us -> none  [the longest x3 5.61 us: per_device(): jnp.sum(dconv_wide * padded[first:first + height, second:second + width,...]
  transfers between devices with their start and end apart: 9 -> 42, of which waited for: 2 -> 15; matrix products, arithmetic and copies ran while one was open for 11% -> 3% of each run, Pallas kernels for 0% -> 10%
where the time goes in v1:
time: 118 us
  starting transfers between devices  49.2 us (42%)
  waiting for transfers between devices  43 us (36%)
  Pallas kernels  20 us (17%)
  local copies, waits for them, and re-layouts  3.08 us (3%)
  other arithmetic  1.79 us (2%)
    ppermute x18, waiting for transfers between devices, turn(): return lax.ppermute(value, 'row', pairs)  33.4 us
    ppermute x18, starting transfers between devices, turn(): return lax.ppermute(value, 'row', pairs)  24.8 us
    pallas_call x11, Pallas kernels, call(): pl.pallas_call(kernel, out_shape=[jax.ShapeDtypeStruct(shape, dtype) for...  20 us
    ppermute x20, starting transfers between devices, swap(): return lax.ppermute(value, 'row', [(i, i ^ other) for i in range(devices)])  18 us
    ppermute x20, waiting for transfers between devices, swap(): return lax.ppermute(value, 'row', [(i, i ^ other) for i in range(devices)])  9.65 us
    ppermute x4, starting transfers between devices, shift(): return lax.ppermute(value, 'row', pairs)  6.46 us
    unnamed x20, local copies, waits for them, and re-layouts  3.08 us
  transfers between devices with their start and end apart: 42, of which 15 were waited for; matrix products, arithmetic and copies ran while one was open for 3% of the time, Pallas kernels for 10%

profile of v1, /device:TPU:0, one launch (start us, length us, event | category | flops | bytes accessed | tf_op | source)
XLA Modules:
  0.0 118.1 jit_solution(1767263347188067451)
XLA Ops:
  0.6 2.4 %collective-permute-start = (bf16[4,64,512]{2,1,0:T(8,128)(2,1)}, bf16[4,64,512]{2,1,0:T(8,128)(2,1)S(1)}, u32[]{:S(2)}, u32[]{:S(2)}) collective-permute-start(bf16[4,64,512]{2,1,0:T(8,128)(2,1)} %features.3), channel_id=1, source_target_pairs={{0,1},{1,2},{2,3},{3,4},{4,5},{5,6},{6,7},{7,8},{8,9},{9,10},{10,1... | collective-permute-start | bytes 786440 | tf_op jit(solution)/shard_map/ppermute | solution.py:395
  3.0 1.3 %collective-permute-start.1 = (bf16[4,64,512]{2,1,0:T(8,128)(2,1)}, bf16[4,64,512]{2,1,0:T(8,128)(2,1)S(1)}, u32[]{:S(2)}, u32[]{:S(2)}) collective-permute-start(bf16[4,64,512]{2,1,0:T(8,128)(2,1)} %features.3), channel_id=1, source_target_pairs={{1,0},{2,1},{3,2},{4,3},{5,4},{6,5},{7,6},{8,7},{9,8},{10,9},{11,1... | collective-permute-start | bytes 786440 | tf_op jit(solution)/shard_map/ppermute | solution.py:395
  4.3 0.8 copy.20.dw
  5.8 0.9 copy-done.2
  7.0 3.3 %collective-permute-start.2 = (bf16[96,512]{1,0:T(8,128)(2,1)S(1)}, bf16[96,512]{1,0:T(8,128)(2,1)S(1)}, u32[]{:S(2)}, u32[]{:S(2)}) collective-permute-start(bf16[96,512]{1,0:T(8,128)(2,1)S(1)} %get-tuple-element.56), channel_id=1, source_target_pairs={{0,1},{1,0},{2,3},{3,2},{4,5},{5,4},{6,7},{7,6},{8,9},{9,8},{10,11... | collective-permute-start | bytes 294920 | tf_op jit(solution)/shard_map/ppermute | solution.py:382
  10.3 1.7 %collective-permute-start.3 = (bf16[96,512]{1,0:T(8,128)(2,1)S(1)}, bf16[96,512]{1,0:T(8,128)(2,1)S(1)}, u32[]{:S(2)}, u32[]{:S(2)}) collective-permute-start(bf16[96,512]{1,0:T(8,128)(2,1)S(1)} %get-tuple-element.57), channel_id=1, source_target_pairs={{0,2},{1,3},{2,0},{3,1},{4,6},{5,7},{6,4},{7,5},{8,10},{9,11},{10,... | collective-permute-start | bytes 294920 | tf_op jit(solution)/shard_map/ppermute | solution.py:382
  12.1 4.2 %collective-permute-done.3.refs_2_ = bf16[96,512]{1,0:T(8,128)(2,1)S(1)} collective-permute-done((bf16[96,512]{1,0:T(8,128)(2,1)S(1)}, bf16[96,512]{1,0:T(8,128)(2,1)S(1)}, u32[]{:S(2)}, u32[]{:S(2)}) %collective-permute-start.3) | collective-permute-done | bytes 98336 | tf_op jit(solution)/shard_map/ppermute | solution.py:382
  16.2 1.7 %collective-permute-done.4.refs_3_ = bf16[96,512]{1,0:T(8,128)(2,1)S(1)} collective-permute-done((bf16[96,512]{1,0:T(8,128)(2,1)S(1)}, bf16[96,512]{1,0:T(8,128)(2,1)S(1)}, u32[]{:S(2)}, u32[]{:S(2)}) %collective-permute-start.4) | collective-permute-done | bytes 98336 | tf_op jit(solution)/shard_map/ppermute | solution.py:382
  17.9 1.9 %collective-permute-start.5 = (bf16[64,512]{1,0:T(8,128)(2,1)S(1)}, bf16[64,512]{1,0:T(8,128)(2,1)S(1)}, u32[]{:S(2)}, u32[]{:S(2)}) collective-permute-start(bf16[64,512]{1,0:T(8,128)(2,1)S(1)} %get-tuple-element.59.refs_0_), channel_id=1, source_target_pairs={{0,4},{1,5},{2,6},{3,7},{4,8},{5,9},{6,10},{7,11},{8,12},{9,13},{1... | collective-permute-start | bytes 196616 | tf_op jit(solution)/shard_map/ppermute | solution.py:388
  19.8 2.6 %collective-permute-start.6 = (bf16[64,512]{1,0:T(8,128)(2,1)S(1)}, bf16[64,512]{1,0:T(8,128)(2,1)S(1)}, u32[]{:S(2)}, u32[]{:S(2)}) collective-permute-start(bf16[64,512]{1,0:T(8,128)(2,1)S(1)} %get-tuple-element.59.refs_0_), channel_id=1, source_target_pairs={{0,8},{1,9},{2,10},{3,11},{4,12},{5,13},{6,14},{7,15},{8,0},{9,1},... | collective-permute-start | bytes 196616 | tf_op jit(solution)/shard_map/ppermute | solution.py:388
  22.4 1.4 %collective-permute-start.7 = (bf16[64,512]{1,0:T(8,128)(2,1)S(1)}, bf16[64,512]{1,0:T(8,128)(2,1)S(1)}, u32[]{:S(2)}, u32[]{:S(2)}) collective-permute-start(bf16[64,512]{1,0:T(8,128)(2,1)S(1)} %get-tuple-element.59.refs_0_), channel_id=1, source_target_pairs={{0,12},{1,13},{2,14},{3,15},{4,0},{5,1},{6,2},{7,3},{8,4},{9,5},{1... | collective-permute-start | bytes 196616 | tf_op jit(solution)/shard_map/ppermute | solution.py:388
  23.8 0.8 collective-permute-done.5.refs_1_
  24.6 2.1 %collective-permute-start.12 = (bf16[256,512]{1,0:T(8,128)(2,1)S(1)}, bf16[256,512]{1,0:T(8,128)(2,1)S(1)}, u32[]{:S(2)}, u32[]{:S(2)}) collective-permute-start(bf16[256,512]{1,0:T(8,128)(2,1)S(1)} %bitcast.14), channel_id=1, source_target_pairs={{0,2},{1,3},{2,0},{3,1},{4,6},{5,7},{6,4},{7,5},{8,10},{9,11},{10,... | collective-permute-start | bytes 786440 | tf_op jit(solution)/shard_map/ppermute | solution.py:382
  26.7 0.6 collective-permute-done.6.refs_2_
  27.6 5.2 %shard_map.179 = (bf16[256,512]{1,0:T(8,128)(2,1)S(1)}, f32[256,512]{1,0:T(8,128)S(1)}, f32[256,128]{1,0:T(8,128)S(1)}, f32[64,512]{1,0:T(8,128)S(1)}) custom-call(bf16[4,64,512]{2,1,0:T(8,128)(2,1)S(1)} %copy-done, bf16[4,64,512]{2,1,0:T(8,128)(2,1)S(1)} %collective-permute-done.low, bf16[4,64,512]{2,1,0:T(8,128)(2,1)S(1)} %collective-permute-done.1.high, ...), custom_call_target="tpu_custom_call" | custom-call | flops 20000000 | bytes 1000000 | tf_op jit(solution)/shard_map/pallas_call | solution.py:24
  32.7 2.1 %collective-permute-start.9 = (bf16[256,512]{1,0:T(8,128)(2,1)S(1)}, bf16[256,512]{1,0:T(8,128)(2,1)S(1)}, u32[]{:S(2)}, u32[]{:S(2)}) collective-permute-start(bf16[256,512]{1,0:T(8,128)(2,1)S(1)} %get-tuple-element.61.refs_0_), channel_id=1, source_target_pairs={{0,2},{1,3},{2,0},{3,1},{4,6},{5,7},{6,4},{7,5},{8,10},{9,11},{10,... | collective-permute-start | bytes 786440 | tf_op jit(solution)/shard_map/ppermute | solution.py:382
  34.8 3.5 %collective-permute-start.18 = (bf16[128,512]{1,0:T(8,128)(2,1)S(1)}, bf16[128,512]{1,0:T(8,128)(2,1)S(1)}, u32[]{:S(2)}, u32[]{:S(2)}) collective-permute-start(bf16[128,512]{1,0:T(8,128)(2,1)S(1)} %copy-done.8), channel_id=1, source_target_pairs={{0,8},{1,9},{2,10},{3,11},{4,12},{5,13},{6,14},{7,15},{8,0},{9,1},... | collective-permute-start | bytes 393224 | tf_op jit(solution)/shard_map/ppermute | solution.py:388
  38.7 1.6 %collective-permute-start.14 = (bf16[128,512]{1,0:T(8,128)(2,1)S(1)}, bf16[128,512]{1,0:T(8,128)(2,1)S(1)}, u32[]{:S(2)}, u32[]{:S(2)}) collective-permute-start(bf16[128,512]{1,0:T(8,128)(2,1)S(1)} %bitcast.23), channel_id=1, source_target_pairs={{0,4},{1,5},{2,6},{3,7},{4,8},{5,9},{6,10},{7,11},{8,12},{9,13},{1... | collective-permute-start | bytes 393224 | tf_op jit(solution)/shard_map/ppermute | solution.py:388
  40.3 7.1 %collective-permute-done.18.refs_14_ = bf16[128,512]{1,0:T(8,128)(2,1)S(1)} collective-permute-done((bf16[128,512]{1,0:T(8,128)(2,1)S(1)}, bf16[128,512]{1,0:T(8,128)(2,1)S(1)}, u32[]{:S(2)}, u32[]{:S(2)}) %collective-permute-start.18) | collective-permute-done | bytes 131104 | tf_op jit(solution)/shard_map/ppermute | solution.py:388
  47.4 0.9 collective-permute-start.15
  48.9 7.6 %collective-permute-done.15.refs_10_ = bf16[128,512]{1,0:T(8,128)(2,1)S(1)} collective-permute-done((bf16[128,512]{1,0:T(8,128)(2,1)S(1)}, bf16[128,512]{1,0:T(8,128)(2,1)S(1)}, u32[]{:S(2)}, u32[]{:S(2)}) %collective-permute-start.15) | collective-permute-done | bytes 131104 | tf_op jit(solution)/shard_map/ppermute | solution.py:388
  56.5 1.7 %collective-permute-start.16 = (bf16[128,512]{1,0:T(8,128)(2,1)S(1)}, bf16[128,512]{1,0:T(8,128)(2,1)S(1)}, u32[]{:S(2)}, u32[]{:S(2)}) collective-permute-start(bf16[128,512]{1,0:T(8,128)(2,1)S(1)} %bitcast.25), channel_id=1, source_target_pairs={{0,12},{1,13},{2,14},{3,15},{4,0},{5,1},{6,2},{7,3},{8,4},{9,5},{1... | collective-permute-start | bytes 393224 | tf_op jit(solution)/shard_map/ppermute | solution.py:388
  58.2 3.8 %collective-permute-done.16.refs_11_ = bf16[128,512]{1,0:T(8,128)(2,1)S(1)} collective-permute-done((bf16[128,512]{1,0:T(8,128)(2,1)S(1)}, bf16[128,512]{1,0:T(8,128)(2,1)S(1)}, u32[]{:S(2)}, u32[]{:S(2)}) %collective-permute-start.16) | collective-permute-done | bytes 131104 | tf_op jit(solution)/shard_map/ppermute | solution.py:388
  62.0 3.4 %shard_map.180 = (f32[128,512]{1,0:T(8,128)S(1)}, bf16[128,512]{1,0:T(8,128)(2,1)S(1)}, bf16[128,512]{1,0:T(8,128)(2,1)S(1)}, bf16[128,512]{1,0:T(8,128)(2,1)S(1...) custom-call(f32[64,512]{1,0:T(8,128)S(1)} %get-tuple-element.60.para, ...), custom_call_target="tpu_custom_call" | custom-call | flops 4000000000 | bytes 1000000 | tf_op jit(solution)/shard_map/pallas_call | solution.py:24
  66.0 4.0 %collective-permute-start.29 = (bf16[128,512]{1,0:T(8,128)(2,1)S(1)}, bf16[128,512]{1,0:T(8,128)(2,1)S(1)}, u32[]{:S(2)}, u32[]{:S(2)}) collective-permute-start(bf16[128,512]{1,0:T(8,128)(2,1)S(1)} %get-tuple-element.78), channel_id=1, source_target_pairs={{0,8},{1,9},{2,10},{3,11},{4,12},{5,13},{6,14},{7,15},{8,0},{9,1},... | collective-permute-start | bytes 393224 | tf_op jit(solution)/shard_map/ppermute | solution.py:388
  70.0 1.4 %shard_map.181 = (f32[128,512]{1,0:T(8,128)S(1)}, bf16[128,512]{1,0:T(8,128)(2,1)S(1)}, bf16[128,512]{1,0:T(8,128)(2,1)S(1)}, bf16[128,512]{1,0:T(8,128)(2,1)S(1...) custom-call(bf16[1024,512]{1,0:T(8,128)(2,1)S(1)} %get-tuple-element, ...), custom_call_target="tpu_custom_call" | custom-call | flops 2000000000 | bytes 1000000 | tf_op jit(solution)/shard_map/pallas_call | solution.py:24
  71.7 2.6 %collective-permute-done.28.refs_1_ = bf16[128,512]{1,0:T(8,128)(2,1)S(1)} collective-permute-done((bf16[128,512]{1,0:T(8,128)(2,1)S(1)}, bf16[128,512]{1,0:T(8,128)(2,1)S(1)}, u32[]{:S(2)}, u32[]{:S(2)}) %collective-permute-start.28) | collective-permute-done | bytes 131104 | tf_op jit(solution)/shard_map/ppermute | solution.py:388
  74.3 1.8 %collective-permute-start.30 = (bf16[128,512]{1,0:T(8,128)(2,1)S(1)}, bf16[128,512]{1,0:T(8,128)(2,1)S(1)}, u32[]{:S(2)}, u32[]{:S(2)}) collective-permute-start(bf16[128,512]{1,0:T(8,128)(2,1)S(1)} %get-tuple-element.79), channel_id=1, source_target_pairs={{0,12},{1,13},{2,14},{3,15},{4,0},{5,1},{6,2},{7,3},{8,4},{9,5},{1... | collective-permute-start | bytes 393224 | tf_op jit(solution)/shard_map/ppermute | solution.py:388
  76.1 2.9 %collective-permute-done.29.refs_2_ = bf16[128,512]{1,0:T(8,128)(2,1)S(1)} collective-permute-done((bf16[128,512]{1,0:T(8,128)(2,1)S(1)}, bf16[128,512]{1,0:T(8,128)(2,1)S(1)}, u32[]{:S(2)}, u32[]{:S(2)}) %collective-permute-start.29) | collective-permute-done | bytes 131104 | tf_op jit(solution)/shard_map/ppermute | solution.py:388
  79.1 1.6 %collective-permute-done.30.refs_3_ = bf16[128,512]{1,0:T(8,128)(2,1)S(1)} collective-permute-done((bf16[128,512]{1,0:T(8,128)(2,1)S(1)}, bf16[128,512]{1,0:T(8,128)(2,1)S(1)}, u32[]{:S(2)}, u32[]{:S(2)}) %collective-permute-start.30) | collective-permute-done | bytes 131104 | tf_op jit(solution)/shard_map/ppermute | solution.py:388
  80.7 0.6 collective-permute-start.35
  81.4 5.9 %collective-permute-done.34 = bf16[128,512]{1,0:T(8,128)(2,1)S(1)} collective-permute-done((bf16[128,512]{1,0:T(8,128)(2,1)S(1)}, bf16[128,512]{1,0:T(8,128)(2,1)S(1)}, u32[]{:S(2)}, u32[]{:S(2)}) %collective-permute-start.34) | collective-permute-done | bytes 131104 | tf_op jit(solution)/shard_map/ppermute | solution.py:388
  87.4 1.8 %collective-permute-start.33 = (f32[32,512]{1,0:T(8,128)S(1)}, f32[32,512]{1,0:T(8,128)S(1)}, u32[]{:S(2)}, u32[]{:S(2)}) collective-permute-start(f32[32,512]{1,0:T(8,128)S(1)} %get-tuple-element.83), channel_id=1, source_target_pairs={{0,3},{1,2},{2,1},{3,0},{4,7},{5,6},{6,5},{7,4},{8,11},{9,10},{10,... | collective-permute-start | bytes 196616 | tf_op jit(solution)/shard_map/ppermute | solution.py:382
  89.6 2.8 %shard_map.186 = (f32[64,128]{1,0:T(8,128)S(1)}, f32[64,128]{1,0:T(8,128)S(1)}, f32[64,128]{1,0:T(8,128)S(1)}, f32[64,128]{1,0:T(8,128)S(1)}) custom-call(bf16[4,64,512]{2,1,0:T(8,128)(2,1)S(1)} %get-tuple-element.75.dconv, bf16[4,64,512]{2,1,0:T(8,128)(2,1)S(1)} %copy-done, bf16[4,64,512]{2,1,0:T(8,128)(2,1)S(1)} %collective-permute-done.low, ...), custom_call_target="tpu_custom_call" | custom-call | flops 20000000 | bytes 1000000 | tf_op jit(solution)/shard_map/pallas_call | solution.py:24
  93.2 1.8 %collective-permute-start.37 = (f32[64,128]{1,0:T(8,128)S(1)}, f32[64,128]{1,0:T(8,128)S(1)}, u32[]{:S(2)}, u32[]{:S(2)}) collective-permute-start(f32[64,128]{1,0:T(8,128)S(1)} %get-tuple-element.91), channel_id=1, source_target_pairs={{0,4},{1,5},{2,6},{3,7},{4,8},{5,9},{6,10},{7,11},{8,12},{9,13},{1... | collective-permute-start | bytes 98312 | tf_op jit(solution)/shard_map/ppermute | solution.py:388
  95.0 2.4 %collective-permute-start.39 = (f32[64,128]{1,0:T(8,128)S(1)}, f32[64,128]{1,0:T(8,128)S(1)}, u32[]{:S(2)}, u32[]{:S(2)}) collective-permute-start(f32[64,128]{1,0:T(8,128)S(1)} %get-tuple-element.93), channel_id=1, source_target_pairs={{0,12},{1,13},{2,14},{3,15},{4,0},{5,1},{6,2},{7,3},{8,4},{9,5},{1... | collective-permute-start | bytes 98312 | tf_op jit(solution)/shard_map/ppermute | solution.py:388
  97.4 0.8 convert_add_fusion
  98.1 0.7 shard_map.185
  98.9 1.5 %collective-permute-start.26 = (bf16[4,64,512]{2,1,0:T(8,128)(2,1)S(1)}, bf16[4,64,512]{2,1,0:T(8,128)(2,1)S(1)}, u32[]{:S(2)}, u32[]{:S(2)}) collective-permute-start(bf16[4,64,512]{2,1,0:T(8,128)(2,1)S(1)} %get-tuple-element.75.dconv), channel_id=1, source_target_pairs={{0,1},{1,2},{2,3},{3,4},{4,5},{5,6},{6,7},{7,8},{8,9},{9,10},{10,1... | collective-permute-start | bytes 786440 | tf_op jit(solution)/shard_map/ppermute | solution.py:395
  100.4 1.3 %collective-permute-start.27 = (bf16[4,64,512]{2,1,0:T(8,128)(2,1)S(1)}, bf16[4,64,512]{2,1,0:T(8,128)(2,1)S(1)}, u32[]{:S(2)}, u32[]{:S(2)}) collective-permute-start(bf16[4,64,512]{2,1,0:T(8,128)(2,1)S(1)} %get-tuple-element.75.dconv), channel_id=1, source_target_pairs={{1,0},{2,1},{3,2},{4,3},{5,4},{6,5},{7,6},{8,7},{9,8},{10,9},{11,1... | collective-permute-start | bytes 786440 | tf_op jit(solution)/shard_map/ppermute | solution.py:395
  101.7 3.2 %collective-permute-start.40 = (f32[64,128]{1,0:T(8,128)S(1)}, f32[64,128]{1,0:T(8,128)S(1)}, u32[]{:S(2)}, u32[]{:S(2)}) collective-permute-start(f32[64,128]{1,0:T(8,128)S(1)} %add_add_fusion.1), channel_id=1, source_target_pairs={{0,1},{1,0},{2,3},{3,2},{4,5},{5,4},{6,7},{7,6},{8,9},{9,8},{10,11... | collective-permute-start | bytes 98312 | tf_op jit(solution)/shard_map/ppermute | solution.py:382
  105.1 0.8 collective-permute-done.40
  105.9 1.9 %collective-permute-start.41 = (f32[64,128]{1,0:T(8,128)S(1)}, f32[64,128]{1,0:T(8,128)S(1)}, u32[]{:S(2)}, u32[]{:S(2)}) collective-permute-start(f32[64,128]{1,0:T(8,128)S(1)} %add.60.refs_0_), channel_id=1, source_target_pairs={{0,2},{1,3},{2,0},{3,1},{4,6},{5,7},{6,4},{7,5},{8,10},{9,11},{10,... | collective-permute-start | bytes 98312 | tf_op jit(solution)/shard_map/ppermute | solution.py:382
  107.8 0.8 add_convert_fusion.1
  108.6 2.9 %collective-permute-done.41.refs_1_ = f32[64,128]{1,0:T(8,128)S(1)} collective-permute-done((f32[64,128]{1,0:T(8,128)S(1)}, f32[64,128]{1,0:T(8,128)S(1)}, u32[]{:S(2)}, u32[]{:S(2)}) %collective-permute-start.41) | collective-permute-done | bytes 32800 | tf_op jit(solution)/shard_map/ppermute | solution.py:382
  111.5 0.7 shard_map.187
  112.3 0.7 copy.21
  112.9 5.1 %shard_map.183 = bf16[4,64,512]{2,1,0:T(8,128)(2,1)} custom-call(bf16[4,64,512]{2,1,0:T(8,128)(2,1)S(1)} %get-tuple-element.75.dconv, bf16[4,64,512]{2,1,0:T(8,128)(2,1)S(1)} %collective-permute-done.26.low, bf16[4,64,512]{2,1,0:T(8,128)(2,1)S(1)} %collective-permute-done.27.high, bf16[4,64,512]{2,1,0:T(8,128)(2,1)S(1)} %copy-done.1, ...), custom_call_target="tpu_custom_call" | custom-call | flops 20000000 | bytes 1000000 | tf_op jit(solution)/shard_map/pallas_call | solution.py:24
  (75 shorter events, 4.6 us)
Async XLA Ops:
  0.6 26.9 %collective-permute-start = (bf16[4,64,512]{2,1,0:T(8,128)(2,1)}, bf16[4,64,512]{2,1,0:T(8,128)(2,1)S(1)}, u32[]{:S(2)}, u32[]{:S(2)}) collective-permute-start(bf16[4,64,512]{2,1,0:T(8,128)(2,1)} %features.3), channel_id=1, source_target_pairs={{0,1},{1,2},{2,3},{3,4},{4,5},{5,6},{6,7},{7,8},{8,9},{9,10},{10,1... | collective-permute-start | bytes 786440 | tf_op jit(solution)/shard_map/ppermute | solution.py:395
  3.0 24.5 %collective-permute-start.1 = (bf16[4,64,512]{2,1,0:T(8,128)(2,1)}, bf16[4,64,512]{2,1,0:T(8,128)(2,1)S(1)}, u32[]{:S(2)}, u32[]{:S(2)}) collective-permute-start(bf16[4,64,512]{2,1,0:T(8,128)(2,1)} %features.3), channel_id=1, source_target_pairs={{1,0},{2,1},{3,2},{4,3},{5,4},{6,5},{7,6},{8,7},{9,8},{10,9},{11,1... | collective-permute-start | bytes 786440 | tf_op jit(solution)/shard_map/ppermute | solution.py:395
  5.1 0.7 copy-start.4
  5.2 0.7 copy-start.5
  5.8 0.9 copy-start.2
  6.8 17.8 %copy-start.1 = (bf16[4,64,512]{2,1,0:T(8,128)(2,1)S(1)}, bf16[4,64,512]{2,1,0:T(8,128)(2,1)}, u32[]{:S(2)}) copy-start(bf16[4,64,512]{2,1,0:T(8,128)(2,1)} %cotangent.3) | copy-start | bytes 786436
  6.8 20.8 %copy-start = (bf16[4,64,512]{2,1,0:T(8,128)(2,1)S(1)}, bf16[4,64,512]{2,1,0:T(8,128)(2,1)}, u32[]{:S(2)}) copy-start(bf16[4,64,512]{2,1,0:T(8,128)(2,1)} %features.3) | copy-start | bytes 786436
  7.0 5.1 %collective-permute-start.2 = (bf16[96,512]{1,0:T(8,128)(2,1)S(1)}, bf16[96,512]{1,0:T(8,128)(2,1)S(1)}, u32[]{:S(2)}, u32[]{:S(2)}) collective-permute-start(bf16[96,512]{1,0:T(8,128)(2,1)S(1)} %get-tuple-element.56), channel_id=1, source_target_pairs={{0,1},{1,0},{2,3},{3,2},{4,5},{5,4},{6,7},{7,6},{8,9},{9,8},{10,11... | collective-permute-start | bytes 294920 | tf_op jit(solution)/shard_map/ppermute | solution.py:382
  10.3 5.9 %collective-permute-start.3 = (bf16[96,512]{1,0:T(8,128)(2,1)S(1)}, bf16[96,512]{1,0:T(8,128)(2,1)S(1)}, u32[]{:S(2)}, u32[]{:S(2)}) collective-permute-start(bf16[96,512]{1,0:T(8,128)(2,1)S(1)} %get-tuple-element.57), channel_id=1, source_target_pairs={{0,2},{1,3},{2,0},{3,1},{4,6},{5,7},{6,4},{7,5},{8,10},{9,11},{10,... | collective-permute-start | bytes 294920 | tf_op jit(solution)/shard_map/ppermute | solution.py:382
  12.0 5.9 %collective-permute-start.4 = (bf16[96,512]{1,0:T(8,128)(2,1)S(1)}, bf16[96,512]{1,0:T(8,128)(2,1)S(1)}, u32[]{:S(2)}, u32[]{:S(2)}) collective-permute-start(bf16[96,512]{1,0:T(8,128)(2,1)S(1)} %get-tuple-element.58), channel_id=1, source_target_pairs={{0,3},{1,2},{2,1},{3,0},{4,7},{5,6},{6,5},{7,4},{8,11},{9,10},{10,... | collective-permute-start | bytes 294920 | tf_op jit(solution)/shard_map/ppermute | solution.py:382
  17.9 6.6 %collective-permute-start.5 = (bf16[64,512]{1,0:T(8,128)(2,1)S(1)}, bf16[64,512]{1,0:T(8,128)(2,1)S(1)}, u32[]{:S(2)}, u32[]{:S(2)}) collective-permute-start(bf16[64,512]{1,0:T(8,128)(2,1)S(1)} %get-tuple-element.59.refs_0_), channel_id=1, source_target_pairs={{0,4},{1,5},{2,6},{3,7},{4,8},{5,9},{6,10},{7,11},{8,12},{9,13},{1... | collective-permute-start | bytes 196616 | tf_op jit(solution)/shard_map/ppermute | solution.py:388
  19.8 7.5 %collective-permute-start.6 = (bf16[64,512]{1,0:T(8,128)(2,1)S(1)}, bf16[64,512]{1,0:T(8,128)(2,1)S(1)}, u32[]{:S(2)}, u32[]{:S(2)}) collective-permute-start(bf16[64,512]{1,0:T(8,128)(2,1)S(1)} %get-tuple-element.59.refs_0_), channel_id=1, source_target_pairs={{0,8},{1,9},{2,10},{3,11},{4,12},{5,13},{6,14},{7,15},{8,0},{9,1},... | collective-permute-start | bytes 196616 | tf_op jit(solution)/shard_map/ppermute | solution.py:388
  22.4 5.1 %collective-permute-start.7 = (bf16[64,512]{1,0:T(8,128)(2,1)S(1)}, bf16[64,512]{1,0:T(8,128)(2,1)S(1)}, u32[]{:S(2)}, u32[]{:S(2)}) collective-permute-start(bf16[64,512]{1,0:T(8,128)(2,1)S(1)} %get-tuple-element.59.refs_0_), channel_id=1, source_target_pairs={{0,12},{1,13},{2,14},{3,15},{4,0},{5,1},{6,2},{7,3},{8,4},{9,5},{1... | collective-permute-start | bytes 196616 | tf_op jit(solution)/shard_map/ppermute | solution.py:388
  24.6 10.3 %copy-start.8 = (bf16[128,512]{1,0:T(8,128)(2,1)S(1)}, bf16[128,512]{1,0:T(8,128)(2,1)}, u32[]{:S(2)}) copy-start(bf16[128,512]{1,0:T(8,128)(2,1)} %refs_12_.1) | copy-start | bytes 393220
  24.6 23.8 %collective-permute-start.12 = (bf16[256,512]{1,0:T(8,128)(2,1)S(1)}, bf16[256,512]{1,0:T(8,128)(2,1)S(1)}, u32[]{:S(2)}, u32[]{:S(2)}) collective-permute-start(bf16[256,512]{1,0:T(8,128)(2,1)S(1)} %bitcast.14), channel_id=1, source_target_pairs={{0,2},{1,3},{2,0},{3,1},{4,6},{5,7},{6,4},{7,5},{8,10},{9,11},{10,... | collective-permute-start | bytes 786440 | tf_op jit(solution)/shard_map/ppermute | solution.py:382
  27.3 11.4 %collective-permute-start.17 = (bf16[128,512]{1,0:T(8,128)(2,1)}, bf16[128,512]{1,0:T(8,128)(2,1)S(1)}, u32[]{:S(2)}, u32[]{:S(2)}) collective-permute-start(bf16[128,512]{1,0:T(8,128)(2,1)} %refs_12_.1), channel_id=1, source_target_pairs={{0,4},{1,5},{2,6},{3,7},{4,8},{5,9},{6,10},{7,11},{8,12},{9,13},{1... | collective-permute-start | bytes 393224 | tf_op jit(solution)/shard_map/ppermute | solution.py:388
  32.7 16.1 %collective-permute-start.9 = (bf16[256,512]{1,0:T(8,128)(2,1)S(1)}, bf16[256,512]{1,0:T(8,128)(2,1)S(1)}, u32[]{:S(2)}, u32[]{:S(2)}) collective-permute-start(bf16[256,512]{1,0:T(8,128)(2,1)S(1)} %get-tuple-element.61.refs_0_), channel_id=1, source_target_pairs={{0,2},{1,3},{2,0},{3,1},{4,6},{5,7},{6,4},{7,5},{8,10},{9,11},{10,... | collective-permute-start | bytes 786440 | tf_op jit(solution)/shard_map/ppermute | solution.py:382
  34.8 12.5 %collective-permute-start.18 = (bf16[128,512]{1,0:T(8,128)(2,1)S(1)}, bf16[128,512]{1,0:T(8,128)(2,1)S(1)}, u32[]{:S(2)}, u32[]{:S(2)}) collective-permute-start(bf16[128,512]{1,0:T(8,128)(2,1)S(1)} %copy-done.8), channel_id=1, source_target_pairs={{0,8},{1,9},{2,10},{3,11},{4,12},{5,13},{6,14},{7,15},{8,0},{9,1},... | collective-permute-start | bytes 393224 | tf_op jit(solution)/shard_map/ppermute | solution.py:388
  38.3 9.1 %collective-permute-start.19 = (bf16[128,512]{1,0:T(8,128)(2,1)S(1)}, bf16[128,512]{1,0:T(8,128)(2,1)S(1)}, u32[]{:S(2)}, u32[]{:S(2)}) collective-permute-start(bf16[128,512]{1,0:T(8,128)(2,1)S(1)} %copy-done.8), channel_id=1, source_target_pairs={{0,12},{1,13},{2,14},{3,15},{4,0},{5,1},{6,2},{7,3},{8,4},{9,5},{1... | collective-permute-start | bytes 393224 | tf_op jit(solution)/shard_map/ppermute | solution.py:388
  38.7 9.6 %collective-permute-start.14 = (bf16[128,512]{1,0:T(8,128)(2,1)S(1)}, bf16[128,512]{1,0:T(8,128)(2,1)S(1)}, u32[]{:S(2)}, u32[]{:S(2)}) collective-permute-start(bf16[128,512]{1,0:T(8,128)(2,1)S(1)} %bitcast.23), channel_id=1, source_target_pairs={{0,4},{1,5},{2,6},{3,7},{4,8},{5,9},{6,10},{7,11},{8,12},{9,13},{1... | collective-permute-start | bytes 393224 | tf_op jit(solution)/shard_map/ppermute | solution.py:388
  47.4 14.6 %collective-permute-start.11 = (bf16[256,512]{1,0:T(8,128)(2,1)S(1)}, bf16[256,512]{1,0:T(8,128)(2,1)S(1)}, u32[]{:S(2)}, u32[]{:S(2)}) collective-permute-start(bf16[256,512]{1,0:T(8,128)(2,1)S(1)} %bitcast.15), channel_id=1, source_target_pairs={{0,1},{1,0},{2,3},{3,2},{4,5},{5,4},{6,7},{7,6},{8,9},{9,8},{10,11... | collective-permute-start | bytes 786440 | tf_op jit(solution)/shard_map/ppermute | solution.py:382
  47.4 9.1 %collective-permute-start.15 = (bf16[128,512]{1,0:T(8,128)(2,1)S(1)}, bf16[128,512]{1,0:T(8,128)(2,1)S(1)}, u32[]{:S(2)}, u32[]{:S(2)}) collective-permute-start(bf16[128,512]{1,0:T(8,128)(2,1)S(1)} %bitcast.24), channel_id=1, source_target_pairs={{0,8},{1,9},{2,10},{3,11},{4,12},{5,13},{6,14},{7,15},{8,0},{9,1},... | collective-permute-start | bytes 393224 | tf_op jit(solution)/shard_map/ppermute | solution.py:388
  48.4 13.7 %collective-permute-start.8 = (bf16[256,512]{1,0:T(8,128)(2,1)S(1)}, bf16[256,512]{1,0:T(8,128)(2,1)S(1)}, u32[]{:S(2)}, u32[]{:S(2)}) collective-permute-start(bf16[256,512]{1,0:T(8,128)(2,1)S(1)} %get-tuple-element.61.refs_0_), channel_id=1, source_target_pairs={{0,1},{1,0},{2,3},{3,2},{4,5},{5,4},{6,7},{7,6},{8,9},{9,8},{10,11... | collective-permute-start | bytes 786440 | tf_op jit(solution)/shard_map/ppermute | solution.py:382
  48.4 13.7 %collective-permute-start.13 = (bf16[256,512]{1,0:T(8,128)(2,1)S(1)}, bf16[256,512]{1,0:T(8,128)(2,1)S(1)}, u32[]{:S(2)}, u32[]{:S(2)}) collective-permute-start(bf16[256,512]{1,0:T(8,128)(2,1)S(1)} %collective-permute-done.12.refs_6_.refs_2_), channel_id=1, source_target_pairs={{0,1},{1,0},{2,3},{3,2},{4,5},{5,4},{6,7},{7,6},{8,9},{9,8},{10,11... | collective-permute-start | bytes 786440 | tf_op jit(solution)/shard_map/ppermute | solution.py:382
  48.9 13.2 %collective-permute-start.10 = (bf16[256,512]{1,0:T(8,128)(2,1)S(1)}, bf16[256,512]{1,0:T(8,128)(2,1)S(1)}, u32[]{:S(2)}, u32[]{:S(2)}) collective-permute-start(bf16[256,512]{1,0:T(8,128)(2,1)S(1)} %collective-permute-done.9.refs_2_), channel_id=1, source_target_pairs={{0,1},{1,0},{2,3},{3,2},{4,5},{5,4},{6,7},{7,6},{8,9},{9,8},{10,11... | collective-permute-start | bytes 786440 | tf_op jit(solution)/shard_map/ppermute | solution.py:382
  56.5 5.5 %collective-permute-start.16 = (bf16[128,512]{1,0:T(8,128)(2,1)S(1)}, bf16[128,512]{1,0:T(8,128)(2,1)S(1)}, u32[]{:S(2)}, u32[]{:S(2)}) collective-permute-start(bf16[128,512]{1,0:T(8,128)(2,1)S(1)} %bitcast.25), channel_id=1, source_target_pairs={{0,12},{1,13},{2,14},{3,15},{4,0},{5,1},{6,2},{7,3},{8,4},{9,5},{1... | collective-permute-start | bytes 393224 | tf_op jit(solution)/shard_map/ppermute | solution.py:388
  65.4 6.1 %collective-permute-start.24 = (bf16[256,512]{1,0:T(8,128)(2,1)S(1)}, bf16[256,512]{1,0:T(8,128)(2,1)S(1)}, u32[]{:S(2)}, u32[]{:S(2)}) collective-permute-start(bf16[256,512]{1,0:T(8,128)(2,1)S(1)} %get-tuple-element.74), channel_id=1, source_target_pairs={{0,1},{1,0},{2,3},{3,2},{4,5},{5,4},{6,7},{7,6},{8,9},{9,8},{10,11... | collective-permute-start | bytes 786440 | tf_op jit(solution)/shard_map/ppermute | solution.py:382
  65.5 21.7 %collective-permute-start.23 = (bf16[256,512]{1,0:T(8,128)(2,1)S(1)}, bf16[256,512]{1,0:T(8,128)(2,1)S(1)}, u32[]{:S(2)}, u32[]{:S(2)}) collective-permute-start(bf16[256,512]{1,0:T(8,128)(2,1)S(1)} %get-tuple-element.72), channel_id=1, source_target_pairs={{0,1},{1,0},{2,3},{3,2},{4,5},{5,4},{6,7},{7,6},{8,9},{9,8},{10,11... | collective-permute-start | bytes 786440 | tf_op jit(solution)/shard_map/ppermute | solution.py:382
  66.0 8.2 %collective-permute-start.28 = (bf16[128,512]{1,0:T(8,128)(2,1)S(1)}, bf16[128,512]{1,0:T(8,128)(2,1)S(1)}, u32[]{:S(2)}, u32[]{:S(2)}) collective-permute-start(bf16[128,512]{1,0:T(8,128)(2,1)S(1)} %get-tuple-element.77), channel_id=1, source_target_pairs={{0,4},{1,5},{2,6},{3,7},{4,8},{5,9},{6,10},{7,11},{8,12},{9,13},{1... | collective-permute-start | bytes 393224 | tf_op jit(solution)/shard_map/ppermute | solution.py:388
  66.0 13.0 %collective-permute-start.29 = (bf16[128,512]{1,0:T(8,128)(2,1)S(1)}, bf16[128,512]{1,0:T(8,128)(2,1)S(1)}, u32[]{:S(2)}, u32[]{:S(2)}) collective-permute-start(bf16[128,512]{1,0:T(8,128)(2,1)S(1)} %get-tuple-element.78), channel_id=1, source_target_pairs={{0,8},{1,9},{2,10},{3,11},{4,12},{5,13},{6,14},{7,15},{8,0},{9,1},... | collective-permute-start | bytes 393224 | tf_op jit(solution)/shard_map/ppermute | solution.py:388
  71.4 15.8 %collective-permute-start.21 = (bf16[256,512]{1,0:T(8,128)(2,1)S(1)}, bf16[256,512]{1,0:T(8,128)(2,1)S(1)}, u32[]{:S(2)}, u32[]{:S(2)}) collective-permute-start(bf16[256,512]{1,0:T(8,128)(2,1)S(1)} %get-tuple-element.68), channel_id=1, source_target_pairs={{0,1},{1,0},{2,3},{3,2},{4,5},{5,4},{6,7},{7,6},{8,9},{9,8},{10,11... | collective-permute-start | bytes 786440 | tf_op jit(solution)/shard_map/ppermute | solution.py:382
  71.6 15.8 %collective-permute-start.25 = (bf16[256,512]{1,0:T(8,128)(2,1)S(1)}, bf16[256,512]{1,0:T(8,128)(2,1)S(1)}, u32[]{:S(2)}, u32[]{:S(2)}) collective-permute-start(bf16[256,512]{1,0:T(8,128)(2,1)S(1)} %add_convert_fusion), channel_id=1, source_target_pairs={{0,2},{1,3},{2,0},{3,1},{4,6},{5,7},{6,4},{7,5},{8,10},{9,11},{10,... | collective-permute-start | bytes 786440 | tf_op jit(solution)/shard_map/ppermute | solution.py:382
  74.3 6.4 %collective-permute-start.30 = (bf16[128,512]{1,0:T(8,128)(2,1)S(1)}, bf16[128,512]{1,0:T(8,128)(2,1)S(1)}, u32[]{:S(2)}, u32[]{:S(2)}) collective-permute-start(bf16[128,512]{1,0:T(8,128)(2,1)S(1)} %get-tuple-element.79), channel_id=1, source_target_pairs={{0,12},{1,13},{2,14},{3,15},{4,0},{5,1},{6,2},{7,3},{8,4},{9,5},{1... | collective-permute-start | bytes 393224 | tf_op jit(solution)/shard_map/ppermute | solution.py:388
  79.0 8.2 %collective-permute-start.34 = (bf16[128,512]{1,0:T(8,128)(2,1)S(1)}, bf16[128,512]{1,0:T(8,128)(2,1)S(1)}, u32[]{:S(2)}, u32[]{:S(2)}) collective-permute-start(bf16[128,512]{1,0:T(8,128)(2,1)S(1)} %get-tuple-element.85), channel_id=1, source_target_pairs={{0,4},{1,5},{2,6},{3,7},{4,8},{5,9},{6,10},{7,11},{8,12},{9,13},{1... | collective-permute-start | bytes 393224 | tf_op jit(solution)/shard_map/ppermute | solution.py:388
  80.7 11.7 %collective-permute-start.35 = (bf16[128,512]{1,0:T(8,128)(2,1)S(1)}, bf16[128,512]{1,0:T(8,128)(2,1)S(1)}, u32[]{:S(2)}, u32[]{:S(2)}) collective-permute-start(bf16[128,512]{1,0:T(8,128)(2,1)S(1)} %get-tuple-element.86), channel_id=1, source_target_pairs={{0,8},{1,9},{2,10},{3,11},{4,12},{5,13},{6,14},{7,15},{8,0},{9,1},... | collective-permute-start | bytes 393224 | tf_op jit(solution)/shard_map/ppermute | solution.py:388
  87.2 5.9 %collective-permute-start.36 = (bf16[128,512]{1,0:T(8,128)(2,1)S(1)}, bf16[128,512]{1,0:T(8,128)(2,1)S(1)}, u32[]{:S(2)}, u32[]{:S(2)}) collective-permute-start(bf16[128,512]{1,0:T(8,128)(2,1)S(1)} %get-tuple-element.87), channel_id=1, source_target_pairs={{0,12},{1,13},{2,14},{3,15},{4,0},{5,1},{6,2},{7,3},{8,4},{9,5},{1... | collective-permute-start | bytes 393224 | tf_op jit(solution)/shard_map/ppermute | solution.py:388
  87.3 5.9 %collective-permute-start.31 = (f32[32,512]{1,0:T(8,128)S(1)}, f32[32,512]{1,0:T(8,128)S(1)}, u32[]{:S(2)}, u32[]{:S(2)}) collective-permute-start(f32[32,512]{1,0:T(8,128)S(1)} %get-tuple-element.81), channel_id=1, source_target_pairs={{0,1},{1,0},{2,3},{3,2},{4,5},{5,4},{6,7},{7,6},{8,9},{9,8},{10,11... | collective-permute-start | bytes 196616 | tf_op jit(solution)/shard_map/ppermute | solution.py:382
  87.3 7.7 %collective-permute-start.32 = (f32[32,512]{1,0:T(8,128)S(1)}, f32[32,512]{1,0:T(8,128)S(1)}, u32[]{:S(2)}, u32[]{:S(2)}) collective-permute-start(f32[32,512]{1,0:T(8,128)S(1)} %get-tuple-element.82), channel_id=1, source_target_pairs={{0,2},{1,3},{2,0},{3,1},{4,6},{5,7},{6,4},{7,5},{8,10},{9,11},{10,... | collective-permute-start | bytes 196616 | tf_op jit(solution)/shard_map/ppermute | solution.py:382
  87.4 7.6 %collective-permute-start.33 = (f32[32,512]{1,0:T(8,128)S(1)}, f32[32,512]{1,0:T(8,128)S(1)}, u32[]{:S(2)}, u32[]{:S(2)}) collective-permute-start(f32[32,512]{1,0:T(8,128)S(1)} %get-tuple-element.83), channel_id=1, source_target_pairs={{0,3},{1,2},{2,1},{3,0},{4,7},{5,6},{6,5},{7,4},{8,11},{9,10},{10,... | collective-permute-start | bytes 196616 | tf_op jit(solution)/shard_map/ppermute | solution.py:382
  92.4 12.6 %collective-permute-start.20 = (bf16[256,512]{1,0:T(8,128)(2,1)S(1)}, bf16[256,512]{1,0:T(8,128)(2,1)S(1)}, u32[]{:S(2)}, u32[]{:S(2)}) collective-permute-start(bf16[256,512]{1,0:T(8,128)(2,1)S(1)} %get-tuple-element.66), channel_id=1, source_target_pairs={{0,1},{1,0},{2,3},{3,2},{4,5},{5,4},{6,7},{7,6},{8,9},{9,8},{10,11... | collective-permute-start | bytes 786440 | tf_op jit(solution)/shard_map/ppermute | solution.py:382
  93.2 11.8 %collective-permute-start.22 = (bf16[256,512]{1,0:T(8,128)(2,1)S(1)}, bf16[256,512]{1,0:T(8,128)(2,1)S(1)}, u32[]{:S(2)}, u32[]{:S(2)}) collective-permute-start(bf16[256,512]{1,0:T(8,128)(2,1)S(1)} %add_convert_fusion.2), channel_id=1, source_target_pairs={{0,2},{1,3},{2,0},{3,1},{4,6},{5,7},{6,4},{7,5},{8,10},{9,11},{10,... | collective-permute-start | bytes 786440 | tf_op jit(solution)/shard_map/ppermute | solution.py:382
  93.2 5.7 %collective-permute-start.37 = (f32[64,128]{1,0:T(8,128)S(1)}, f32[64,128]{1,0:T(8,128)S(1)}, u32[]{:S(2)}, u32[]{:S(2)}) collective-permute-start(f32[64,128]{1,0:T(8,128)S(1)} %get-tuple-element.91), channel_id=1, source_target_pairs={{0,4},{1,5},{2,6},{3,7},{4,8},{5,9},{6,10},{7,11},{8,12},{9,13},{1... | collective-permute-start | bytes 98312 | tf_op jit(solution)/shard_map/ppermute | solution.py:388
  94.9 5.5 %collective-permute-start.38 = (f32[64,128]{1,0:T(8,128)S(1)}, f32[64,128]{1,0:T(8,128)S(1)}, u32[]{:S(2)}, u32[]{:S(2)}) collective-permute-start(f32[64,128]{1,0:T(8,128)S(1)} %get-tuple-element.92), channel_id=1, source_target_pairs={{0,8},{1,9},{2,10},{3,11},{4,12},{5,13},{6,14},{7,15},{8,0},{9,1},... | collective-permute-start | bytes 98312 | tf_op jit(solution)/shard_map/ppermute | solution.py:388
  95.0 6.7 %collective-permute-start.39 = (f32[64,128]{1,0:T(8,128)S(1)}, f32[64,128]{1,0:T(8,128)S(1)}, u32[]{:S(2)}, u32[]{:S(2)}) collective-permute-start(f32[64,128]{1,0:T(8,128)S(1)} %get-tuple-element.93), channel_id=1, source_target_pairs={{0,12},{1,13},{2,14},{3,15},{4,0},{5,1},{6,2},{7,3},{8,4},{9,5},{1... | collective-permute-start | bytes 98312 | tf_op jit(solution)/shard_map/ppermute | solution.py:388
  98.9 14.0 %collective-permute-start.26 = (bf16[4,64,512]{2,1,0:T(8,128)(2,1)S(1)}, bf16[4,64,512]{2,1,0:T(8,128)(2,1)S(1)}, u32[]{:S(2)}, u32[]{:S(2)}) collective-permute-start(bf16[4,64,512]{2,1,0:T(8,128)(2,1)S(1)} %get-tuple-element.75.dconv), channel_id=1, source_target_pairs={{0,1},{1,2},{2,3},{3,4},{4,5},{5,6},{6,7},{7,8},{8,9},{9,10},{10,1... | collective-permute-start | bytes 786440 | tf_op jit(solution)/shard_map/ppermute | solution.py:395
  100.4 12.5 %collective-permute-start.27 = (bf16[4,64,512]{2,1,0:T(8,128)(2,1)S(1)}, bf16[4,64,512]{2,1,0:T(8,128)(2,1)S(1)}, u32[]{:S(2)}, u32[]{:S(2)}) collective-permute-start(bf16[4,64,512]{2,1,0:T(8,128)(2,1)S(1)} %get-tuple-element.75.dconv), channel_id=1, source_target_pairs={{1,0},{2,1},{3,2},{4,3},{5,4},{6,5},{7,6},{8,7},{9,8},{10,9},{11,1... | collective-permute-start | bytes 786440 | tf_op jit(solution)/shard_map/ppermute | solution.py:395
  101.7 4.2 %collective-permute-start.40 = (f32[64,128]{1,0:T(8,128)S(1)}, f32[64,128]{1,0:T(8,128)S(1)}, u32[]{:S(2)}, u32[]{:S(2)}) collective-permute-start(f32[64,128]{1,0:T(8,128)S(1)} %add_add_fusion.1), channel_id=1, source_target_pairs={{0,1},{1,0},{2,3},{3,2},{4,5},{5,4},{6,7},{7,6},{8,9},{9,8},{10,11... | collective-permute-start | bytes 98312 | tf_op jit(solution)/shard_map/ppermute | solution.py:382
  105.9 5.6 %collective-permute-start.41 = (f32[64,128]{1,0:T(8,128)S(1)}, f32[64,128]{1,0:T(8,128)S(1)}, u32[]{:S(2)}, u32[]{:S(2)}) collective-permute-start(f32[64,128]{1,0:T(8,128)S(1)} %add.60.refs_0_), channel_id=1, source_target_pairs={{0,2},{1,3},{2,0},{3,1},{4,6},{5,7},{6,4},{7,5},{8,10},{9,11},{10,... | collective-permute-start | bytes 98312 | tf_op jit(solution)/shard_map/ppermute | solution.py:382
  (3 other events, 2.0 us)

commit v2 on v1

v2 whole, which is shorter than its diff:
```python
import functools
import math

import jax
import jax.numpy as jnp
from jax import lax
from jax.experimental import pallas as pl
from jax.experimental.pallas import tpu as pltpu
from jax.sharding import PartitionSpec as P

eps = 1e-06
lanes = 128
taps = 49
f32 = jnp.float32
bf16 = jnp.bfloat16
row_bias, row_gain, row_shift, row_down, row_up = 49, 50, 51, 52, 53


def round_up(value, unit):
    return (value + unit - 1) // unit * unit


def call(kernel, outs, args, scratch=(), mib=24, flops=1000, moved=1000, space=pltpu.VMEM):
    return pl.pallas_call(
        kernel,
        out_shape=[jax.ShapeDtypeStruct(shape, dtype) for shape, dtype in outs],
        in_specs=[pl.BlockSpec(memory_space=space)] * len(args),
        out_specs=[pl.BlockSpec(memory_space=pltpu.VMEM)] * len(outs),
        scratch_shapes=list(scratch),
        compiler_params=pltpu.CompilerParams(vmem_limit_bytes=mib * 1024 * 1024),
        cost_estimate=pl.CostEstimate(flops=flops, bytes_accessed=moved, transcendentals=0),
    )(*args)


def place(quads):
    index = lax.axis_index("row")
    return index // quads, lax.rem(index, quads)


def one_hot(rows, columns, offset):
    down = lax.broadcasted_iota(jnp.int32, (rows, columns), 0)
    across = lax.broadcasted_iota(jnp.int32, (rows, columns), 1)
    return (across == down + offset).astype(f32)


def pack_kernel(quads, layers, rows, *refs):
    given, refs = refs[:7], refs[7:]
    near, small, far, (held, head, *local), sems = (
        refs[: quads // 2],
        refs[quads // 2],
        refs[quads // 2 + 1],
        refs[quads // 2 + 2 : -1],
        refs[-1],
    )
    copies = [
        pltpu.make_async_copy(source, target, sems.at[i])
        for i, (source, target) in enumerate(zip(given, local))
    ]
    for copy in copies:
        copy.start()
    for copy in copies:
        copy.wait()
    dw, db, gain, shift, down, upb, up = local
    _, member = place(quads)
    own = dw.shape[0]
    part = upb.shape[1]
    step = round_up(own, 16)
    spread = one_hot(own, lanes, member * own).astype(bf16)
    held[...] = jnp.zeros_like(held)
    held[row_bias : row_bias + 1, :] = db[...].astype(f32)
    held[row_gain : row_gain + 1, :] = gain[...].astype(f32)
    held[row_shift : row_shift + 1, :] = shift[...].astype(f32)
    held[row_down : row_down + 1, :] = down[...].astype(f32)
    head[...] = jnp.dot(held[...].astype(bf16), spread, preferred_element_type=f32)
    head[0:taps, :] = lax.dot_general(
        dw[...], spread, (((0,), (0,)), ((), ())), preferred_element_type=f32
    )
    for s in range(quads):
        head[row_up + s : row_up + s + 1, 0:part] = jnp.where(
            member == s, upb[...].astype(f32), 0.0
        )
    small[...] = head[...].astype(bf16)
    far[0:rows, :] = head[...].astype(bf16)
    wide = [up[:, i * part : (i + 1) * part] for i in range(layers * quads)]
    for other in range(quads):
        partner = jnp.bitwise_xor(member, other)
        if other < quads // 2:
            out, base = near[other], 0
        else:
            out, base = far, rows + (other - quads // 2) * layers * step
        if step != own or part != lanes:
            out[base : base + layers * step, :] = jnp.zeros((layers * step, lanes), bf16)
        for z in range(layers):
            piece = wide[z * quads]
            for s in range(1, quads):
                piece = jnp.where(partner == s, wide[z * quads + s], piece)
            out[base + z * step : base + z * step + own, 0:part] = piece


def unpack_kernel(quads, layers, down, *refs):
    pieces, out = refs[:-1], refs[-1]
    _, member = place(quads)
    blocks, own, share = out.shape
    ahead = blocks - quads
    part = share // layers
    step = round_up(own, 16)
    for i in range(ahead):
        out[i] = down[i * own : (i + 1) * own, :]
    for other, piece in enumerate(pieces):
        to = ahead + jnp.bitwise_xor(member, other)
        for z in range(layers):
            block = piece[z * step : (z + 1) * step, :]
            out[to, :, z * part : (z + 1) * part] = block[0:own, 0:part]


def fill(padded, block, outer, inner, width):
    height = block.shape[0]
    even = lax.rem(lax.axis_index("row"), 2) == 0
    rows, columns, chans = padded.shape
    zero = jnp.zeros((rows, 8, chans), f32)
    padded[:, 0:8, :] = zero
    padded[:, 8 + width :, :] = jnp.zeros((rows, columns - 8 - width, chans), f32)
    low = jnp.where(even, outer[height - 3 :, :, :], inner[height - 3 :, :, :])
    high = jnp.where(even, inner[0:3, :, :], outer[0:3, :, :])
    padded[0:3, 8 : 8 + width, :] = low.astype(f32)
    padded[3 : 3 + height, 8 : 8 + width, :] = block[...].astype(f32)
    padded[3 + height :, 8 : 8 + width, :] = high.astype(f32)


def slide(padded, weights, height, width, at, flip):
    tiles = (width // 8, 8, lanes)
    sums = [jnp.zeros(tiles, f32) for _ in range(height)]
    for second in range(7):
        order = [first * 7 + second for first in range(7)]
        order = [taps - 1 - tap if flip else tap for tap in order]
        held = [jnp.broadcast_to(weights[tap : tap + 1, at], tiles[1:]) for tap in order]
        for row in range(height + 6):
            piece = padded[row, 5 + second : 5 + second + width, at].reshape(tiles)
            for out in range(height):
                if 0 <= row - out < 7:
                    sums[out] = sums[out] + piece * held[row - out]
    return [value.reshape(width, lanes) for value in sums]


def conv_kernel(quads, layers, features, outer, inner, *refs):
    smalls, (normal, normed, inv, params, bias, padded, conv) = refs[:-7], refs[-7:]
    height, width, chans = features.shape
    layer, member = place(quads)
    for other, small in enumerate(smalls):
        at = pl.multiple_of(jnp.bitwise_xor(layer, other) * lanes, lanes)
        params[:, pl.ds(at, lanes)] = small[...].astype(f32)
    part = bias.shape[1] // layers
    for z in range(layers):
        at = slice(z * lanes, z * lanes + part)
        value = params[row_up : row_up + 1, at]
        for s in range(1, quads):
            value = jnp.where(member == s, params[row_up + s : row_up + s + 1, at], value)
        bias[:, z * part : (z + 1) * part] = jnp.broadcast_to(value, (8, part))
    fill(padded, features, outer, inner, width)

    def chunk(i, carry):
        at = pl.ds(pl.multiple_of(i * lanes, lanes), lanes)
        sums = slide(padded, params, height, width, at, False)
        for out in range(height):
            conv[out * width : (out + 1) * width, at] = (
                sums[out] + params[row_bias : row_bias + 1, at]
            )
        return carry

    lax.fori_loop(0, chans // lanes, chunk, 0)

    def norm(i, carry):
        at = pl.ds(pl.multiple_of(i * width, width), width)
        value = conv[at, :]
        centered = value - jnp.mean(value, axis=1, keepdims=True)
        var = jnp.mean(centered * centered, axis=1, keepdims=True)
        scale = lax.rsqrt(var + eps)
        value = centered * scale
        normed[at, :] = value
        inv[at, :] = jnp.broadcast_to(scale, (width, lanes))
        normal[at, :] = (
            value * params[row_gain : row_gain + 1, 0:chans]
            + params[row_shift : row_shift + 1, 0:chans]
        ).astype(bf16)
        return carry

    lax.fori_loop(0, height, norm, 0)


def back_kernel(dconv, outer, inner, cotangent, params, out, padded):
    height, width, chans = dconv.shape
    fill(padded, dconv, outer, inner, width)

    def chunk(i, carry):
        at = pl.ds(pl.multiple_of(i * lanes, lanes), lanes)
        sums = slide(padded, params, height, width, at, True)
        for row in range(height):
            out[row, :, at] = (cotangent[row, :, at].astype(f32) + sums[row]).astype(bf16)
        return carry

    lax.fori_loop(0, chans // lanes, chunk, 0)


def taps_kernel(
    quads, layers, scale, dconv, features, outer, inner, cotangent, norms, upb, *refs
):
    kept, sent, padded, grads = refs
    height, width, chans = dconv.shape
    layer, member = place(quads)
    fill(padded, features, outer, inner, width)
    grads[...] = jnp.zeros_like(grads)

    def fold(value):
        return jnp.sum(value.reshape(width // 8, 8, lanes), axis=0)

    def chunk(i, carry):
        at = pl.ds(pl.multiple_of(i * lanes, lanes), lanes)
        own = [dconv[row, :, at].astype(f32) for row in range(height)]
        for second in range(7):
            sums = [jnp.zeros((8, lanes), f32) for _ in range(7)]
            for row in range(height + 6):
                piece = padded[row, 5 + second : 5 + second + width, at]
                for out in range(height):
                    first = row - out
                    if 0 <= first < 7:
                        sums[first] = sums[first] + fold(own[out] * piece)
            for first in range(7):
                tap = first * 7 + second
                grads[tap : tap + 1, at] = (
                    jnp.sum(sums[first], axis=0, keepdims=True) * scale
                )
        total = fold(own[0])
        for row in range(1, height):
            total = total + fold(own[row])
        grads[row_bias : row_bias + 1, at] = jnp.sum(total, axis=0, keepdims=True) * scale
        total = fold(cotangent[0, :, at].astype(f32))
        for row in range(1, height):
            total = total + fold(cotangent[row, :, at].astype(f32))
        grads[row_down : row_down + 1, at] = jnp.sum(total, axis=0, keepdims=True) * scale
        grads[row_gain : row_gain + 1, at] = norms[0:1, at] * scale
        grads[row_shift : row_shift + 1, at] = norms[1:2, at] * scale
        return carry

    lax.fori_loop(0, chans // lanes, chunk, 0)
    part = upb.shape[1] // layers
    for z in range(layers):
        bias = upb[0:1, z * part : (z + 1) * part] * scale
        for s in range(quads):
            grads[row_up + s : row_up + s + 1, z * lanes : z * lanes + part] = jnp.where(
                member == s, bias, 0.0
            )
    for other in range(layers):
        at = pl.multiple_of(jnp.bitwise_xor(layer, other) * lanes, lanes)
        out, i = (kept, other) if other < layers // 2 else (sent, other - layers // 2)
        out[i] = grads[:, pl.ds(at, lanes)]


def mlp_kernel(quads, layers, bias_row, *refs):
    normals, refs = refs[:quads], refs[quads:]
    cots, refs = refs[:quads], refs[quads:]
    weights, (total, even, odd, act, upb, down, up) = refs[:-7], refs[-7:]
    layer, _ = place(quads)
    cells, chans = normals[0].shape
    hidden_units = act.shape[1]
    part = hidden_units // layers
    for step in range(layers):
        source = lax.rem(layer - step + layers, layers)
        if len(weights) == layers:
            one, two = weights[step].at[0:part], weights[step].at[part:]
        else:
            one, two = weights[step], weights[layers + step]
        down[pl.ds(pl.multiple_of(source * part, part), part), :] = one[...]
        up[pl.ds(pl.multiple_of(source * lanes, lanes), lanes), :] = two[...]
    bias = bias_row[0:1, :]
    bias_sum = jnp.zeros((1, hidden_units), f32)
    for i in range(quads):
        hidden = jnp.dot(normals[i][...], up[...], preferred_element_type=f32) + bias
        dact = lax.dot_general(
            cots[i][...], down[...], (((1,), (1,)), ((), ())), preferred_element_type=f32
        )
        cumulative = 0.5 * (1.0 + lax.erf(hidden * (1.0 / math.sqrt(2.0))))
        density = jnp.exp(-0.5 * hidden * hidden) * (1.0 / math.sqrt(2.0 * math.pi))
        act[i * cells : (i + 1) * cells, :] = (hidden * cumulative).astype(bf16)
        dhidden = (dact * (cumulative + hidden * density)).astype(bf16)
        bias_sum = bias_sum + jnp.sum(dhidden.astype(f32), axis=0, keepdims=True)
        dnorm = lax.dot_general(
            dhidden, up[...], (((1,), (1,)), ((), ())), preferred_element_type=f32
        )
        at = slice(i // 2 * cells, (i // 2 + 1) * cells)
        if i % 2:
            odd[at, :] = dnorm.astype(bf16)
        else:
            even[at, :] = dnorm
        grad = lax.dot_general(
            normals[i][...], dhidden, (((0,), (0,)), ((), ())), preferred_element_type=f32
        )
        total[...] = grad if i == 0 else total[...] + grad
    upb[...] = jnp.broadcast_to(bias_sum, upb.shape)


def out_kernel(quads, layers, scale, total_up, act, down, *refs):
    cots, refs = refs[:quads], refs[quads:]
    own_down, own_up, refs = refs[0], refs[1], refs[2:]
    sends, (even, odd, total) = refs[:-3], refs[-3:]
    layer, _ = place(quads)
    cells = cots[0].shape[0]
    part = down.shape[0] // layers
    for i in range(quads):
        block = act[i * cells : (i + 1) * cells, :]
        grad = lax.dot_general(
            block, cots[i][...], (((0,), (0,)), ((), ())), preferred_element_type=f32
        )
        total[...] = grad if i == 0 else total[...] + grad
    for step in range(layers):
        if step == 0:
            one, two = own_down, own_up
        elif len(sends) == layers - 1:
            one, two = sends[step - 1].at[0:part], sends[step - 1].at[part:]
        else:
            one, two = sends[step - 1], sends[layers - 2 + step]
        to = lax.rem(layer + step, layers)
        piece = total[pl.ds(pl.multiple_of(to * part, part), part), :] * scale
        one[...] = piece.astype(one.dtype)
        piece = total_up[pl.ds(pl.multiple_of(to * lanes, lanes), lanes), :] * scale
        two[...] = piece.astype(two.dtype)
    for i in range(quads):
        block = act[i * cells : (i + 1) * cells, :]
        mixed = jnp.dot(block, down[...], preferred_element_type=f32)
        at = slice(i // 2 * cells, (i // 2 + 1) * cells)
        if i % 2:
            odd[at, :] = mixed.astype(bf16)
        else:
            even[at, :] = mixed


def norm_back_kernel(normed, inv, params, *refs):
    parts, (dconv, norms) = refs[:-2], refs[-2:]
    height, width, chans = dconv.shape
    gain_sum = jnp.zeros((1, chans), f32)
    shift_sum = jnp.zeros((1, chans), f32)
    for row in range(height):
        at = slice(row * width, (row + 1) * width)
        dnorm = parts[0][at, :].astype(f32)
        for part in parts[1:]:
            dnorm = dnorm + part[at, :].astype(f32)
        value = normed[at, :]
        gain_sum = gain_sum + jnp.sum(dnorm * value, axis=0, keepdims=True)
        shift_sum = shift_sum + jnp.sum(dnorm, axis=0, keepdims=True)
        scaled = dnorm * params[row_gain : row_gain + 1, 0:chans]
        mean = jnp.mean(scaled, axis=1, keepdims=True)
        cross = jnp.mean(scaled * value, axis=1, keepdims=True)
        dconv[row, :, :] = (inv[at, 0:1] * (scaled - mean - value * cross)).astype(bf16)
    norms[0:1, :] = gain_sum
    norms[1:2, :] = shift_sum


def up_split_kernel(quads, part, *refs):
    own_down, own_up, refs = refs[0], refs[1], refs[2:]
    terms, out_down, outs = refs[: -quads - 1], refs[-quads - 1], refs[-quads:]
    _, member = place(quads)
    if terms[0].shape[0] > lanes:
        downs = [term.at[0:part] for term in terms]
        ups = [term.at[part:] for term in terms]
    else:
        downs, ups = terms[: len(terms) // 2], terms[len(terms) // 2 :]
    total = own_down[...]
    for term in downs:
        total = total + term[...].astype(f32)
    out_down[...] = total
    own = outs[0].shape[0]
    for other, out in enumerate(outs):
        row = pl.multiple_of(jnp.bitwise_xor(member, other) * own, own)
        piece = own_up[pl.ds(row, own), :]
        for term in ups:
            piece = piece + term[pl.ds(row, own), :].astype(f32)
        out[...] = piece.astype(out.dtype)


def up_join_kernel(quads, layers, *refs):
    pieces, out = refs[:-1], refs[-1]
    _, member = place(quads)
    part = out.shape[1] // (quads * layers)
    for s in range(quads):
        held = pieces[s][...].astype(f32)
        for m in range(1, quads):
            held = jnp.where(member == m, pieces[s ^ m][...].astype(f32), held)
        for z in range(layers):
            at = (z * quads + s) * part
            out[:, at : at + part] = held[:, z * part : (z + 1) * part]


def small_kernel(quads, part_up, *refs):
    parts, outs = refs[:-6], refs[-6:]
    _, member = place(quads)
    total = parts[0][...]
    for part in parts[1:]:
        total = total + part[...]
    own = outs[0].shape[0]
    down = lax.broadcasted_iota(jnp.int32, (lanes, own), 0)
    across = lax.broadcasted_iota(jnp.int32, (lanes, own), 1)
    pick = (down == across + member * own).astype(f32)
    mine = jnp.dot(total, pick, preferred_element_type=f32, precision=lax.Precision.HIGHEST)
    outs[0][...] = lax.dot_general(
        pick,
        total[0:taps, :],
        (((0,), (1,)), ((), ())),
        preferred_element_type=f32,
        precision=lax.Precision.HIGHEST,
    )
    for row, out in zip((row_bias, row_gain, row_shift, row_down), outs[1:5]):
        out[...] = mine[row : row + 1, :]
    at = lax.broadcasted_iota(jnp.int32, total.shape, 0)
    chosen = jnp.where(at == row_up + member, total, 0.0)
    outs[5][...] = jnp.sum(chosen, axis=0, keepdims=True)[:, 0:part_up]


def per_device(
    features,
    cotangent,
    depth_weight,
    depth_bias,
    norm_gain,
    norm_shift,
    up_weight,
    up_bias,
    down_weight,
    down_bias,
):
    height, width, chans = features.shape
    devices = lax.axis_size("row")
    own, hidden_units = up_weight.shape
    part = down_weight.shape[0]
    layers = chans // lanes
    quads = devices // layers
    share = layers * part
    cells = height * width
    scale = 1.0 / math.sqrt(cells * devices)
    rows = round_up(row_up + quads, 16)

    def swap(value, other):
        return lax.ppermute(value, "row", [(i, i ^ other) for i in range(devices)])

    def turn(value, step=1):
        pairs = [
            (i, (i // quads + step) % layers * quads + i % quads) for i in range(devices)
        ]
        return lax.ppermute(value, "row", pairs)

    def halo(value):
        pairs = [(i, i + 1) for i in range(1, devices - 1, 2)]
        pairs = pairs + [(target, source) for source, target in pairs]
        return lax.ppermute(value, "row", pairs), swap(value, 1)

    def cross(value, other):
        return lax.ppermute(
            value, "row", [(i, (i // quads ^ other) * quads + i % quads) for i in range(devices)]
        )

    def add(one, two, kind):
        return (one.astype(f32) + two.astype(f32)).astype(kind)

    bits = []
    while 1 << len(bits) < quads:
        bits.append(1 << len(bits))

    def exchange(pieces, bit, extra=None):
        keys = sorted(key for key in pieces if key[0] & bit)
        blocks = [pieces[key] for key in keys]
        ahead, size = 0, blocks[0].shape[0]
        if extra is not None and extra.shape[1] == blocks[0].shape[1]:
            ahead = extra.shape[0]
            got = swap(jnp.concatenate([extra] + blocks, axis=0), bit)
            extra = got[:ahead]
        else:
            got = swap(jnp.concatenate(blocks, axis=0), bit)
            extra = None if extra is None else swap(extra, bit)
        kept = {key: piece for key, piece in pieces.items() if not key[0] & bit}
        for i, (target, source) in enumerate(keys):
            at = ahead + i * size
            kept[target ^ bit, source ^ bit] = got[at : at + size]
        return kept, extra

    def spread(held, bits):
        for bit in reversed(bits):
            held.update({i ^ bit: swap(block, bit) for i, block in list(held.items())})

    def near(even, odd):
        return even, swap(odd, bits[0])

    def far(even, odd):
        held = add(even, odd, f32).reshape(-1, cells, chans)
        for bit in bits[1:-1]:
            pairs = held.reshape(-1, 2, cells, chans)
            held = pairs[:, 0] + swap(pairs[:, 1].astype(bf16), bit).astype(f32)
        return held[0], held[1].astype(bf16)

    step = round_up(own, 16)
    block = layers * step
    *pieces, small, far_pack = call(
        functools.partial(pack_kernel, quads, layers, rows),
        [((block, lanes), bf16)] * (quads // 2)
        + [((rows, lanes), bf16), ((rows + quads // 2 * block, lanes), bf16)],
        (
            depth_weight.T,
            depth_bias.reshape(1, own),
            norm_gain.reshape(1, own),
            norm_shift.reshape(1, own),
            down_bias.reshape(1, own),
            up_bias.reshape(1, part),
            up_weight,
        ),
        [pltpu.VMEM((rows, own), f32), pltpu.VMEM((rows, lanes), f32)]
        + [pltpu.VMEM((own, taps), bf16)]
        + [pltpu.VMEM((1, own), bf16)] * 4
        + [pltpu.VMEM((1, part), bf16), pltpu.VMEM((own, hidden_units), bf16)]
        + [pltpu.SemaphoreType.DMA((7,))],
        space=pl.ANY,
        mib=60,
    )
    features, cotangent, down_weight = lax.optimization_barrier(
        (features, cotangent, down_weight, small)
    )[:3]
    got = swap(far_pack, bits[-1])
    pieces = {(i, 0): piece for i, piece in enumerate(pieces)}
    for i in range(quads // 2):
        pieces[i, bits[-1]] = got[rows + i * block : rows + (i + 1) * block]
    small = small + got[:rows]
    small, pieces = lax.optimization_barrier((small, pieces))
    for bit in reversed(bits[:-1]):
        pieces, got = exchange(pieces, bit, small)
        small = small + got
    small, pieces = lax.optimization_barrier((small, pieces))
    merged = share == chans and own % 16 == 0 and part % own == 0
    (up,) = call(
        functools.partial(unpack_kernel, quads, layers),
        [(((part // own if merged else 0) + quads, own, share), bf16)],
        [down_weight] + [pieces[0, i] for i in range(quads)],
    )
    up = up.reshape(-1, share)
    weights = [[up]] if merged else [[down_weight], [up]]
    for held in weights:
        held.extend(turn(held[0], step) for step in range(1, layers))
    outer, inner = halo(features)
    cots = {0: cotangent.reshape(cells, chans)}
    spread(cots, bits[1:])
    smalls = small
    other = 1
    while other < layers:
        smalls = jnp.concatenate([smalls, cross(smalls, other)], axis=0)
        other *= 2
    first = [held[1] for held in weights]
    smalls, first = lax.optimization_barrier((smalls, first))
    for held, value in zip(weights, first):
        held[1] = value
    smalls = [smalls[i * rows : (i + 1) * rows] for i in range(layers)]

    rim = (height + 6, width + 16, chans)
    normal, normed, inv, params, bias = call(
        functools.partial(conv_kernel, quads, layers),
        [
            ((cells, chans), bf16),
            ((cells, chans), f32),
            ((cells, lanes), f32),
            ((rows, chans), f32),
            ((8, share), f32),
        ],
        (features, outer, inner, *smalls),
        [pltpu.VMEM(rim, f32), pltpu.VMEM((cells, chans), f32)],
    )
    first = [held[-1] for held in weights]
    normal, cots, first = lax.optimization_barrier((normal, cots, first))
    for held, value in zip(weights, first):
        held[-1] = value
    normals = {0: normal}
    spread(normals, bits[1:])
    normals, weights = lax.optimization_barrier((normals, weights))
    spread(cots, bits[:1])
    spread(normals, bits[:1])
    normals, cots = ([held[i] for i in range(quads)] for held in (normals, cots))

    half = quads // 2 * cells
    total_up, even, odd, act, upb, down_full = call(
        functools.partial(mlp_kernel, quads, layers),
        [((chans, share), f32), ((half, chans), f32), ((half, chans), bf16)]
        + [((quads * cells, share), bf16), ((8, share), f32), ((share, chans), bf16)],
        (bias, *normals, *cots, *(block for held in weights for block in held)),
        [pltpu.VMEM((chans, share), bf16)],
        mib=40,
    )
    sums = near(even, odd)
    if merged:
        shapes = [(part + lanes, chans)] * (layers - 1)
    else:
        shapes = [(part, chans)] * (layers - 1) + [(lanes, share)] * (layers - 1)
    own_down, own_up, *sends, even, odd = call(
        functools.partial(out_kernel, quads, layers, scale),
        [((part, chans), f32), ((lanes, share), f32)]
        + [(shape, bf16) for shape in shapes]
        + [((half, chans), f32), ((half, chans), bf16)],
        (total_up, act, down_full, *cots),
        [pltpu.VMEM((share, chans), f32)],
        mib=40,
    )
    sums, sends = lax.optimization_barrier((sums, sends))
    kept, sent = far(*sums)
    dnorms = [kept, swap(sent, bits[-1])]
    terms = [turn(send, i % (layers - 1) + 1) for i, send in enumerate(sends)]
    dnorms, even, odd, terms[0] = lax.optimization_barrier((dnorms, even, odd, terms[0]))

    dconv, norms = call(
        norm_back_kernel,
        [((height, width, chans), bf16), ((8, chans), f32)],
        (normed, inv, params, *dnorms),
    )
    even, odd = lax.optimization_barrier((even, odd, dconv))[:2]
    outer_back, inner_back = halo(dconv)
    sums = near(even, odd)
    kept, sent = call(
        functools.partial(taps_kernel, quads, layers, scale),
        [((layers // 2, rows, lanes), f32)] * 2,
        (dconv, features, outer, inner, cotangent, norms, upb),
        [pltpu.VMEM(rim, f32), pltpu.VMEM((rows, chans), f32)],
    )
    mixed, across = far(*sums)
    across = swap(across, bits[-1])
    kept, sent, terms[2:] = lax.optimization_barrier((kept, sent, terms[2:]))
    total = kept + cross(sent, layers // 2)
    total, outer_back, inner_back, terms, across = lax.optimization_barrier(
        (total, outer_back, inner_back, terms, across)
    )
    while total.shape[0] > 1:
        middle = total.shape[0] // 2
        total = total[:middle] + cross(total[middle:], middle)
    total = total[0]
    grad_down_weight, *pieces = call(
        functools.partial(up_split_kernel, quads, part),
        [((part, chans), f32), ((own, share), f32)] + [((own, share), bf16)] * (quads - 1),
        (own_down, own_up, *terms),
    )
    pieces = {(i, 0): piece for i, piece in enumerate(pieces)}
    pieces, _ = exchange(pieces, bits[-1])
    for bit in bits[:-1]:
        total = total + swap(total, bit)
    total, outer_back, inner_back, across = lax.optimization_barrier(
        (total, outer_back, inner_back, across)
    )
    last = swap(total, bits[-1])
    (grad_features,) = call(
        back_kernel,
        [((height, width, chans), bf16)],
        (dconv, outer_back, inner_back, cotangent, params),
        [pltpu.VMEM(rim, f32)],
    )
    for bit in reversed(bits[:-1]):
        pieces, _ = exchange(pieces, bit)
    small_outs = call(
        functools.partial(small_kernel, quads, part),
        [((own, taps), f32)] + [((1, own), f32)] * 4 + [((1, part), f32)],
        (total, last),
    )
    grad_depth_weight = small_outs[0].T
    grad_depth_bias, grad_norm_gain, grad_norm_shift, grad_down_bias, grad_up_bias = (
        value.reshape(-1) for value in small_outs[1:]
    )

    (grad_up_weight,) = call(
        functools.partial(up_join_kernel, quads, layers),
        [((own, hidden_units), f32)],
        [pieces[0, i] for i in range(quads)],
    )
    mixed = mixed + across.astype(f32)
    block_out = (
        features.astype(f32)
        + (mixed + params[row_down, 0:chans]).reshape(height, width, chans)
    ).astype(bf16)
    return (
        block_out,
        grad_features,
        grad_up_weight,
        grad_down_weight,
        grad_depth_weight,
        grad_depth_bias,
        grad_norm_gain,
        grad_norm_shift,
        grad_up_bias,
        grad_down_bias,
    )


def solution(mesh):
    placed = (
        P(("groups", "row"), None, None),
        P(("groups", "row"), None, None),
        P(None, "row"),
        P("row"),
        P("row"),
        P("row"),
        P("row", None),
        P("row"),
        P("row", None),
        P("row"),
    )
    return jax.shard_map(
        per_device,
        mesh=mesh,
        in_specs=placed,
        out_specs=(
            P(("groups", "row"), None, None),
            P(("groups", "row"), None, None),
            P(("groups", "row"), None),
            P(("groups", "row"), None),
            P("groups", "row"),
            P(("groups", "row")),
            P(("groups", "row")),
            P(("groups", "row")),
            P(("groups", "row")),
            P(("groups", "row")),
        ),
        check_vma=False,
    )
```

time: 118 us -> 100 us (0.85)
  starting transfers between devices: 49.2 us -> 35.6 us
  local copies, waits for them, and re-layouts: 3.08 us -> 0.9 us
  waiting for transfers between devices: 43 us -> 41.6 us
    ppermute x18 -> x6, waiting for transfers between devices: 33.4 us -> 11.7 us  [turn(): return lax.ppermute(value, 'row', pairs)]
    ppermute x18 -> x6, starting transfers between devices: 24.8 us -> 8.52 us  [turn(): return lax.ppermute(value, 'row', pairs)]
    ppermute x4 -> x6, waiting for transfers between devices: 0.01 us -> 16.2 us  [the longest x4 16.2 us: cross(): lax.ppermute(value, 'row', [(i, (i // quads ^ other) * quads + i % quads)...]
    ppermute x4 -> x6, starting transfers between devices: 6.46 us -> 12.4 us  [the longest x4 11.1 us: cross(): lax.ppermute(value, 'row', [(i, (i // quads ^ other) * quads + i % quads)...]
    ppermute x20 -> x18, waiting for transfers between devices: 9.65 us -> 13.6 us  [swap(): return lax.ppermute(value, 'row', [(i, i ^ other) for i in range(devices)])]
    ppermute x20 -> x18, starting transfers between devices: 18 us -> 14.7 us  [swap(): return lax.ppermute(value, 'row', [(i, i ^ other) for i in range(devices)])]
    unnamed x20 -> x12, local copies, waits for them, and re-layouts: 3.08 us -> 0.76 us
  transfers between devices with their start and end apart: 42 -> 30, of which waited for: 15 -> 15; matrix products, arithmetic and copies ran while one was open for 3% -> 1% of each run, Pallas kernels for 10% -> 13%
where the time goes in v2:
time: 100 us; the launch traced here: 99.9 us
  waiting for transfers between devices  41.6 us (42%)
  starting transfers between devices  35.6 us (36%)
  Pallas kernels  19.6 us (20%)
  other arithmetic  1.21 us (1%)
  between operations  1 us (1%)
    pallas_call x11, Pallas kernels, call(): pl.pallas_call(kernel, out_shape=[jax.ShapeDtypeStruct(shape, dtype) for...  19.6 us
    ppermute x4, waiting for transfers between devices, cross(): lax.ppermute(value, 'row', [(i, (i // quads ^ other) * quads + i % quads)...  16.2 us
    ppermute x18, starting transfers between devices, swap(): return lax.ppermute(value, 'row', [(i, i ^ other) for i in range(devices)])  14.7 us
    ppermute x18, waiting for transfers between devices, swap(): return lax.ppermute(value, 'row', [(i, i ^ other) for i in range(devices)])  13.6 us
    ppermute x6, waiting for transfers between devices, turn(): return lax.ppermute(value, 'row', pairs)  11.7 us
    ppermute x4, starting transfers between devices, cross(): lax.ppermute(value, 'row', [(i, (i // quads ^ other) * quads + i % quads)...  11.1 us
    ppermute x6, starting transfers between devices, turn(): return lax.ppermute(value, 'row', pairs)  8.52 us
  transfers between devices with their start and end apart: 30, of which 15 were waited for; matrix products, arithmetic and copies ran while one was open for 1% of the time, Pallas kernels for 13%

profile of v2, /device:TPU:0, one launch (start us, length us, event | category | flops | bytes accessed | tf_op | source)
XLA Modules:
  0.0 99.9 jit_solution(17679693934092895148)
XLA Ops:
  0.6 1.9 %shard_map.177 = (bf16[128,128]{1,0:T(8,128)(2,1)}, bf16[128,128]{1,0:T(8,128)(2,1)}, bf16[64,128]{1,0:T(8,128)(2,1)}, bf16[320,128]{1,0:T(8,128)(2,1)}) custom-call(bf16[32,49]{1,0:T(8,128)(2,1)} %bitcast.28, bf16[1,32]{1,0:T(2,128)(2,1)} %bitcast.29, bf16[1,32]{1,0:T(2,128)(2,1)} %bitcast.30, bf16[1,32]{1,0:T(2,128)(2,1)} %bitcast.31, ...), custom_call_target="tpu_custom_call" | custom-call | flops 1000 | bytes 1000 | tf_op jit(solution)/shard_map/pallas_call | solution.py:24
  2.5 3.0 %collective-permute-start.2 = (bf16[320,128]{1,0:T(8,128)(2,1)}, bf16[320,128]{1,0:T(8,128)(2,1)S(1)}, u32[]{:S(2)}, u32[]{:S(2)}) collective-permute-start(bf16[320,128]{1,0:T(8,128)(2,1)} %get-tuple-element.100), channel_id=1, source_target_pairs={{0,2},{1,3},{2,0},{3,1},{4,6},{5,7},{6,4},{7,5},{8,10},{9,11},{10,... | collective-permute-start | bytes 245768 | tf_op jit(solution)/shard_map/ppermute | solution.py:441
  5.6 2.7 %collective-permute-done.2 = bf16[320,128]{1,0:T(8,128)(2,1)S(1)} collective-permute-done((bf16[320,128]{1,0:T(8,128)(2,1)}, bf16[320,128]{1,0:T(8,128)(2,1)S(1)}, u32[]{:S(2)}, u32[]{:S(2)}) %collective-permute-start.2) | collective-permute-done | bytes 81952 | tf_op jit(solution)/shard_map/ppermute | solution.py:441
  8.3 0.7 copy-done.4
  9.1 1.3 %collective-permute-done.3 = bf16[320,128]{1,0:T(8,128)(2,1)S(1)} collective-permute-done((bf16[320,128]{1,0:T(8,128)(2,1)S(1)}, bf16[320,128]{1,0:T(8,128)(2,1)S(1)}, u32[]{:S(2)}, u32[]{:S(2)}) %collective-permute-start.3) | collective-permute-done | bytes 81952 | tf_op jit(solution)/shard_map/ppermute | solution.py:441
  10.4 2.1 %collective-permute-start.4 = (bf16[64,128]{1,0:T(8,128)(2,1)S(1)}, bf16[64,128]{1,0:T(8,128)(2,1)S(1)}, u32[]{:S(2)}, u32[]{:S(2)}) collective-permute-start(bf16[64,128]{1,0:T(8,128)(2,1)S(1)} %slice_add_fusion.1), channel_id=1, source_target_pairs={{0,4},{1,5},{2,6},{3,7},{4,0},{5,1},{6,2},{7,3},{8,12},{9,13},{10,... | collective-permute-start | bytes 49160 | tf_op jit(solution)/shard_map/ppermute | solution.py:455
  12.6 0.7 collective-permute-start.6
  13.3 1.0 collective-permute-done.4
  14.2 3.0 %collective-permute-start.5 = (bf16[128,128]{1,0:T(8,128)(2,1)S(1)}, bf16[128,128]{1,0:T(8,128)(2,1)S(1)}, u32[]{:S(2)}, u32[]{:S(2)}) collective-permute-start(bf16[128,128]{1,0:T(8,128)(2,1)S(1)} %pad_maximum_fusion.4), channel_id=1, source_target_pairs={{0,8},{1,9},{2,10},{3,11},{4,12},{5,13},{6,14},{7,15},{8,0},{9,1},... | collective-permute-start | bytes 98312 | tf_op jit(solution)/shard_map/ppermute | solution.py:455
  17.3 0.7 collective-permute-start
  17.9 2.9 %collective-permute-start.1 = (bf16[4,64,512]{2,1,0:T(8,128)(2,1)S(1)}, bf16[4,64,512]{2,1,0:T(8,128)(2,1)S(1)}, u32[]{:S(2)}, u32[]{:S(2)}) collective-permute-start(bf16[4,64,512]{2,1,0:T(8,128)(2,1)S(1)} %copy-done.1), channel_id=1, source_target_pairs={{0,1},{1,0},{2,3},{3,2},{4,5},{5,4},{6,7},{7,6},{8,9},{9,8},{10,11... | collective-permute-start | bytes 786440 | tf_op jit(solution)/shard_map/ppermute | solution.py:441
  20.9 1.7 %collective-permute-start.7 = (bf16[256,512]{1,0:T(8,128)(2,1)S(1)}, bf16[256,512]{1,0:T(8,128)(2,1)S(1)}, u32[]{:S(2)}, u32[]{:S(2)}) collective-permute-start(bf16[256,512]{1,0:T(8,128)(2,1)S(1)} %bitcast.18), channel_id=1, source_target_pairs={{0,2},{1,3},{2,0},{3,1},{4,6},{5,7},{6,4},{7,5},{8,10},{9,11},{10,... | collective-permute-start | bytes 786440 | tf_op jit(solution)/shard_map/ppermute | solution.py:441
  22.6 1.3 %collective-permute-done.5 = bf16[128,128]{1,0:T(8,128)(2,1)S(1)} collective-permute-done((bf16[128,128]{1,0:T(8,128)(2,1)S(1)}, bf16[128,128]{1,0:T(8,128)(2,1)S(1)}, u32[]{:S(2)}, u32[]{:S(2)}) %collective-permute-start.5) | collective-permute-done | bytes 32800 | tf_op jit(solution)/shard_map/ppermute | solution.py:455
  23.9 1.7 %collective-permute-start.8 = (bf16[256,512]{1,0:T(8,128)(2,1)S(1)}, bf16[256,512]{1,0:T(8,128)(2,1)S(1)}, u32[]{:S(2)}, u32[]{:S(2)}) collective-permute-start(bf16[256,512]{1,0:T(8,128)(2,1)S(1)} %bitcast.23), channel_id=1, source_target_pairs={{0,12},{1,13},{2,14},{3,15},{4,0},{5,1},{6,2},{7,3},{8,4},{9,5},{1... | collective-permute-start | bytes 786440 | tf_op jit(solution)/shard_map/ppermute | solution.py:447
  25.7 3.7 %shard_map.179 = (bf16[256,512]{1,0:T(8,128)(2,1)S(1)}, f32[256,512]{1,0:T(8,128)S(1)}, f32[256,128]{1,0:T(8,128)S(1)}, f32[64,512]{1,0:T(8,128)S(1)}, f32[8,512]{1,0:T(8,128)S(1)}) custom-call(bf16[4,64,512]{2,1,0:T(8,128)(2,1)S(1)} %copy-done.1, bf16[4,64,512]{2,1,0:T(8,128)(2,1)S(1)} %collective-permute-done.outer, ...), custom_call_target="tpu_custom_call" | custom-call | flops 1000 | bytes 1000 | tf_op jit(solution)/shard_map/pallas_call | solution.py:24
  29.5 1.7 %collective-permute-done.7.refs_6_.refs_2_ = bf16[256,512]{1,0:T(8,128)(2,1)S(1)} collective-permute-done((bf16[256,512]{1,0:T(8,128)(2,1)S(1)}, bf16[256,512]{1,0:T(8,128)(2,1)S(1)}, u32[]{:S(2)}, u32[]{:S(2)}) %collective-permute-start.7) | collective-permute-done | bytes 262176 | tf_op jit(solution)/shard_map/ppermute | solution.py:441
  31.1 1.6 %collective-permute-done.8.refs_11_ = bf16[256,512]{1,0:T(8,128)(2,1)S(1)} collective-permute-done((bf16[256,512]{1,0:T(8,128)(2,1)S(1)}, bf16[256,512]{1,0:T(8,128)(2,1)S(1)}, u32[]{:S(2)}, u32[]{:S(2)}) %collective-permute-start.8) | collective-permute-done | bytes 262176 | tf_op jit(solution)/shard_map/ppermute | solution.py:447
  32.7 2.1 %collective-permute-start.9 = (bf16[256,512]{1,0:T(8,128)(2,1)S(1)}, bf16[256,512]{1,0:T(8,128)(2,1)S(1)}, u32[]{:S(2)}, u32[]{:S(2)}) collective-permute-start(bf16[256,512]{1,0:T(8,128)(2,1)S(1)} %get-tuple-element.121.refs_0_), channel_id=1, source_target_pairs={{0,2},{1,3},{2,0},{3,1},{4,6},{5,7},{6,4},{7,5},{8,10},{9,11},{10,... | collective-permute-start | bytes 786440 | tf_op jit(solution)/shard_map/ppermute | solution.py:441
  34.8 0.5 collective-permute-start.14
  35.3 8.3 %collective-permute-done.10.refs_10_ = bf16[256,512]{1,0:T(8,128)(2,1)S(1)} collective-permute-done((bf16[256,512]{1,0:T(8,128)(2,1)S(1)}, bf16[256,512]{1,0:T(8,128)(2,1)S(1)}, u32[]{:S(2)}, u32[]{:S(2)}) %collective-permute-start.10) | collective-permute-done | bytes 262176 | tf_op jit(solution)/shard_map/ppermute | solution.py:447
  43.6 0.5 collective-permute-start.12
  44.1 1.0 %collective-permute-done.11.refs_1_ = bf16[256,512]{1,0:T(8,128)(2,1)S(1)} collective-permute-done((bf16[256,512]{1,0:T(8,128)(2,1)S(1)}, bf16[256,512]{1,0:T(8,128)(2,1)S(1)}, u32[]{:S(2)}, u32[]{:S(2)}) %collective-permute-start.11) | collective-permute-done | bytes 262176 | tf_op jit(solution)/shard_map/ppermute | solution.py:441
  45.2 0.4 collective-permute-done.12.refs_3_
  45.5 3.3 %shard_map.180 = (f32[512,512]{1,0:T(8,128)S(1)}, f32[512,512]{1,0:T(8,128)S(1)}, bf16[512,512]{1,0:T(8,128)(2,1)S(1)}, bf16[1024,512]{1,0:T(8,128)(2,1)S(1)}, f...) custom-call(f32[8,512]{1,0:T(8,128)S(1)} %get-tuple-element.115.bias_row, ...), custom_call_target="tpu_custom_call" | custom-call | flops 1000 | bytes 1000 | tf_op jit(solution)/shard_map/pallas_call | solution.py:24
  48.8 0.2 collective-permute-start.15
  49.0 1.4 %shard_map.181 = (f32[128,512]{1,0:T(8,128)S(1)}, f32[128,512]{1,0:T(8,128)S(1)}, bf16[256,512]{1,0:T(8,128)(2,1)S(1)}, bf16[256,512]{1,0:T(8,128)(2,1)S(1)}, bf...) custom-call(f32[512,512]{1,0:T(8,128)S(1)} %get-tuple-element.131.total_up, ...), custom_call_target="tpu_custom_call" | custom-call | flops 1000 | bytes 1000 | tf_op jit(solution)/shard_map/pallas_call | solution.py:24
  50.4 0.3 collective-permute-done.15
  50.8 0.2 convert_add_fusion.1
  51.0 3.2 %collective-permute-start.17 = (bf16[256,512]{1,0:T(8,128)(2,1)S(1)}, bf16[256,512]{1,0:T(8,128)(2,1)S(1)}, u32[]{:S(2)}, u32[]{:S(2)}) collective-permute-start(bf16[256,512]{1,0:T(8,128)(2,1)S(1)} %get-tuple-element.141), channel_id=1, source_target_pairs={{0,4},{1,5},{2,6},{3,7},{4,8},{5,9},{6,10},{7,11},{8,12},{9,13},{1... | collective-permute-start | bytes 786440 | tf_op jit(solution)/shard_map/ppermute | solution.py:447
  54.3 5.1 %collective-permute-done.16.refs_1_ = bf16[256,512]{1,0:T(8,128)(2,1)S(1)} collective-permute-done((bf16[256,512]{1,0:T(8,128)(2,1)S(1)}, bf16[256,512]{1,0:T(8,128)(2,1)S(1)}, u32[]{:S(2)}, u32[]{:S(2)}) %collective-permute-start.16) | collective-permute-done | bytes 262176 | tf_op jit(solution)/shard_map/ppermute | solution.py:441
  59.4 1.9 %collective-permute-done.17.refs_2_ = bf16[256,512]{1,0:T(8,128)(2,1)S(1)} collective-permute-done((bf16[256,512]{1,0:T(8,128)(2,1)S(1)}, bf16[256,512]{1,0:T(8,128)(2,1)S(1)}, u32[]{:S(2)}, u32[]{:S(2)}) %collective-permute-start.17) | collective-permute-done | bytes 262176 | tf_op jit(solution)/shard_map/ppermute | solution.py:447
  61.3 0.3 shard_map.182
  61.7 1.4 %collective-permute-start.19 = (bf16[256,512]{1,0:T(8,128)(2,1)S(1)}, bf16[256,512]{1,0:T(8,128)(2,1)S(1)}, u32[]{:S(2)}, u32[]{:S(2)}) collective-permute-start(bf16[256,512]{1,0:T(8,128)(2,1)S(1)} %get-tuple-element.156), channel_id=1, source_target_pairs={{0,12},{1,13},{2,14},{3,15},{4,0},{5,1},{6,2},{7,3},{8,4},{9,5},{1... | collective-permute-start | bytes 786440 | tf_op jit(solution)/shard_map/ppermute | solution.py:447
  63.0 1.5 %collective-permute-start.23 = (bf16[256,512]{1,0:T(8,128)(2,1)S(1)}, bf16[256,512]{1,0:T(8,128)(2,1)S(1)}, u32[]{:S(2)}, u32[]{:S(2)}) collective-permute-start(bf16[256,512]{1,0:T(8,128)(2,1)S(1)} %get-tuple-element.160), channel_id=1, source_target_pairs={{0,8},{1,9},{2,10},{3,11},{4,12},{5,13},{6,14},{7,15},{8,0},{9,1},... | collective-permute-start | bytes 786440 | tf_op jit(solution)/shard_map/ppermute | solution.py:447
  64.5 0.7 collective-permute-start.21
  65.2 3.1 %collective-permute-start.22 = (bf16[4,64,512]{2,1,0:T(8,128)(2,1)S(1)}, bf16[4,64,512]{2,1,0:T(8,128)(2,1)S(1)}, u32[]{:S(2)}, u32[]{:S(2)}) collective-permute-start(bf16[4,64,512]{2,1,0:T(8,128)(2,1)S(1)} %get-tuple-element.149.dconv), channel_id=1, source_target_pairs={{0,1},{1,0},{2,3},{3,2},{4,5},{5,4},{6,7},{7,6},{8,9},{9,8},{10,11... | collective-permute-start | bytes 786440 | tf_op jit(solution)/shard_map/ppermute | solution.py:441
  68.3 0.2 convert_add_fusion
  68.6 2.8 %shard_map.183 = (f32[2,64,128]{2,1,0:T(8,128)S(1)}, f32[2,64,128]{2,1,0:T(8,128)S(1)}) custom-call(bf16[4,64,512]{2,1,0:T(8,128)(2,1)S(1)} %get-tuple-element.149.dconv, bf16[4,64,512]{2,1,0:T(8,128)(2,1)S(1)} %copy-done.1, bf16[4,64,512]{2,1,0:T(8,128)(2,1)S(1)} %collective-permute-done.outer, bf16[4,64,512]{2,1,0:T(8,128)(2,1)S(1)} %collective-permute-done.1.inner, ...), custom_call_target="tpu_custom_call" | custom-call | flops 1000 | bytes 1000 | tf_op jit(solution)/shard_map/pallas_call | solution.py:24
  71.5 5.9 %collective-permute-start.20 = (f32[2,64,128]{2,1,0:T(8,128)S(1)}, f32[2,64,128]{2,1,0:T(8,128)S(1)}, u32[]{:S(2)}, u32[]{:S(2)}) collective-permute-start(f32[2,64,128]{2,1,0:T(8,128)S(1)} %get-tuple-element.158), channel_id=1, source_target_pairs={{0,8},{1,9},{2,10},{3,11},{4,12},{5,13},{6,14},{7,15},{8,0},{9,1},... | collective-permute-start | bytes 196616 | tf_op jit(solution)/shard_map/ppermute | solution.py:455
  77.3 10.8 %collective-permute-done.20 = f32[2,64,128]{2,1,0:T(8,128)S(1)} collective-permute-done((f32[2,64,128]{2,1,0:T(8,128)S(1)}, f32[2,64,128]{2,1,0:T(8,128)S(1)}, u32[]{:S(2)}, u32[]{:S(2)}) %collective-permute-start.20) | collective-permute-done | bytes 65568 | tf_op jit(solution)/shard_map/ppermute | solution.py:455
  88.3 0.8 shard_map.185
  89.0 3.1 %collective-permute-done.25 = f32[1,64,128]{2,1,0:T(8,128)S(1)} collective-permute-done((f32[1,64,128]{2,1,0:T(8,128)S(1)}, f32[1,64,128]{2,1,0:T(8,128)S(1)}, u32[]{:S(2)}, u32[]{:S(2)}) %collective-permute-start.25) | collective-permute-done | bytes 32800 | tf_op jit(solution)/shard_map/ppermute | solution.py:455
  92.2 1.2 %collective-permute-done.26 = f32[64,128]{1,0:T(8,128)S(1)} collective-permute-done((f32[64,128]{1,0:T(8,128)S(1)}, f32[64,128]{1,0:T(8,128)S(1)}, u32[]{:S(2)}, u32[]{:S(2)}) %collective-permute-start.26) | collective-permute-done | bytes 32800 | tf_op jit(solution)/shard_map/ppermute | solution.py:441
  93.4 0.2 collective-permute-start.28
  93.7 0.8 add_convert_fusion
  94.5 3.7 %shard_map.184 = bf16[4,64,512]{2,1,0:T(8,128)(2,1)} custom-call(bf16[4,64,512]{2,1,0:T(8,128)(2,1)S(1)} %get-tuple-element.149.dconv, bf16[4,64,512]{2,1,0:T(8,128)(2,1)S(1)} %collective-permute-done.21.outer, bf16[4,64,512]{2,1,0:T(8,128)(2,1)S(1)} %collective-permute-done.22.inner, bf16[4,64,512]{2,1,0:T(8,128)(2,1)S(1)} %copy-done, ...), custom_call_target="tpu_custom_call" | custom-call | flops 1000 | bytes 1000 | tf_op jit(solution)/shard_map/pallas_call | solution.py:24
  98.2 0.9 shard_map.187
  99.1 0.8 shard_map.186
  (59 shorter events, 0.9 us)
Async XLA Ops:
  2.5 5.7 %copy-start.5 = (bf16[64,128]{1,0:T(8,128)(2,1)S(1)}, bf16[64,128]{1,0:T(8,128)(2,1)}, u32[]{:S(2)}) copy-start(bf16[64,128]{1,0:T(8,128)(2,1)} %get-tuple-element.98) | copy-start | bytes 49156
  2.5 5.7 %collective-permute-start.2 = (bf16[320,128]{1,0:T(8,128)(2,1)}, bf16[320,128]{1,0:T(8,128)(2,1)S(1)}, u32[]{:S(2)}, u32[]{:S(2)}) collective-permute-start(bf16[320,128]{1,0:T(8,128)(2,1)} %get-tuple-element.100), channel_id=1, source_target_pairs={{0,2},{1,3},{2,0},{3,1},{4,6},{5,7},{6,4},{7,5},{8,10},{9,11},{10,... | collective-permute-start | bytes 245768 | tf_op jit(solution)/shard_map/ppermute | solution.py:441
  8.2 0.8 copy-start.4
  9.0 3.5 %copy-start.2 = (bf16[128,512]{1,0:T(8,128)(2,1)S(1)}, bf16[128,512]{1,0:T(8,128)(2,1)}, u32[]{:S(2)}) copy-start(bf16[128,512]{1,0:T(8,128)(2,1)} %down) | copy-start | bytes 393220
  9.0 1.3 %collective-permute-start.3 = (bf16[320,128]{1,0:T(8,128)(2,1)S(1)}, bf16[320,128]{1,0:T(8,128)(2,1)S(1)}, u32[]{:S(2)}, u32[]{:S(2)}) collective-permute-start(bf16[320,128]{1,0:T(8,128)(2,1)S(1)} %pad_maximum_fusion), channel_id=1, source_target_pairs={{0,1},{1,0},{2,3},{3,2},{4,5},{5,4},{6,7},{7,6},{8,9},{9,8},{10,11... | collective-permute-start | bytes 245768 | tf_op jit(solution)/shard_map/ppermute | solution.py:441
  10.4 2.2 %copy-start.3 = (bf16[128,128]{1,0:T(8,128)(2,1)S(1)}, bf16[128,128]{1,0:T(8,128)(2,1)}, u32[]{:S(2)}) copy-start(bf16[128,128]{1,0:T(8,128)(2,1)} %get-tuple-element.110.refs_0_) | copy-start | bytes 98308
  10.4 6.9 %copy-start.1 = (bf16[4,64,512]{2,1,0:T(8,128)(2,1)S(1)}, bf16[4,64,512]{2,1,0:T(8,128)(2,1)}, u32[]{:S(2)}) copy-start(bf16[4,64,512]{2,1,0:T(8,128)(2,1)} %features.1) | copy-start | bytes 786436
  10.4 10.5 %copy-start = (bf16[4,64,512]{2,1,0:T(8,128)(2,1)S(1)}, bf16[4,64,512]{2,1,0:T(8,128)(2,1)}, u32[]{:S(2)}) copy-start(bf16[4,64,512]{2,1,0:T(8,128)(2,1)} %cotangent.1) | copy-start | bytes 786436
  10.4 3.8 %collective-permute-start.4 = (bf16[64,128]{1,0:T(8,128)(2,1)S(1)}, bf16[64,128]{1,0:T(8,128)(2,1)S(1)}, u32[]{:S(2)}, u32[]{:S(2)}) collective-permute-start(bf16[64,128]{1,0:T(8,128)(2,1)S(1)} %slice_add_fusion.1), channel_id=1, source_target_pairs={{0,4},{1,5},{2,6},{3,7},{4,0},{5,1},{6,2},{7,3},{8,12},{9,13},{10,... | collective-permute-start | bytes 49160 | tf_op jit(solution)/shard_map/ppermute | solution.py:455
  12.6 13.0 %collective-permute-start.6 = (bf16[256,512]{1,0:T(8,128)(2,1)S(1)}, bf16[256,512]{1,0:T(8,128)(2,1)S(1)}, u32[]{:S(2)}, u32[]{:S(2)}) collective-permute-start(bf16[256,512]{1,0:T(8,128)(2,1)S(1)} %bitcast.22), channel_id=1, source_target_pairs={{0,4},{1,5},{2,6},{3,7},{4,8},{5,9},{6,10},{7,11},{8,12},{9,13},{1... | collective-permute-start | bytes 786440 | tf_op jit(solution)/shard_map/ppermute | solution.py:447
  14.2 9.7 %collective-permute-start.5 = (bf16[128,128]{1,0:T(8,128)(2,1)S(1)}, bf16[128,128]{1,0:T(8,128)(2,1)S(1)}, u32[]{:S(2)}, u32[]{:S(2)}) collective-permute-start(bf16[128,128]{1,0:T(8,128)(2,1)S(1)} %pad_maximum_fusion.4), channel_id=1, source_target_pairs={{0,8},{1,9},{2,10},{3,11},{4,12},{5,13},{6,14},{7,15},{8,0},{9,1},... | collective-permute-start | bytes 98312 | tf_op jit(solution)/shard_map/ppermute | solution.py:455
  17.3 8.4 %collective-permute-start = (bf16[4,64,512]{2,1,0:T(8,128)(2,1)S(1)}, bf16[4,64,512]{2,1,0:T(8,128)(2,1)S(1)}, u32[]{:S(2)}, u32[]{:S(2)}) collective-permute-start(bf16[4,64,512]{2,1,0:T(8,128)(2,1)S(1)} %copy-done.1), channel_id=1, source_target_pairs={{1,2},{3,4},{5,6},{7,8},{9,10},{11,12},{13,14},{2,1},{4,3},{6,5},{... | collective-permute-start | bytes 786440 | tf_op jit(solution)/shard_map/ppermute | solution.py:452
  17.9 7.8 %collective-permute-start.1 = (bf16[4,64,512]{2,1,0:T(8,128)(2,1)S(1)}, bf16[4,64,512]{2,1,0:T(8,128)(2,1)S(1)}, u32[]{:S(2)}, u32[]{:S(2)}) collective-permute-start(bf16[4,64,512]{2,1,0:T(8,128)(2,1)S(1)} %copy-done.1), channel_id=1, source_target_pairs={{0,1},{1,0},{2,3},{3,2},{4,5},{5,4},{6,7},{7,6},{8,9},{9,8},{10,11... | collective-permute-start | bytes 786440 | tf_op jit(solution)/shard_map/ppermute | solution.py:441
  20.9 10.2 %collective-permute-start.7 = (bf16[256,512]{1,0:T(8,128)(2,1)S(1)}, bf16[256,512]{1,0:T(8,128)(2,1)S(1)}, u32[]{:S(2)}, u32[]{:S(2)}) collective-permute-start(bf16[256,512]{1,0:T(8,128)(2,1)S(1)} %bitcast.18), channel_id=1, source_target_pairs={{0,2},{1,3},{2,0},{3,1},{4,6},{5,7},{6,4},{7,5},{8,10},{9,11},{10,... | collective-permute-start | bytes 786440 | tf_op jit(solution)/shard_map/ppermute | solution.py:441
  23.9 8.8 %collective-permute-start.8 = (bf16[256,512]{1,0:T(8,128)(2,1)S(1)}, bf16[256,512]{1,0:T(8,128)(2,1)S(1)}, u32[]{:S(2)}, u32[]{:S(2)}) collective-permute-start(bf16[256,512]{1,0:T(8,128)(2,1)S(1)} %bitcast.23), channel_id=1, source_target_pairs={{0,12},{1,13},{2,14},{3,15},{4,0},{5,1},{6,2},{7,3},{8,4},{9,5},{1... | collective-permute-start | bytes 786440 | tf_op jit(solution)/shard_map/ppermute | solution.py:447
  25.6 18.0 %collective-permute-start.10 = (bf16[256,512]{1,0:T(8,128)(2,1)S(1)}, bf16[256,512]{1,0:T(8,128)(2,1)S(1)}, u32[]{:S(2)}, u32[]{:S(2)}) collective-permute-start(bf16[256,512]{1,0:T(8,128)(2,1)S(1)} %bitcast.24), channel_id=1, source_target_pairs={{0,8},{1,9},{2,10},{3,11},{4,12},{5,13},{6,14},{7,15},{8,0},{9,1},... | collective-permute-start | bytes 786440 | tf_op jit(solution)/shard_map/ppermute | solution.py:447
  32.7 10.9 %collective-permute-start.9 = (bf16[256,512]{1,0:T(8,128)(2,1)S(1)}, bf16[256,512]{1,0:T(8,128)(2,1)S(1)}, u32[]{:S(2)}, u32[]{:S(2)}) collective-permute-start(bf16[256,512]{1,0:T(8,128)(2,1)S(1)} %get-tuple-element.121.refs_0_), channel_id=1, source_target_pairs={{0,2},{1,3},{2,0},{3,1},{4,6},{5,7},{6,4},{7,5},{8,10},{9,11},{10,... | collective-permute-start | bytes 786440 | tf_op jit(solution)/shard_map/ppermute | solution.py:441
  34.8 9.3 %collective-permute-start.13 = (bf16[256,512]{1,0:T(8,128)(2,1)S(1)}, bf16[256,512]{1,0:T(8,128)(2,1)S(1)}, u32[]{:S(2)}, u32[]{:S(2)}) collective-permute-start(bf16[256,512]{1,0:T(8,128)(2,1)S(1)} %bitcast.19), channel_id=1, source_target_pairs={{0,1},{1,0},{2,3},{3,2},{4,5},{5,4},{6,7},{7,6},{8,9},{9,8},{10,11... | collective-permute-start | bytes 786440 | tf_op jit(solution)/shard_map/ppermute | solution.py:441
  34.8 9.3 %collective-permute-start.14 = (bf16[256,512]{1,0:T(8,128)(2,1)S(1)}, bf16[256,512]{1,0:T(8,128)(2,1)S(1)}, u32[]{:S(2)}, u32[]{:S(2)}) collective-permute-start(bf16[256,512]{1,0:T(8,128)(2,1)S(1)} %collective-permute-done.7.refs_6_.refs_2_), channel_id=1, source_target_pairs={{0,1},{1,0},{2,3},{3,2},{4,5},{5,4},{6,7},{7,6},{8,9},{9,8},{10,11... | collective-permute-start | bytes 786440 | tf_op jit(solution)/shard_map/ppermute | solution.py:441
  43.6 1.5 %collective-permute-start.11 = (bf16[256,512]{1,0:T(8,128)(2,1)S(1)}, bf16[256,512]{1,0:T(8,128)(2,1)S(1)}, u32[]{:S(2)}, u32[]{:S(2)}) collective-permute-start(bf16[256,512]{1,0:T(8,128)(2,1)S(1)} %get-tuple-element.121.refs_0_), channel_id=1, source_target_pairs={{0,1},{1,0},{2,3},{3,2},{4,5},{5,4},{6,7},{7,6},{8,9},{9,8},{10,11... | collective-permute-start | bytes 786440 | tf_op jit(solution)/shard_map/ppermute | solution.py:441
  43.6 1.9 %collective-permute-start.12 = (bf16[256,512]{1,0:T(8,128)(2,1)S(1)}, bf16[256,512]{1,0:T(8,128)(2,1)S(1)}, u32[]{:S(2)}, u32[]{:S(2)}) collective-permute-start(bf16[256,512]{1,0:T(8,128)(2,1)S(1)} %collective-permute-done.9.refs_2_), channel_id=1, source_target_pairs={{0,1},{1,0},{2,3},{3,2},{4,5},{5,4},{6,7},{7,6},{8,9},{9,8},{10,11... | collective-permute-start | bytes 786440 | tf_op jit(solution)/shard_map/ppermute | solution.py:441
  48.8 2.0 %collective-permute-start.15 = (bf16[512,512]{1,0:T(8,128)(2,1)S(1)}, bf16[512,512]{1,0:T(8,128)(2,1)S(1)}, u32[]{:S(2)}, u32[]{:S(2)}) collective-permute-start(bf16[512,512]{1,0:T(8,128)(2,1)S(1)} %get-tuple-element.130), channel_id=1, source_target_pairs={{0,1},{1,0},{2,3},{3,2},{4,5},{5,4},{6,7},{7,6},{8,9},{9,8},{10,11... | collective-permute-start | bytes 1572872 | tf_op jit(solution)/shard_map/ppermute | solution.py:441
  51.0 8.4 %collective-permute-start.16 = (bf16[256,512]{1,0:T(8,128)(2,1)S(1)}, bf16[256,512]{1,0:T(8,128)(2,1)S(1)}, u32[]{:S(2)}, u32[]{:S(2)}) collective-permute-start(bf16[256,512]{1,0:T(8,128)(2,1)S(1)} %slice.113), channel_id=1, source_target_pairs={{0,2},{1,3},{2,0},{3,1},{4,6},{5,7},{6,4},{7,5},{8,10},{9,11},{10,... | collective-permute-start | bytes 786440 | tf_op jit(solution)/shard_map/ppermute | solution.py:441
  51.0 10.2 %collective-permute-start.17 = (bf16[256,512]{1,0:T(8,128)(2,1)S(1)}, bf16[256,512]{1,0:T(8,128)(2,1)S(1)}, u32[]{:S(2)}, u32[]{:S(2)}) collective-permute-start(bf16[256,512]{1,0:T(8,128)(2,1)S(1)} %get-tuple-element.141), channel_id=1, source_target_pairs={{0,4},{1,5},{2,6},{3,7},{4,8},{5,9},{6,10},{7,11},{8,12},{9,13},{1... | collective-permute-start | bytes 786440 | tf_op jit(solution)/shard_map/ppermute | solution.py:447
  61.6 6.7 %collective-permute-start.18 = (bf16[512,512]{1,0:T(8,128)(2,1)S(1)}, bf16[512,512]{1,0:T(8,128)(2,1)S(1)}, u32[]{:S(2)}, u32[]{:S(2)}) collective-permute-start(bf16[512,512]{1,0:T(8,128)(2,1)S(1)} %get-tuple-element.151), channel_id=1, source_target_pairs={{0,1},{1,0},{2,3},{3,2},{4,5},{5,4},{6,7},{7,6},{8,9},{9,8},{10,11... | collective-permute-start | bytes 1572872 | tf_op jit(solution)/shard_map/ppermute | solution.py:441
  61.7 9.8 %collective-permute-start.19 = (bf16[256,512]{1,0:T(8,128)(2,1)S(1)}, bf16[256,512]{1,0:T(8,128)(2,1)S(1)}, u32[]{:S(2)}, u32[]{:S(2)}) collective-permute-start(bf16[256,512]{1,0:T(8,128)(2,1)S(1)} %get-tuple-element.156), channel_id=1, source_target_pairs={{0,12},{1,13},{2,14},{3,15},{4,0},{5,1},{6,2},{7,3},{8,4},{9,5},{1... | collective-permute-start | bytes 786440 | tf_op jit(solution)/shard_map/ppermute | solution.py:447
  63.0 25.1 %collective-permute-start.23 = (bf16[256,512]{1,0:T(8,128)(2,1)S(1)}, bf16[256,512]{1,0:T(8,128)(2,1)S(1)}, u32[]{:S(2)}, u32[]{:S(2)}) collective-permute-start(bf16[256,512]{1,0:T(8,128)(2,1)S(1)} %get-tuple-element.160), channel_id=1, source_target_pairs={{0,8},{1,9},{2,10},{3,11},{4,12},{5,13},{6,14},{7,15},{8,0},{9,1},... | collective-permute-start | bytes 786440 | tf_op jit(solution)/shard_map/ppermute | solution.py:447
  64.5 23.6 %collective-permute-start.21 = (bf16[4,64,512]{2,1,0:T(8,128)(2,1)S(1)}, bf16[4,64,512]{2,1,0:T(8,128)(2,1)S(1)}, u32[]{:S(2)}, u32[]{:S(2)}) collective-permute-start(bf16[4,64,512]{2,1,0:T(8,128)(2,1)S(1)} %get-tuple-element.149.dconv), channel_id=1, source_target_pairs={{1,2},{3,4},{5,6},{7,8},{9,10},{11,12},{13,14},{2,1},{4,3},{6,5},{... | collective-permute-start | bytes 786440 | tf_op jit(solution)/shard_map/ppermute | solution.py:452
  65.2 23.0 %collective-permute-start.22 = (bf16[4,64,512]{2,1,0:T(8,128)(2,1)S(1)}, bf16[4,64,512]{2,1,0:T(8,128)(2,1)S(1)}, u32[]{:S(2)}, u32[]{:S(2)}) collective-permute-start(bf16[4,64,512]{2,1,0:T(8,128)(2,1)S(1)} %get-tuple-element.149.dconv), channel_id=1, source_target_pairs={{0,1},{1,0},{2,3},{3,2},{4,5},{5,4},{6,7},{7,6},{8,9},{9,8},{10,11... | collective-permute-start | bytes 786440 | tf_op jit(solution)/shard_map/ppermute | solution.py:441
  68.5 19.7 %collective-permute-start.24 = (bf16[256,512]{1,0:T(8,128)(2,1)S(1)}, bf16[256,512]{1,0:T(8,128)(2,1)S(1)}, u32[]{:S(2)}, u32[]{:S(2)}) collective-permute-start(bf16[256,512]{1,0:T(8,128)(2,1)S(1)} %slice.112), channel_id=1, source_target_pairs={{0,2},{1,3},{2,0},{3,1},{4,6},{5,7},{6,4},{7,5},{8,10},{9,11},{10,... | collective-permute-start | bytes 786440 | tf_op jit(solution)/shard_map/ppermute | solution.py:441
  71.5 16.7 %collective-permute-start.20 = (f32[2,64,128]{2,1,0:T(8,128)S(1)}, f32[2,64,128]{2,1,0:T(8,128)S(1)}, u32[]{:S(2)}, u32[]{:S(2)}) collective-permute-start(f32[2,64,128]{2,1,0:T(8,128)S(1)} %get-tuple-element.158), channel_id=1, source_target_pairs={{0,8},{1,9},{2,10},{3,11},{4,12},{5,13},{6,14},{7,15},{8,0},{9,1},... | collective-permute-start | bytes 196616 | tf_op jit(solution)/shard_map/ppermute | solution.py:455
  88.2 4.0 %collective-permute-start.25 = (f32[1,64,128]{2,1,0:T(8,128)S(1)}, f32[1,64,128]{2,1,0:T(8,128)S(1)}, u32[]{:S(2)}, u32[]{:S(2)}) collective-permute-start(f32[1,64,128]{2,1,0:T(8,128)S(1)} %slice.84), channel_id=1, source_target_pairs={{0,4},{1,5},{2,6},{3,7},{4,0},{5,1},{6,2},{7,3},{8,12},{9,13},{10,... | collective-permute-start | bytes 98312 | tf_op jit(solution)/shard_map/ppermute | solution.py:455
  89.0 4.4 %collective-permute-start.27 = (bf16[64,512]{1,0:T(8,128)(2,1)S(1)}, bf16[64,512]{1,0:T(8,128)(2,1)S(1)}, u32[]{:S(2)}, u32[]{:S(2)}) collective-permute-start(bf16[64,512]{1,0:T(8,128)(2,1)S(1)} %pad_maximum_fusion.2), channel_id=1, source_target_pairs={{0,2},{1,3},{2,0},{3,1},{4,6},{5,7},{6,4},{7,5},{8,10},{9,11},{10,... | collective-permute-start | bytes 196616 | tf_op jit(solution)/shard_map/ppermute | solution.py:441
  92.2 1.2 %collective-permute-start.26 = (f32[64,128]{1,0:T(8,128)S(1)}, f32[64,128]{1,0:T(8,128)S(1)}, u32[]{:S(2)}, u32[]{:S(2)}) collective-permute-start(f32[64,128]{1,0:T(8,128)S(1)} %add_bitcast_fusion), channel_id=1, source_target_pairs={{0,1},{1,0},{2,3},{3,2},{4,5},{5,4},{6,7},{7,6},{8,9},{9,8},{10,11... | collective-permute-start | bytes 98312 | tf_op jit(solution)/shard_map/ppermute | solution.py:441
  93.4 4.8 %collective-permute-start.29 = (f32[64,128]{1,0:T(8,128)S(1)}, f32[64,128]{1,0:T(8,128)S(1)}, u32[]{:S(2)}, u32[]{:S(2)}) collective-permute-start(f32[64,128]{1,0:T(8,128)S(1)} %add.43.refs_0_), channel_id=1, source_target_pairs={{0,2},{1,3},{2,0},{3,1},{4,6},{5,7},{6,4},{7,5},{8,10},{9,11},{10,... | collective-permute-start | bytes 98312 | tf_op jit(solution)/shard_map/ppermute | solution.py:441
  93.4 5.7 %collective-permute-start.28 = (bf16[64,512]{1,0:T(8,128)(2,1)S(1)}, bf16[64,512]{1,0:T(8,128)(2,1)S(1)}, u32[]{:S(2)}, u32[]{:S(2)}) collective-permute-start(bf16[64,512]{1,0:T(8,128)(2,1)S(1)} %pad_maximum_fusion.3), channel_id=1, source_target_pairs={{0,1},{1,0},{2,3},{3,2},{4,5},{5,4},{6,7},{7,6},{8,9},{9,8},{10,11... | collective-permute-start | bytes 196616 | tf_op jit(solution)/shard_map/ppermute | solution.py:441

commit v3 on v2

--- a/solution.py
+++ b/solution.py
@@ -204,7 +204,7 @@
 def taps_kernel(
     quads, layers, scale, dconv, features, outer, inner, cotangent, norms, upb, *refs
 ):
-    kept, sent, padded, grads = refs
+    out, padded, grads = refs
     height, width, chans = dconv.shape
     layer, member = place(quads)
     fill(padded, features, outer, inner, width)
@@ -251,8 +251,7 @@
             )
     for other in range(layers):
         at = pl.multiple_of(jnp.bitwise_xor(layer, other) * lanes, lanes)
-        out, i = (kept, other) if other < layers // 2 else (sent, other - layers // 2)
-        out[i] = grads[:, pl.ds(at, lanes)]
+        out[other] = grads[:, pl.ds(at, lanes)]
 
 
 def mlp_kernel(quads, layers, bias_row, *refs):
@@ -605,33 +604,28 @@
     kept, sent = far(*sums)
     dnorms = [kept, swap(sent, bits[-1])]
     terms = [turn(send, i % (layers - 1) + 1) for i, send in enumerate(sends)]
-    dnorms, even, odd, terms[0] = lax.optimization_barrier((dnorms, even, odd, terms[0]))
+    mixed, across = far(*near(even, odd))
+    across = swap(across, bits[-1])
+    dnorms, terms[0] = lax.optimization_barrier((dnorms, terms[0]))
 
     dconv, norms = call(
         norm_back_kernel,
         [((height, width, chans), bf16), ((8, chans), f32)],
         (normed, inv, params, *dnorms),
     )
-    even, odd = lax.optimization_barrier((even, odd, dconv))[:2]
-    outer_back, inner_back = halo(dconv)
-    sums = near(even, odd)
-    kept, sent = call(
+    (total,) = call(
         functools.partial(taps_kernel, quads, layers, scale),
-        [((layers // 2, rows, lanes), f32)] * 2,
+        [((layers, rows, lanes), f32)],
         (dconv, features, outer, inner, cotangent, norms, upb),
         [pltpu.VMEM(rim, f32), pltpu.VMEM((rows, chans), f32)],
     )
-    mixed, across = far(*sums)
-    across = swap(across, bits[-1])
-    kept, sent, terms[2:] = lax.optimization_barrier((kept, sent, terms[2:]))
-    total = kept + cross(sent, layers // 2)
-    total, outer_back, inner_back, terms, across = lax.optimization_barrier(
-        (total, outer_back, inner_back, terms, across)
-    )
-    while total.shape[0] > 1:
-        middle = total.shape[0] // 2
-        total = total[:middle] + cross(total[middle:], middle)
-    total = total[0]
+    total, dconv, across, terms[2:] = lax.optimization_barrier(
+        (total, dconv, across, terms[2:])
+    )
+    outer_back, inner_back = halo(dconv)
+    for bit in bits:
+        total = total + swap(total, bit)
+    total, terms, inner_back = lax.optimization_barrier((total, terms, inner_back))
     grad_down_weight, *pieces = call(
         functools.partial(up_split_kernel, quads, part),
         [((part, chans), f32), ((own, share), f32)] + [((own, share), bf16)] * (quads - 1),
@@ -639,18 +633,24 @@
     )
     pieces = {(i, 0): piece for i, piece in enumerate(pieces)}
     pieces, _ = exchange(pieces, bits[-1])
-    for bit in bits[:-1]:
-        total = total + swap(total, bit)
-    total, outer_back, inner_back, across = lax.optimization_barrier(
-        (total, outer_back, inner_back, across)
-    )
-    last = swap(total, bits[-1])
+    while total.shape[0] > 2:
+        middle = total.shape[0] // 2
+        total = total[:middle] + cross(total[middle:], middle)
     (grad_features,) = call(
         back_kernel,
         [((height, width, chans), bf16)],
         (dconv, outer_back, inner_back, cotangent, params),
         [pltpu.VMEM(rim, f32)],
     )
+    block_out = (
+        features.astype(f32)
+        + (mixed + across.astype(f32) + params[row_down, 0:chans]).reshape(height, width, chans)
+    ).astype(bf16)
+    total, grad_features, block_out, pieces = lax.optimization_barrier(
+        (total, grad_features, block_out, pieces)
+    )
+    last = cross(total[1], 1)
+    total = total[0]
     for bit in reversed(bits[:-1]):
         pieces, _ = exchange(pieces, bit)
     small_outs = call(
@@ -668,11 +668,6 @@
         [((own, hidden_units), f32)],
         [pieces[0, i] for i in range(quads)],
     )
-    mixed = mixed + across.astype(f32)
-    block_out = (
-        features.astype(f32)
-        + (mixed + params[row_down, 0:chans]).reshape(height, width, chans)
-    ).astype(bf16)
     return (
         block_out,
         grad_features,

time: 100 us -> 94.8 us (0.948)
  waiting for transfers between devices: 41.6 us -> 32.1 us
  starting transfers between devices: 35.6 us -> 39.8 us
    ppermute x4, waiting for transfers between devices: 16.2 us -> 4.27 us  [cross(): lax.ppermute(value, 'row', [(i, (i // quads ^ other) * quads + i % quads)...]
    ppermute x18, starting transfers between devices: 14.7 us -> 19.8 us  [swap(): return lax.ppermute(value, 'row', [(i, i ^ other) for i in range(devices)])]
    ppermute x6, waiting for transfers between devices: 11.7 us -> 13.5 us  [turn(): return lax.ppermute(value, 'row', pairs)]
    ppermute x6, starting transfers between devices: 8.52 us -> 7.19 us  [turn(): return lax.ppermute(value, 'row', pairs)]
  transfers between devices with their start and end apart: 30 -> 30, of which waited for: 15 -> 16; matrix products, arithmetic and copies ran while one was open for 1% -> 1% of each run, Pallas kernels for 13% -> 14%
where the time goes in v3:
time: 94.8 us; the launch traced here: 94.5 us
  starting transfers between devices  39.8 us (42%)
  waiting for transfers between devices  32.1 us (34%)
  Pallas kernels  19.6 us (21%)
  other arithmetic  1.23 us (1%)
    ppermute x18, starting transfers between devices, swap(): return lax.ppermute(value, 'row', [(i, i ^ other) for i in range(devices)])  19.8 us
    pallas_call x11, Pallas kernels, call(): pl.pallas_call(kernel, out_shape=[jax.ShapeDtypeStruct(shape, dtype) for...  19.6 us
    ppermute x18, waiting for transfers between devices, swap(): return lax.ppermute(value, 'row', [(i, i ^ other) for i in range(devices)])  14.3 us
    ppermute x6, waiting for transfers between devices, turn(): return lax.ppermute(value, 'row', pairs)  13.5 us
    ppermute x4, starting transfers between devices, cross(): lax.ppermute(value, 'row', [(i, (i // quads ^ other) * quads + i % quads)...  11.4 us
    ppermute x6, starting transfers between devices, turn(): return lax.ppermute(value, 'row', pairs)  7.19 us
    ppermute x4, waiting for transfers between devices, cross(): lax.ppermute(value, 'row', [(i, (i // quads ^ other) * quads + i % quads)...  4.27 us
  transfers between devices with their start and end apart: 30, of which 16 were waited for; matrix products, arithmetic and copies ran while one was open for 1% of the time, Pallas kernels for 14%

profile of v3, /device:TPU:0, one launch (start us, length us, event | category | flops | bytes accessed | tf_op | source)
XLA Modules:
  0.0 94.5 jit_solution(10528728666947912249)
XLA Ops:
  0.6 1.9 %shard_map.177 = (bf16[128,128]{1,0:T(8,128)(2,1)}, bf16[128,128]{1,0:T(8,128)(2,1)}, bf16[64,128]{1,0:T(8,128)(2,1)}, bf16[320,128]{1,0:T(8,128)(2,1)}) custom-call(bf16[32,49]{1,0:T(8,128)(2,1)} %bitcast.30, bf16[1,32]{1,0:T(2,128)(2,1)} %bitcast.31, bf16[1,32]{1,0:T(2,128)(2,1)} %bitcast.32, bf16[1,32]{1,0:T(2,128)(2,1)} %bitcast.33, ...), custom_call_target="tpu_custom_call" | custom-call | flops 1000 | bytes 1000 | tf_op jit(solution)/shard_map/pallas_call | solution.py:24
  2.5 3.0 %collective-permute-start.2 = (bf16[320,128]{1,0:T(8,128)(2,1)}, bf16[320,128]{1,0:T(8,128)(2,1)S(1)}, u32[]{:S(2)}, u32[]{:S(2)}) collective-permute-start(bf16[320,128]{1,0:T(8,128)(2,1)} %get-tuple-element.96), channel_id=1, source_target_pairs={{0,2},{1,3},{2,0},{3,1},{4,6},{5,7},{6,4},{7,5},{8,10},{9,11},{10,... | collective-permute-start | bytes 245768 | tf_op jit(solution)/shard_map/ppermute | solution.py:440
  5.6 2.7 %collective-permute-done.2 = bf16[320,128]{1,0:T(8,128)(2,1)S(1)} collective-permute-done((bf16[320,128]{1,0:T(8,128)(2,1)}, bf16[320,128]{1,0:T(8,128)(2,1)S(1)}, u32[]{:S(2)}, u32[]{:S(2)}) %collective-permute-start.2) | collective-permute-done | bytes 81952 | tf_op jit(solution)/shard_map/ppermute | solution.py:440
  8.3 0.7 copy-done.4
  9.1 1.3 %collective-permute-done.3 = bf16[320,128]{1,0:T(8,128)(2,1)S(1)} collective-permute-done((bf16[320,128]{1,0:T(8,128)(2,1)S(1)}, bf16[320,128]{1,0:T(8,128)(2,1)S(1)}, u32[]{:S(2)}, u32[]{:S(2)}) %collective-permute-start.3) | collective-permute-done | bytes 81952 | tf_op jit(solution)/shard_map/ppermute | solution.py:440
  10.4 2.1 %collective-permute-start.4 = (bf16[64,128]{1,0:T(8,128)(2,1)S(1)}, bf16[64,128]{1,0:T(8,128)(2,1)S(1)}, u32[]{:S(2)}, u32[]{:S(2)}) collective-permute-start(bf16[64,128]{1,0:T(8,128)(2,1)S(1)} %slice_add_fusion.2), channel_id=1, source_target_pairs={{0,4},{1,5},{2,6},{3,7},{4,0},{5,1},{6,2},{7,3},{8,12},{9,13},{10,... | collective-permute-start | bytes 49160 | tf_op jit(solution)/shard_map/ppermute | solution.py:454
  12.6 0.7 collective-permute-start.6
  13.3 1.0 %collective-permute-done.4 = bf16[64,128]{1,0:T(8,128)(2,1)S(1)} collective-permute-done((bf16[64,128]{1,0:T(8,128)(2,1)S(1)}, bf16[64,128]{1,0:T(8,128)(2,1)S(1)}, u32[]{:S(2)}, u32[]{:S(2)}) %collective-permute-start.4) | collective-permute-done | bytes 16416 | tf_op jit(solution)/shard_map/ppermute | solution.py:454
  14.2 3.0 %collective-permute-start.5 = (bf16[128,128]{1,0:T(8,128)(2,1)S(1)}, bf16[128,128]{1,0:T(8,128)(2,1)S(1)}, u32[]{:S(2)}, u32[]{:S(2)}) collective-permute-start(bf16[128,128]{1,0:T(8,128)(2,1)S(1)} %pad_maximum_fusion.4), channel_id=1, source_target_pairs={{0,8},{1,9},{2,10},{3,11},{4,12},{5,13},{6,14},{7,15},{8,0},{9,1},... | collective-permute-start | bytes 98312 | tf_op jit(solution)/shard_map/ppermute | solution.py:454
  17.3 0.7 collective-permute-start
  17.9 2.9 %collective-permute-start.1 = (bf16[4,64,512]{2,1,0:T(8,128)(2,1)S(1)}, bf16[4,64,512]{2,1,0:T(8,128)(2,1)S(1)}, u32[]{:S(2)}, u32[]{:S(2)}) collective-permute-start(bf16[4,64,512]{2,1,0:T(8,128)(2,1)S(1)} %copy-done.1), channel_id=1, source_target_pairs={{0,1},{1,0},{2,3},{3,2},{4,5},{5,4},{6,7},{7,6},{8,9},{9,8},{10,11... | collective-permute-start | bytes 786440 | tf_op jit(solution)/shard_map/ppermute | solution.py:440
  20.9 1.7 %collective-permute-start.7 = (bf16[256,512]{1,0:T(8,128)(2,1)S(1)}, bf16[256,512]{1,0:T(8,128)(2,1)S(1)}, u32[]{:S(2)}, u32[]{:S(2)}) collective-permute-start(bf16[256,512]{1,0:T(8,128)(2,1)S(1)} %bitcast.20), channel_id=1, source_target_pairs={{0,2},{1,3},{2,0},{3,1},{4,6},{5,7},{6,4},{7,5},{8,10},{9,11},{10,... | collective-permute-start | bytes 786440 | tf_op jit(solution)/shard_map/ppermute | solution.py:440
  22.6 1.3 %collective-permute-done.5 = bf16[128,128]{1,0:T(8,128)(2,1)S(1)} collective-permute-done((bf16[128,128]{1,0:T(8,128)(2,1)S(1)}, bf16[128,128]{1,0:T(8,128)(2,1)S(1)}, u32[]{:S(2)}, u32[]{:S(2)}) %collective-permute-start.5) | collective-permute-done | bytes 32800 | tf_op jit(solution)/shard_map/ppermute | solution.py:454
  23.9 1.7 %collective-permute-start.8 = (bf16[256,512]{1,0:T(8,128)(2,1)S(1)}, bf16[256,512]{1,0:T(8,128)(2,1)S(1)}, u32[]{:S(2)}, u32[]{:S(2)}) collective-permute-start(bf16[256,512]{1,0:T(8,128)(2,1)S(1)} %bitcast.25), channel_id=1, source_target_pairs={{0,12},{1,13},{2,14},{3,15},{4,0},{5,1},{6,2},{7,3},{8,4},{9,5},{1... | collective-permute-start | bytes 786440 | tf_op jit(solution)/shard_map/ppermute | solution.py:446
  25.7 3.7 %shard_map.179 = (bf16[256,512]{1,0:T(8,128)(2,1)S(1)}, f32[256,512]{1,0:T(8,128)S(1)}, f32[256,128]{1,0:T(8,128)S(1)}, f32[64,512]{1,0:T(8,128)S(1)}, f32[8,512]{1,0:T(8,128)S(1)}) custom-call(bf16[4,64,512]{2,1,0:T(8,128)(2,1)S(1)} %copy-done.1, bf16[4,64,512]{2,1,0:T(8,128)(2,1)S(1)} %collective-permute-done.outer, ...), custom_call_target="tpu_custom_call" | custom-call | flops 1000 | bytes 1000 | tf_op jit(solution)/shard_map/pallas_call | solution.py:24
  29.5 1.7 %collective-permute-done.7.refs_6_.refs_2_ = bf16[256,512]{1,0:T(8,128)(2,1)S(1)} collective-permute-done((bf16[256,512]{1,0:T(8,128)(2,1)S(1)}, bf16[256,512]{1,0:T(8,128)(2,1)S(1)}, u32[]{:S(2)}, u32[]{:S(2)}) %collective-permute-start.7) | collective-permute-done | bytes 262176 | tf_op jit(solution)/shard_map/ppermute | solution.py:440
  31.1 1.6 %collective-permute-done.8.refs_11_ = bf16[256,512]{1,0:T(8,128)(2,1)S(1)} collective-permute-done((bf16[256,512]{1,0:T(8,128)(2,1)S(1)}, bf16[256,512]{1,0:T(8,128)(2,1)S(1)}, u32[]{:S(2)}, u32[]{:S(2)}) %collective-permute-start.8) | collective-permute-done | bytes 262176 | tf_op jit(solution)/shard_map/ppermute | solution.py:446
  32.7 2.1 %collective-permute-start.9 = (bf16[256,512]{1,0:T(8,128)(2,1)S(1)}, bf16[256,512]{1,0:T(8,128)(2,1)S(1)}, u32[]{:S(2)}, u32[]{:S(2)}) collective-permute-start(bf16[256,512]{1,0:T(8,128)(2,1)S(1)} %get-tuple-element.120.refs_0_), channel_id=1, source_target_pairs={{0,2},{1,3},{2,0},{3,1},{4,6},{5,7},{6,4},{7,5},{8,10},{9,11},{10,... | collective-permute-start | bytes 786440 | tf_op jit(solution)/shard_map/ppermute | solution.py:440
  34.8 0.5 collective-permute-start.14
  35.3 8.3 %collective-permute-done.10.refs_10_ = bf16[256,512]{1,0:T(8,128)(2,1)S(1)} collective-permute-done((bf16[256,512]{1,0:T(8,128)(2,1)S(1)}, bf16[256,512]{1,0:T(8,128)(2,1)S(1)}, u32[]{:S(2)}, u32[]{:S(2)}) %collective-permute-start.10) | collective-permute-done | bytes 262176 | tf_op jit(solution)/shard_map/ppermute | solution.py:446
  43.6 0.5 collective-permute-start.12
  44.1 1.0 %collective-permute-done.11.refs_1_ = bf16[256,512]{1,0:T(8,128)(2,1)S(1)} collective-permute-done((bf16[256,512]{1,0:T(8,128)(2,1)S(1)}, bf16[256,512]{1,0:T(8,128)(2,1)S(1)}, u32[]{:S(2)}, u32[]{:S(2)}) %collective-permute-start.11) | collective-permute-done | bytes 262176 | tf_op jit(solution)/shard_map/ppermute | solution.py:440
  45.2 0.4 collective-permute-done.12.refs_3_
  45.5 3.3 %shard_map.180 = (f32[512,512]{1,0:T(8,128)S(1)}, f32[512,512]{1,0:T(8,128)S(1)}, bf16[512,512]{1,0:T(8,128)(2,1)S(1)}, bf16[1024,512]{1,0:T(8,128)(2,1)S(1)}, f...) custom-call(f32[8,512]{1,0:T(8,128)S(1)} %get-tuple-element.114.bias_row, ...), custom_call_target="tpu_custom_call" | custom-call | flops 1000 | bytes 1000 | tf_op jit(solution)/shard_map/pallas_call | solution.py:24
  49.0 1.4 %shard_map.181 = (f32[128,512]{1,0:T(8,128)S(1)}, f32[128,512]{1,0:T(8,128)S(1)}, bf16[256,512]{1,0:T(8,128)(2,1)S(1)}, bf16[256,512]{1,0:T(8,128)(2,1)S(1)}, bf...) custom-call(f32[512,512]{1,0:T(8,128)S(1)} %get-tuple-element.130.total_up, ...), custom_call_target="tpu_custom_call" | custom-call | flops 1000 | bytes 1000 | tf_op jit(solution)/shard_map/pallas_call | solution.py:24
  50.4 0.4 collective-permute-start.18
  51.1 3.2 %collective-permute-start.17 = (bf16[256,512]{1,0:T(8,128)(2,1)S(1)}, bf16[256,512]{1,0:T(8,128)(2,1)S(1)}, u32[]{:S(2)}, u32[]{:S(2)}) collective-permute-start(bf16[256,512]{1,0:T(8,128)(2,1)S(1)} %get-tuple-element.138), channel_id=1, source_target_pairs={{0,4},{1,5},{2,6},{3,7},{4,8},{5,9},{6,10},{7,11},{8,12},{9,13},{1... | collective-permute-start | bytes 786440 | tf_op jit(solution)/shard_map/ppermute | solution.py:446
  54.6 2.0 %collective-permute-start.19 = (bf16[256,512]{1,0:T(8,128)(2,1)S(1)}, bf16[256,512]{1,0:T(8,128)(2,1)S(1)}, u32[]{:S(2)}, u32[]{:S(2)}) collective-permute-start(bf16[256,512]{1,0:T(8,128)(2,1)S(1)} %slice.122), channel_id=1, source_target_pairs={{0,2},{1,3},{2,0},{3,1},{4,6},{5,7},{6,4},{7,5},{8,10},{9,11},{10,... | collective-permute-start | bytes 786440 | tf_op jit(solution)/shard_map/ppermute | solution.py:440
  56.6 0.7 collective-permute-start.20
  57.3 0.9 collective-permute-start.23
  58.2 2.1 %collective-permute-done.16.refs_1_ = bf16[256,512]{1,0:T(8,128)(2,1)S(1)} collective-permute-done((bf16[256,512]{1,0:T(8,128)(2,1)S(1)}, bf16[256,512]{1,0:T(8,128)(2,1)S(1)}, u32[]{:S(2)}, u32[]{:S(2)}) %collective-permute-start.16) | collective-permute-done | bytes 262176 | tf_op jit(solution)/shard_map/ppermute | solution.py:440
  60.3 1.9 %collective-permute-done.17.refs_2_ = bf16[256,512]{1,0:T(8,128)(2,1)S(1)} collective-permute-done((bf16[256,512]{1,0:T(8,128)(2,1)S(1)}, bf16[256,512]{1,0:T(8,128)(2,1)S(1)}, u32[]{:S(2)}, u32[]{:S(2)}) %collective-permute-start.17) | collective-permute-done | bytes 262176 | tf_op jit(solution)/shard_map/ppermute | solution.py:446
  62.5 2.8 %shard_map.183 = f32[4,64,128]{2,1,0:T(8,128)S(1)} custom-call(bf16[4,64,512]{2,1,0:T(8,128)(2,1)S(1)} %get-tuple-element.151.dconv, bf16[4,64,512]{2,1,0:T(8,128)(2,1)S(1)} %copy-done.1, bf16[4,64,512]{2,1,0:T(8,128)(2,1)S(1)} %collective-permute-done.outer, bf16[4,64,512]{2,1,0:T(8,128)(2,1)S(1)} %collective-permute-done.1.inner, ...), custom_call_target="tpu_custom_call" | custom-call | flops 1000 | bytes 1000 | tf_op jit(solution)/shard_map/pallas_call | solution.py:24
  65.4 1.6 %collective-permute-done.20.refs_4_ = bf16[256,512]{1,0:T(8,128)(2,1)S(1)} collective-permute-done((bf16[256,512]{1,0:T(8,128)(2,1)S(1)}, bf16[256,512]{1,0:T(8,128)(2,1)S(1)}, u32[]{:S(2)}, u32[]{:S(2)}) %collective-permute-start.20) | collective-permute-done | bytes 262176 | tf_op jit(solution)/shard_map/ppermute | solution.py:446
  67.0 0.7 collective-permute-start.26
  67.7 3.1 %collective-permute-start.21 = (f32[4,64,128]{2,1,0:T(8,128)S(1)}, f32[4,64,128]{2,1,0:T(8,128)S(1)}, u32[]{:S(2)}, u32[]{:S(2)}) collective-permute-start(f32[4,64,128]{2,1,0:T(8,128)S(1)} %shard_map.183), channel_id=1, source_target_pairs={{0,1},{1,0},{2,3},{3,2},{4,5},{5,4},{6,7},{7,6},{8,9},{9,8},{10,11... | collective-permute-start | bytes 393224 | tf_op jit(solution)/shard_map/ppermute | solution.py:440
  70.9 0.9 collective-permute-done.21
  71.8 1.3 %collective-permute-start.22 = (f32[4,64,128]{2,1,0:T(8,128)S(1)}, f32[4,64,128]{2,1,0:T(8,128)S(1)}, u32[]{:S(2)}, u32[]{:S(2)}) collective-permute-start(f32[4,64,128]{2,1,0:T(8,128)S(1)} %add.41), channel_id=1, source_target_pairs={{0,2},{1,3},{2,0},{3,1},{4,6},{5,7},{6,4},{7,5},{8,10},{9,11},{10,... | collective-permute-start | bytes 393224 | tf_op jit(solution)/shard_map/ppermute | solution.py:440
  73.1 0.8 add_convert_fusion
  73.8 4.3 %collective-permute-done.22 = f32[4,64,128]{2,1,0:T(8,128)S(1)} collective-permute-done((f32[4,64,128]{2,1,0:T(8,128)S(1)}, f32[4,64,128]{2,1,0:T(8,128)S(1)}, u32[]{:S(2)}, u32[]{:S(2)}) %collective-permute-start.22) | collective-permute-done | bytes 131104 | tf_op jit(solution)/shard_map/ppermute | solution.py:440
  78.3 3.0 %collective-permute-start.25 = (f32[2,64,128]{2,1,0:T(8,128)S(1)}, f32[2,64,128]{2,1,0:T(8,128)S(1)}, u32[]{:S(2)}, u32[]{:S(2)}) collective-permute-start(f32[2,64,128]{2,1,0:T(8,128)S(1)} %slice.89), channel_id=1, source_target_pairs={{0,8},{1,9},{2,10},{3,11},{4,12},{5,13},{6,14},{7,15},{8,0},{9,1},... | collective-permute-start | bytes 196616 | tf_op jit(solution)/shard_map/ppermute | solution.py:454
  81.3 0.8 shard_map.185
  82.1 1.5 %collective-permute-start.27 = (bf16[64,512]{1,0:T(8,128)(2,1)S(1)}, bf16[64,512]{1,0:T(8,128)(2,1)S(1)}, u32[]{:S(2)}, u32[]{:S(2)}) collective-permute-start(bf16[64,512]{1,0:T(8,128)(2,1)S(1)} %pad_maximum_fusion.2), channel_id=1, source_target_pairs={{0,2},{1,3},{2,0},{3,1},{4,6},{5,7},{6,4},{7,5},{8,10},{9,11},{10,... | collective-permute-start | bytes 196616 | tf_op jit(solution)/shard_map/ppermute | solution.py:440
  83.5 3.7 %shard_map.184 = bf16[4,64,512]{2,1,0:T(8,128)(2,1)} custom-call(bf16[4,64,512]{2,1,0:T(8,128)(2,1)S(1)} %get-tuple-element.151.dconv, bf16[4,64,512]{2,1,0:T(8,128)(2,1)S(1)} %collective-permute-done.26.outer, bf16[4,64,512]{2,1,0:T(8,128)(2,1)S(1)} %collective-permute-done.24.inner, bf16[4,64,512]{2,1,0:T(8,128)(2,1)S(1)} %copy-done, ...), custom_call_target="tpu_custom_call" | custom-call | flops 1000 | bytes 1000 | tf_op jit(solution)/shard_map/pallas_call | solution.py:24
  87.6 3.3 %collective-permute-start.29 = (f32[64,128]{1,0:T(8,128)S(1)}, f32[64,128]{1,0:T(8,128)S(1)}, u32[]{:S(2)}, u32[]{:S(2)}) collective-permute-start(f32[64,128]{1,0:T(8,128)S(1)} %get-tuple-element.182), channel_id=1, source_target_pairs={{0,4},{1,5},{2,6},{3,7},{4,0},{5,1},{6,2},{7,3},{8,12},{9,13},{10,... | collective-permute-start | bytes 98312 | tf_op jit(solution)/shard_map/ppermute | solution.py:454
  90.9 2.0 %collective-permute-done.29.refs_1_ = f32[64,128]{1,0:T(8,128)S(1)} collective-permute-done((f32[64,128]{1,0:T(8,128)S(1)}, f32[64,128]{1,0:T(8,128)S(1)}, u32[]{:S(2)}, u32[]{:S(2)}) %collective-permute-start.29) | collective-permute-done | bytes 32800 | tf_op jit(solution)/shard_map/ppermute | solution.py:454
  92.9 0.9 shard_map.187
  93.8 0.8 shard_map.186
  (60 shorter events, 1.9 us)
Async XLA Ops:
  2.5 5.7 %copy-start.5 = (bf16[64,128]{1,0:T(8,128)(2,1)S(1)}, bf16[64,128]{1,0:T(8,128)(2,1)}, u32[]{:S(2)}) copy-start(bf16[64,128]{1,0:T(8,128)(2,1)} %get-tuple-element.94) | copy-start | bytes 49156
  2.5 5.7 %collective-permute-start.2 = (bf16[320,128]{1,0:T(8,128)(2,1)}, bf16[320,128]{1,0:T(8,128)(2,1)S(1)}, u32[]{:S(2)}, u32[]{:S(2)}) collective-permute-start(bf16[320,128]{1,0:T(8,128)(2,1)} %get-tuple-element.96), channel_id=1, source_target_pairs={{0,2},{1,3},{2,0},{3,1},{4,6},{5,7},{6,4},{7,5},{8,10},{9,11},{10,... | collective-permute-start | bytes 245768 | tf_op jit(solution)/shard_map/ppermute | solution.py:440
  8.2 0.8 copy-start.4
  9.0 3.5 %copy-start.2 = (bf16[128,512]{1,0:T(8,128)(2,1)S(1)}, bf16[128,512]{1,0:T(8,128)(2,1)}, u32[]{:S(2)}) copy-start(bf16[128,512]{1,0:T(8,128)(2,1)} %down) | copy-start | bytes 393220
  9.0 1.3 %collective-permute-start.3 = (bf16[320,128]{1,0:T(8,128)(2,1)S(1)}, bf16[320,128]{1,0:T(8,128)(2,1)S(1)}, u32[]{:S(2)}, u32[]{:S(2)}) collective-permute-start(bf16[320,128]{1,0:T(8,128)(2,1)S(1)} %pad_maximum_fusion), channel_id=1, source_target_pairs={{0,1},{1,0},{2,3},{3,2},{4,5},{5,4},{6,7},{7,6},{8,9},{9,8},{10,11... | collective-permute-start | bytes 245768 | tf_op jit(solution)/shard_map/ppermute | solution.py:440
  10.4 2.2 %copy-start.3 = (bf16[128,128]{1,0:T(8,128)(2,1)S(1)}, bf16[128,128]{1,0:T(8,128)(2,1)}, u32[]{:S(2)}) copy-start(bf16[128,128]{1,0:T(8,128)(2,1)} %get-tuple-element.106.refs_0_) | copy-start | bytes 98308
  10.4 6.9 %copy-start.1 = (bf16[4,64,512]{2,1,0:T(8,128)(2,1)S(1)}, bf16[4,64,512]{2,1,0:T(8,128)(2,1)}, u32[]{:S(2)}) copy-start(bf16[4,64,512]{2,1,0:T(8,128)(2,1)} %features.1) | copy-start | bytes 786436
  10.4 10.5 %copy-start = (bf16[4,64,512]{2,1,0:T(8,128)(2,1)S(1)}, bf16[4,64,512]{2,1,0:T(8,128)(2,1)}, u32[]{:S(2)}) copy-start(bf16[4,64,512]{2,1,0:T(8,128)(2,1)} %cotangent.1) | copy-start | bytes 786436
  10.4 3.8 %collective-permute-start.4 = (bf16[64,128]{1,0:T(8,128)(2,1)S(1)}, bf16[64,128]{1,0:T(8,128)(2,1)S(1)}, u32[]{:S(2)}, u32[]{:S(2)}) collective-permute-start(bf16[64,128]{1,0:T(8,128)(2,1)S(1)} %slice_add_fusion.2), channel_id=1, source_target_pairs={{0,4},{1,5},{2,6},{3,7},{4,0},{5,1},{6,2},{7,3},{8,12},{9,13},{10,... | collective-permute-start | bytes 49160 | tf_op jit(solution)/shard_map/ppermute | solution.py:454
  12.6 13.0 %collective-permute-start.6 = (bf16[256,512]{1,0:T(8,128)(2,1)S(1)}, bf16[256,512]{1,0:T(8,128)(2,1)S(1)}, u32[]{:S(2)}, u32[]{:S(2)}) collective-permute-start(bf16[256,512]{1,0:T(8,128)(2,1)S(1)} %bitcast.24), channel_id=1, source_target_pairs={{0,4},{1,5},{2,6},{3,7},{4,8},{5,9},{6,10},{7,11},{8,12},{9,13},{1... | collective-permute-start | bytes 786440 | tf_op jit(solution)/shard_map/ppermute | solution.py:446
  14.2 9.7 %collective-permute-start.5 = (bf16[128,128]{1,0:T(8,128)(2,1)S(1)}, bf16[128,128]{1,0:T(8,128)(2,1)S(1)}, u32[]{:S(2)}, u32[]{:S(2)}) collective-permute-start(bf16[128,128]{1,0:T(8,128)(2,1)S(1)} %pad_maximum_fusion.4), channel_id=1, source_target_pairs={{0,8},{1,9},{2,10},{3,11},{4,12},{5,13},{6,14},{7,15},{8,0},{9,1},... | collective-permute-start | bytes 98312 | tf_op jit(solution)/shard_map/ppermute | solution.py:454
  17.3 8.4 %collective-permute-start = (bf16[4,64,512]{2,1,0:T(8,128)(2,1)S(1)}, bf16[4,64,512]{2,1,0:T(8,128)(2,1)S(1)}, u32[]{:S(2)}, u32[]{:S(2)}) collective-permute-start(bf16[4,64,512]{2,1,0:T(8,128)(2,1)S(1)} %copy-done.1), channel_id=1, source_target_pairs={{1,2},{3,4},{5,6},{7,8},{9,10},{11,12},{13,14},{2,1},{4,3},{6,5},{... | collective-permute-start | bytes 786440 | tf_op jit(solution)/shard_map/ppermute | solution.py:451
  17.9 7.8 %collective-permute-start.1 = (bf16[4,64,512]{2,1,0:T(8,128)(2,1)S(1)}, bf16[4,64,512]{2,1,0:T(8,128)(2,1)S(1)}, u32[]{:S(2)}, u32[]{:S(2)}) collective-permute-start(bf16[4,64,512]{2,1,0:T(8,128)(2,1)S(1)} %copy-done.1), channel_id=1, source_target_pairs={{0,1},{1,0},{2,3},{3,2},{4,5},{5,4},{6,7},{7,6},{8,9},{9,8},{10,11... | collective-permute-start | bytes 786440 | tf_op jit(solution)/shard_map/ppermute | solution.py:440
  20.9 10.2 %collective-permute-start.7 = (bf16[256,512]{1,0:T(8,128)(2,1)S(1)}, bf16[256,512]{1,0:T(8,128)(2,1)S(1)}, u32[]{:S(2)}, u32[]{:S(2)}) collective-permute-start(bf16[256,512]{1,0:T(8,128)(2,1)S(1)} %bitcast.20), channel_id=1, source_target_pairs={{0,2},{1,3},{2,0},{3,1},{4,6},{5,7},{6,4},{7,5},{8,10},{9,11},{10,... | collective-permute-start | bytes 786440 | tf_op jit(solution)/shard_map/ppermute | solution.py:440
  23.9 8.8 %collective-permute-start.8 = (bf16[256,512]{1,0:T(8,128)(2,1)S(1)}, bf16[256,512]{1,0:T(8,128)(2,1)S(1)}, u32[]{:S(2)}, u32[]{:S(2)}) collective-permute-start(bf16[256,512]{1,0:T(8,128)(2,1)S(1)} %bitcast.25), channel_id=1, source_target_pairs={{0,12},{1,13},{2,14},{3,15},{4,0},{5,1},{6,2},{7,3},{8,4},{9,5},{1... | collective-permute-start | bytes 786440 | tf_op jit(solution)/shard_map/ppermute | solution.py:446
  25.6 18.0 %collective-permute-start.10 = (bf16[256,512]{1,0:T(8,128)(2,1)S(1)}, bf16[256,512]{1,0:T(8,128)(2,1)S(1)}, u32[]{:S(2)}, u32[]{:S(2)}) collective-permute-start(bf16[256,512]{1,0:T(8,128)(2,1)S(1)} %bitcast.26), channel_id=1, source_target_pairs={{0,8},{1,9},{2,10},{3,11},{4,12},{5,13},{6,14},{7,15},{8,0},{9,1},... | collective-permute-start | bytes 786440 | tf_op jit(solution)/shard_map/ppermute | solution.py:446
  32.7 10.9 %collective-permute-start.9 = (bf16[256,512]{1,0:T(8,128)(2,1)S(1)}, bf16[256,512]{1,0:T(8,128)(2,1)S(1)}, u32[]{:S(2)}, u32[]{:S(2)}) collective-permute-start(bf16[256,512]{1,0:T(8,128)(2,1)S(1)} %get-tuple-element.120.refs_0_), channel_id=1, source_target_pairs={{0,2},{1,3},{2,0},{3,1},{4,6},{5,7},{6,4},{7,5},{8,10},{9,11},{10,... | collective-permute-start | bytes 786440 | tf_op jit(solution)/shard_map/ppermute | solution.py:440
  34.8 9.3 %collective-permute-start.13 = (bf16[256,512]{1,0:T(8,128)(2,1)S(1)}, bf16[256,512]{1,0:T(8,128)(2,1)S(1)}, u32[]{:S(2)}, u32[]{:S(2)}) collective-permute-start(bf16[256,512]{1,0:T(8,128)(2,1)S(1)} %bitcast.21), channel_id=1, source_target_pairs={{0,1},{1,0},{2,3},{3,2},{4,5},{5,4},{6,7},{7,6},{8,9},{9,8},{10,11... | collective-permute-start | bytes 786440 | tf_op jit(solution)/shard_map/ppermute | solution.py:440
  34.8 9.3 %collective-permute-start.14 = (bf16[256,512]{1,0:T(8,128)(2,1)S(1)}, bf16[256,512]{1,0:T(8,128)(2,1)S(1)}, u32[]{:S(2)}, u32[]{:S(2)}) collective-permute-start(bf16[256,512]{1,0:T(8,128)(2,1)S(1)} %collective-permute-done.7.refs_6_.refs_2_), channel_id=1, source_target_pairs={{0,1},{1,0},{2,3},{3,2},{4,5},{5,4},{6,7},{7,6},{8,9},{9,8},{10,11... | collective-permute-start | bytes 786440 | tf_op jit(solution)/shard_map/ppermute | solution.py:440
  43.6 1.5 %collective-permute-start.11 = (bf16[256,512]{1,0:T(8,128)(2,1)S(1)}, bf16[256,512]{1,0:T(8,128)(2,1)S(1)}, u32[]{:S(2)}, u32[]{:S(2)}) collective-permute-start(bf16[256,512]{1,0:T(8,128)(2,1)S(1)} %get-tuple-element.120.refs_0_), channel_id=1, source_target_pairs={{0,1},{1,0},{2,3},{3,2},{4,5},{5,4},{6,7},{7,6},{8,9},{9,8},{10,11... | collective-permute-start | bytes 786440 | tf_op jit(solution)/shard_map/ppermute | solution.py:440
  43.6 1.9 %collective-permute-start.12 = (bf16[256,512]{1,0:T(8,128)(2,1)S(1)}, bf16[256,512]{1,0:T(8,128)(2,1)S(1)}, u32[]{:S(2)}, u32[]{:S(2)}) collective-permute-start(bf16[256,512]{1,0:T(8,128)(2,1)S(1)} %collective-permute-done.9.refs_2_), channel_id=1, source_target_pairs={{0,1},{1,0},{2,3},{3,2},{4,5},{5,4},{6,7},{7,6},{8,9},{9,8},{10,11... | collective-permute-start | bytes 786440 | tf_op jit(solution)/shard_map/ppermute | solution.py:440
  48.8 2.1 %collective-permute-start.15 = (bf16[512,512]{1,0:T(8,128)(2,1)S(1)}, bf16[512,512]{1,0:T(8,128)(2,1)S(1)}, u32[]{:S(2)}, u32[]{:S(2)}) collective-permute-start(bf16[512,512]{1,0:T(8,128)(2,1)S(1)} %get-tuple-element.129), channel_id=1, source_target_pairs={{0,1},{1,0},{2,3},{3,2},{4,5},{5,4},{6,7},{7,6},{8,9},{9,8},{10,11... | collective-permute-start | bytes 1572872 | tf_op jit(solution)/shard_map/ppermute | solution.py:440
  50.4 3.9 %collective-permute-start.18 = (bf16[512,512]{1,0:T(8,128)(2,1)S(1)}, bf16[512,512]{1,0:T(8,128)(2,1)S(1)}, u32[]{:S(2)}, u32[]{:S(2)}) collective-permute-start(bf16[512,512]{1,0:T(8,128)(2,1)S(1)} %get-tuple-element.145), channel_id=1, source_target_pairs={{0,1},{1,0},{2,3},{3,2},{4,5},{5,4},{6,7},{7,6},{8,9},{9,8},{10,11... | collective-permute-start | bytes 1572872 | tf_op jit(solution)/shard_map/ppermute | solution.py:440
  51.1 9.2 %collective-permute-start.16 = (bf16[256,512]{1,0:T(8,128)(2,1)S(1)}, bf16[256,512]{1,0:T(8,128)(2,1)S(1)}, u32[]{:S(2)}, u32[]{:S(2)}) collective-permute-start(bf16[256,512]{1,0:T(8,128)(2,1)S(1)} %slice.123), channel_id=1, source_target_pairs={{0,2},{1,3},{2,0},{3,1},{4,6},{5,7},{6,4},{7,5},{8,10},{9,11},{10,... | collective-permute-start | bytes 786440 | tf_op jit(solution)/shard_map/ppermute | solution.py:440
  51.1 11.0 %collective-permute-start.17 = (bf16[256,512]{1,0:T(8,128)(2,1)S(1)}, bf16[256,512]{1,0:T(8,128)(2,1)S(1)}, u32[]{:S(2)}, u32[]{:S(2)}) collective-permute-start(bf16[256,512]{1,0:T(8,128)(2,1)S(1)} %get-tuple-element.138), channel_id=1, source_target_pairs={{0,4},{1,5},{2,6},{3,7},{4,8},{5,9},{6,10},{7,11},{8,12},{9,13},{1... | collective-permute-start | bytes 786440 | tf_op jit(solution)/shard_map/ppermute | solution.py:446
  54.6 10.8 %collective-permute-start.19 = (bf16[256,512]{1,0:T(8,128)(2,1)S(1)}, bf16[256,512]{1,0:T(8,128)(2,1)S(1)}, u32[]{:S(2)}, u32[]{:S(2)}) collective-permute-start(bf16[256,512]{1,0:T(8,128)(2,1)S(1)} %slice.122), channel_id=1, source_target_pairs={{0,2},{1,3},{2,0},{3,1},{4,6},{5,7},{6,4},{7,5},{8,10},{9,11},{10,... | collective-permute-start | bytes 786440 | tf_op jit(solution)/shard_map/ppermute | solution.py:440
  56.6 10.4 %collective-permute-start.20 = (bf16[256,512]{1,0:T(8,128)(2,1)S(1)}, bf16[256,512]{1,0:T(8,128)(2,1)S(1)}, u32[]{:S(2)}, u32[]{:S(2)}) collective-permute-start(bf16[256,512]{1,0:T(8,128)(2,1)S(1)} %get-tuple-element.146), channel_id=1, source_target_pairs={{0,12},{1,13},{2,14},{3,15},{4,0},{5,1},{6,2},{7,3},{8,4},{9,5},{1... | collective-permute-start | bytes 786440 | tf_op jit(solution)/shard_map/ppermute | solution.py:446
  57.3 21.0 %collective-permute-start.23 = (bf16[256,512]{1,0:T(8,128)(2,1)S(1)}, bf16[256,512]{1,0:T(8,128)(2,1)S(1)}, u32[]{:S(2)}, u32[]{:S(2)}) collective-permute-start(bf16[256,512]{1,0:T(8,128)(2,1)S(1)} %get-tuple-element.149), channel_id=1, source_target_pairs={{0,8},{1,9},{2,10},{3,11},{4,12},{5,13},{6,14},{7,15},{8,0},{9,1},... | collective-permute-start | bytes 786440 | tf_op jit(solution)/shard_map/ppermute | solution.py:446
  67.0 11.3 %collective-permute-start.24 = (bf16[4,64,512]{2,1,0:T(8,128)(2,1)S(1)}, bf16[4,64,512]{2,1,0:T(8,128)(2,1)S(1)}, u32[]{:S(2)}, u32[]{:S(2)}) collective-permute-start(bf16[4,64,512]{2,1,0:T(8,128)(2,1)S(1)} %get-tuple-element.151.dconv), channel_id=1, source_target_pairs={{0,1},{1,0},{2,3},{3,2},{4,5},{5,4},{6,7},{7,6},{8,9},{9,8},{10,11... | collective-permute-start | bytes 786440 | tf_op jit(solution)/shard_map/ppermute | solution.py:440
  67.0 16.6 %collective-permute-start.26 = (bf16[4,64,512]{2,1,0:T(8,128)(2,1)S(1)}, bf16[4,64,512]{2,1,0:T(8,128)(2,1)S(1)}, u32[]{:S(2)}, u32[]{:S(2)}) collective-permute-start(bf16[4,64,512]{2,1,0:T(8,128)(2,1)S(1)} %get-tuple-element.151.dconv), channel_id=1, source_target_pairs={{1,2},{3,4},{5,6},{7,8},{9,10},{11,12},{13,14},{2,1},{4,3},{6,5},{... | collective-permute-start | bytes 786440 | tf_op jit(solution)/shard_map/ppermute | solution.py:451
  67.7 4.1 %collective-permute-start.21 = (f32[4,64,128]{2,1,0:T(8,128)S(1)}, f32[4,64,128]{2,1,0:T(8,128)S(1)}, u32[]{:S(2)}, u32[]{:S(2)}) collective-permute-start(f32[4,64,128]{2,1,0:T(8,128)S(1)} %shard_map.183), channel_id=1, source_target_pairs={{0,1},{1,0},{2,3},{3,2},{4,5},{5,4},{6,7},{7,6},{8,9},{9,8},{10,11... | collective-permute-start | bytes 393224 | tf_op jit(solution)/shard_map/ppermute | solution.py:440
  71.8 6.4 %collective-permute-start.22 = (f32[4,64,128]{2,1,0:T(8,128)S(1)}, f32[4,64,128]{2,1,0:T(8,128)S(1)}, u32[]{:S(2)}, u32[]{:S(2)}) collective-permute-start(f32[4,64,128]{2,1,0:T(8,128)S(1)} %add.41), channel_id=1, source_target_pairs={{0,2},{1,3},{2,0},{3,1},{4,6},{5,7},{6,4},{7,5},{8,10},{9,11},{10,... | collective-permute-start | bytes 393224 | tf_op jit(solution)/shard_map/ppermute | solution.py:440
  78.3 8.9 %collective-permute-start.25 = (f32[2,64,128]{2,1,0:T(8,128)S(1)}, f32[2,64,128]{2,1,0:T(8,128)S(1)}, u32[]{:S(2)}, u32[]{:S(2)}) collective-permute-start(f32[2,64,128]{2,1,0:T(8,128)S(1)} %slice.89), channel_id=1, source_target_pairs={{0,8},{1,9},{2,10},{3,11},{4,12},{5,13},{6,14},{7,15},{8,0},{9,1},... | collective-permute-start | bytes 196616 | tf_op jit(solution)/shard_map/ppermute | solution.py:454
  82.1 5.2 %collective-permute-start.27 = (bf16[64,512]{1,0:T(8,128)(2,1)S(1)}, bf16[64,512]{1,0:T(8,128)(2,1)S(1)}, u32[]{:S(2)}, u32[]{:S(2)}) collective-permute-start(bf16[64,512]{1,0:T(8,128)(2,1)S(1)} %pad_maximum_fusion.2), channel_id=1, source_target_pairs={{0,2},{1,3},{2,0},{3,1},{4,6},{5,7},{6,4},{7,5},{8,10},{9,11},{10,... | collective-permute-start | bytes 196616 | tf_op jit(solution)/shard_map/ppermute | solution.py:440
  87.3 6.5 %collective-permute-start.28 = (bf16[64,512]{1,0:T(8,128)(2,1)S(1)}, bf16[64,512]{1,0:T(8,128)(2,1)S(1)}, u32[]{:S(2)}, u32[]{:S(2)}) collective-permute-start(bf16[64,512]{1,0:T(8,128)(2,1)S(1)} %pad_maximum_fusion.3), channel_id=1, source_target_pairs={{0,1},{1,0},{2,3},{3,2},{4,5},{5,4},{6,7},{7,6},{8,9},{9,8},{10,11... | collective-permute-start | bytes 196616 | tf_op jit(solution)/shard_map/ppermute | solution.py:440
  87.6 5.2 %collective-permute-start.29 = (f32[64,128]{1,0:T(8,128)S(1)}, f32[64,128]{1,0:T(8,128)S(1)}, u32[]{:S(2)}, u32[]{:S(2)}) collective-permute-start(f32[64,128]{1,0:T(8,128)S(1)} %get-tuple-element.182), channel_id=1, source_target_pairs={{0,4},{1,5},{2,6},{3,7},{4,0},{5,1},{6,2},{7,3},{8,12},{9,13},{10,... | collective-permute-start | bytes 98312 | tf_op jit(solution)/shard_map/ppermute | solution.py:454

commit v4 on v3

--- a/solution.py
+++ b/solution.py
@@ -566,10 +566,7 @@
         (features, outer, inner, *smalls),
         [pltpu.VMEM(rim, f32), pltpu.VMEM((cells, chans), f32)],
     )
-    first = [held[-1] for held in weights]
-    normal, cots, first = lax.optimization_barrier((normal, cots, first))
-    for held, value in zip(weights, first):
-        held[-1] = value
+    normal, cots = lax.optimization_barrier((normal, cots))
     normals = {0: normal}
     spread(normals, bits[1:])
     normals, weights = lax.optimization_barrier((normals, weights))
@@ -604,9 +601,10 @@
     kept, sent = far(*sums)
     dnorms = [kept, swap(sent, bits[-1])]
     terms = [turn(send, i % (layers - 1) + 1) for i, send in enumerate(sends)]
-    mixed, across = far(*near(even, odd))
+    sums = near(even, odd)
+    dnorms, sums = lax.optimization_barrier((dnorms, sums))
+    mixed, across = far(*sums)
     across = swap(across, bits[-1])
-    dnorms, terms[0] = lax.optimization_barrier((dnorms, terms[0]))
 
     dconv, norms = call(
         norm_back_kernel,
@@ -619,12 +617,13 @@
         (dconv, features, outer, inner, cotangent, norms, upb),
         [pltpu.VMEM(rim, f32), pltpu.VMEM((rows, chans), f32)],
     )
-    total, dconv, across, terms[2:] = lax.optimization_barrier(
-        (total, dconv, across, terms[2:])
+    for bit in bits[:-1]:
+        total = total + swap(total, bit)
+    total, dconv, across, terms[0], terms[2:] = lax.optimization_barrier(
+        (total, dconv, across, terms[0], terms[2:])
     )
     outer_back, inner_back = halo(dconv)
-    for bit in bits:
-        total = total + swap(total, bit)
+    total = total + swap(total, bits[-1])
     total, terms, inner_back = lax.optimization_barrier((total, terms, inner_back))
     grad_down_weight, *pieces = call(
         functools.partial(up_split_kernel, quads, part),
@@ -650,9 +649,14 @@
         (total, grad_features, block_out, pieces)
     )
     last = cross(total[1], 1)
-    total = total[0]
     for bit in reversed(bits[:-1]):
         pieces, _ = exchange(pieces, bit)
+    (grad_up_weight,) = call(
+        functools.partial(up_join_kernel, quads, layers),
+        [((own, hidden_units), f32)],
+        [pieces[0, i] for i in range(quads)],
+    )
+    total, grad_up_weight = lax.optimization_barrier((total[0], grad_up_weight))
     small_outs = call(
         functools.partial(small_kernel, quads, part),
         [((own, taps), f32)] + [((1, own), f32)] * 4 + [((1, part), f32)],
@@ -663,11 +667,6 @@
         value.reshape(-1) for value in small_outs[1:]
     )
 
-    (grad_up_weight,) = call(
-        functools.partial(up_join_kernel, quads, layers),
-        [((own, hidden_units), f32)],
-        [pieces[0, i] for i in range(quads)],
-    )
     return (
         block_out,
         grad_features,

time: 94.8 us -> 92.2 us (0.973)
  waiting for transfers between devices: 32.1 us -> 28.8 us
    ppermute x6, waiting for transfers between devices: 13.5 us -> 6.37 us  [turn(): return lax.ppermute(value, 'row', pairs)]
    ppermute x18, waiting for transfers between devices: 14.3 us -> 18.9 us  [swap(): return lax.ppermute(value, 'row', [(i, i ^ other) for i in range(devices)])]
    ppermute x18, starting transfers between devices: 19.8 us -> 22.4 us  [swap(): return lax.ppermute(value, 'row', [(i, i ^ other) for i in range(devices)])]
    ppermute x4, starting transfers between devices: 11.4 us -> 9.18 us  [cross(): lax.ppermute(value, 'row', [(i, (i // quads ^ other) * quads + i % quads)...]
  transfers between devices with their start and end apart: 30 -> 30, of which waited for: 16 -> 15; matrix products, arithmetic and copies ran while one was open for 1% -> 1% of each run, Pallas kernels for 14% -> 15%
where the time goes in v4:
time: 92.2 us; the launch traced here: 91.9 us
  starting transfers between devices  40.5 us (44%)
  waiting for transfers between devices  28.8 us (31%)
  Pallas kernels  19.6 us (21%)
  other arithmetic  1.23 us (1%)
  between operations  0.94 us (1%)
    ppermute x18, starting transfers between devices, swap(): return lax.ppermute(value, 'row', [(i, i ^ other) for i in range(devices)])  22.4 us
    pallas_call x11, Pallas kernels, call(): pl.pallas_call(kernel, out_shape=[jax.ShapeDtypeStruct(shape, dtype) for...  19.6 us
    ppermute x18, waiting for transfers between devices, swap(): return lax.ppermute(value, 'row', [(i, i ^ other) for i in range(devices)])  18.9 us
    ppermute x4, starting transfers between devices, cross(): lax.ppermute(value, 'row', [(i, (i // quads ^ other) * quads + i % quads)...  9.18 us
    ppermute x6, starting transfers between devices, turn(): return lax.ppermute(value, 'row', pairs)  7.61 us
    ppermute x6, waiting for transfers between devices, turn(): return lax.ppermute(value, 'row', pairs)  6.37 us
    ppermute x4, waiting for transfers between devices, cross(): lax.ppermute(value, 'row', [(i, (i // quads ^ other) * quads + i % quads)...  3.51 us
  transfers between devices with their start and end apart: 30, of which 15 were waited for; matrix products, arithmetic and copies ran while one was open for 1% of the time, Pallas kernels for 15%

profile of v4, /device:TPU:0, one launch (start us, length us, event | category | flops | bytes accessed | tf_op | source)
XLA Modules:
  0.0 91.9 jit_solution(8222145050893593474)
XLA Ops:
  0.6 1.9 %shard_map.177 = (bf16[128,128]{1,0:T(8,128)(2,1)}, bf16[128,128]{1,0:T(8,128)(2,1)}, bf16[64,128]{1,0:T(8,128)(2,1)}, bf16[320,128]{1,0:T(8,128)(2,1)}) custom-call(bf16[32,49]{1,0:T(8,128)(2,1)} %bitcast.30, bf16[1,32]{1,0:T(2,128)(2,1)} %bitcast.31, bf16[1,32]{1,0:T(2,128)(2,1)} %bitcast.32, bf16[1,32]{1,0:T(2,128)(2,1)} %bitcast.33, ...), custom_call_target="tpu_custom_call" | custom-call | flops 1000 | bytes 1000 | tf_op jit(solution)/shard_map/pallas_call | solution.py:24
  2.5 3.0 %collective-permute-start.2 = (bf16[320,128]{1,0:T(8,128)(2,1)}, bf16[320,128]{1,0:T(8,128)(2,1)S(1)}, u32[]{:S(2)}, u32[]{:S(2)}) collective-permute-start(bf16[320,128]{1,0:T(8,128)(2,1)} %get-tuple-element.99), channel_id=1, source_target_pairs={{0,2},{1,3},{2,0},{3,1},{4,6},{5,7},{6,4},{7,5},{8,10},{9,11},{10,... | collective-permute-start | bytes 245768 | tf_op jit(solution)/shard_map/ppermute | solution.py:440
  5.6 2.7 %collective-permute-done.2 = bf16[320,128]{1,0:T(8,128)(2,1)S(1)} collective-permute-done((bf16[320,128]{1,0:T(8,128)(2,1)}, bf16[320,128]{1,0:T(8,128)(2,1)S(1)}, u32[]{:S(2)}, u32[]{:S(2)}) %collective-permute-start.2) | collective-permute-done | bytes 81952 | tf_op jit(solution)/shard_map/ppermute | solution.py:440
  8.3 0.7 copy-done.4
  9.1 1.3 %collective-permute-done.3 = bf16[320,128]{1,0:T(8,128)(2,1)S(1)} collective-permute-done((bf16[320,128]{1,0:T(8,128)(2,1)S(1)}, bf16[320,128]{1,0:T(8,128)(2,1)S(1)}, u32[]{:S(2)}, u32[]{:S(2)}) %collective-permute-start.3) | collective-permute-done | bytes 81952 | tf_op jit(solution)/shard_map/ppermute | solution.py:440
  10.4 2.1 %collective-permute-start.4 = (bf16[64,128]{1,0:T(8,128)(2,1)S(1)}, bf16[64,128]{1,0:T(8,128)(2,1)S(1)}, u32[]{:S(2)}, u32[]{:S(2)}) collective-permute-start(bf16[64,128]{1,0:T(8,128)(2,1)S(1)} %slice_add_fusion.2), channel_id=1, source_target_pairs={{0,4},{1,5},{2,6},{3,7},{4,0},{5,1},{6,2},{7,3},{8,12},{9,13},{10,... | collective-permute-start | bytes 49160 | tf_op jit(solution)/shard_map/ppermute | solution.py:454
  12.6 0.7 collective-permute-start.6
  13.3 1.0 %collective-permute-done.4 = bf16[64,128]{1,0:T(8,128)(2,1)S(1)} collective-permute-done((bf16[64,128]{1,0:T(8,128)(2,1)S(1)}, bf16[64,128]{1,0:T(8,128)(2,1)S(1)}, u32[]{:S(2)}, u32[]{:S(2)}) %collective-permute-start.4) | collective-permute-done | bytes 16416 | tf_op jit(solution)/shard_map/ppermute | solution.py:454
  14.2 3.0 %collective-permute-start.5 = (bf16[128,128]{1,0:T(8,128)(2,1)S(1)}, bf16[128,128]{1,0:T(8,128)(2,1)S(1)}, u32[]{:S(2)}, u32[]{:S(2)}) collective-permute-start(bf16[128,128]{1,0:T(8,128)(2,1)S(1)} %pad_maximum_fusion.4), channel_id=1, source_target_pairs={{0,8},{1,9},{2,10},{3,11},{4,12},{5,13},{6,14},{7,15},{8,0},{9,1},... | collective-permute-start | bytes 98312 | tf_op jit(solution)/shard_map/ppermute | solution.py:454
  17.3 0.7 collective-permute-start
  17.9 2.9 %collective-permute-start.1 = (bf16[4,64,512]{2,1,0:T(8,128)(2,1)S(1)}, bf16[4,64,512]{2,1,0:T(8,128)(2,1)S(1)}, u32[]{:S(2)}, u32[]{:S(2)}) collective-permute-start(bf16[4,64,512]{2,1,0:T(8,128)(2,1)S(1)} %copy-done.1), channel_id=1, source_target_pairs={{0,1},{1,0},{2,3},{3,2},{4,5},{5,4},{6,7},{7,6},{8,9},{9,8},{10,11... | collective-permute-start | bytes 786440 | tf_op jit(solution)/shard_map/ppermute | solution.py:440
  20.9 1.7 %collective-permute-start.7 = (bf16[256,512]{1,0:T(8,128)(2,1)S(1)}, bf16[256,512]{1,0:T(8,128)(2,1)S(1)}, u32[]{:S(2)}, u32[]{:S(2)}) collective-permute-start(bf16[256,512]{1,0:T(8,128)(2,1)S(1)} %bitcast.20), channel_id=1, source_target_pairs={{0,2},{1,3},{2,0},{3,1},{4,6},{5,7},{6,4},{7,5},{8,10},{9,11},{10,... | collective-permute-start | bytes 786440 | tf_op jit(solution)/shard_map/ppermute | solution.py:440
  22.6 1.3 %collective-permute-done.5 = bf16[128,128]{1,0:T(8,128)(2,1)S(1)} collective-permute-done((bf16[128,128]{1,0:T(8,128)(2,1)S(1)}, bf16[128,128]{1,0:T(8,128)(2,1)S(1)}, u32[]{:S(2)}, u32[]{:S(2)}) %collective-permute-start.5) | collective-permute-done | bytes 32800 | tf_op jit(solution)/shard_map/ppermute | solution.py:454
  23.9 2.4 %collective-permute-start.10 = (bf16[256,512]{1,0:T(8,128)(2,1)S(1)}, bf16[256,512]{1,0:T(8,128)(2,1)S(1)}, u32[]{:S(2)}, u32[]{:S(2)}) collective-permute-start(bf16[256,512]{1,0:T(8,128)(2,1)S(1)} %bitcast.26), channel_id=1, source_target_pairs={{0,12},{1,13},{2,14},{3,15},{4,0},{5,1},{6,2},{7,3},{8,4},{9,5},{1... | collective-permute-start | bytes 786440 | tf_op jit(solution)/shard_map/ppermute | solution.py:446
  26.3 3.7 %shard_map.179 = (bf16[256,512]{1,0:T(8,128)(2,1)S(1)}, f32[256,512]{1,0:T(8,128)S(1)}, f32[256,128]{1,0:T(8,128)S(1)}, f32[64,512]{1,0:T(8,128)S(1)}, f32[8,512]{1,0:T(8,128)S(1)}) custom-call(bf16[4,64,512]{2,1,0:T(8,128)(2,1)S(1)} %copy-done.1, bf16[4,64,512]{2,1,0:T(8,128)(2,1)S(1)} %collective-permute-done.outer, ...), custom_call_target="tpu_custom_call" | custom-call | flops 1000 | bytes 1000 | tf_op jit(solution)/shard_map/pallas_call | solution.py:24
  30.0 1.1 %collective-permute-done.7.refs_6_.refs_2_ = bf16[256,512]{1,0:T(8,128)(2,1)S(1)} collective-permute-done((bf16[256,512]{1,0:T(8,128)(2,1)S(1)}, bf16[256,512]{1,0:T(8,128)(2,1)S(1)}, u32[]{:S(2)}, u32[]{:S(2)}) %collective-permute-start.7) | collective-permute-done | bytes 262176 | tf_op jit(solution)/shard_map/ppermute | solution.py:440
  31.1 3.3 %collective-permute-start.8 = (bf16[256,512]{1,0:T(8,128)(2,1)S(1)}, bf16[256,512]{1,0:T(8,128)(2,1)S(1)}, u32[]{:S(2)}, u32[]{:S(2)}) collective-permute-start(bf16[256,512]{1,0:T(8,128)(2,1)S(1)} %get-tuple-element.122.refs_0_), channel_id=1, source_target_pairs={{0,2},{1,3},{2,0},{3,1},{4,6},{5,7},{6,4},{7,5},{8,10},{9,11},{10,... | collective-permute-start | bytes 786440 | tf_op jit(solution)/shard_map/ppermute | solution.py:440
  34.4 0.3 collective-permute-start.13
  34.9 3.6 %collective-permute-done.9.refs_10_ = bf16[256,512]{1,0:T(8,128)(2,1)S(1)} collective-permute-done((bf16[256,512]{1,0:T(8,128)(2,1)S(1)}, bf16[256,512]{1,0:T(8,128)(2,1)S(1)}, u32[]{:S(2)}, u32[]{:S(2)}) %collective-permute-start.9) | collective-permute-done | bytes 262176 | tf_op jit(solution)/shard_map/ppermute | solution.py:446
  38.5 3.0 %collective-permute-done.8.refs_2_ = bf16[256,512]{1,0:T(8,128)(2,1)S(1)} collective-permute-done((bf16[256,512]{1,0:T(8,128)(2,1)S(1)}, bf16[256,512]{1,0:T(8,128)(2,1)S(1)}, u32[]{:S(2)}, u32[]{:S(2)}) %collective-permute-start.8) | collective-permute-done | bytes 262176 | tf_op jit(solution)/shard_map/ppermute | solution.py:440
  41.5 0.5 collective-permute-start.12
  42.0 1.0 %collective-permute-done.11.refs_1_ = bf16[256,512]{1,0:T(8,128)(2,1)S(1)} collective-permute-done((bf16[256,512]{1,0:T(8,128)(2,1)S(1)}, bf16[256,512]{1,0:T(8,128)(2,1)S(1)}, u32[]{:S(2)}, u32[]{:S(2)}) %collective-permute-start.11) | collective-permute-done | bytes 262176 | tf_op jit(solution)/shard_map/ppermute | solution.py:440
  43.0 0.4 collective-permute-done.12.refs_3_
  43.4 3.3 %shard_map.180 = (f32[512,512]{1,0:T(8,128)S(1)}, f32[512,512]{1,0:T(8,128)S(1)}, bf16[512,512]{1,0:T(8,128)(2,1)S(1)}, bf16[1024,512]{1,0:T(8,128)(2,1)S(1)}, f...) custom-call(f32[8,512]{1,0:T(8,128)S(1)} %get-tuple-element.117.bias_row, ...), custom_call_target="tpu_custom_call" | custom-call | flops 1000 | bytes 1000 | tf_op jit(solution)/shard_map/pallas_call | solution.py:24
  46.9 1.4 %shard_map.181 = (f32[128,512]{1,0:T(8,128)S(1)}, f32[128,512]{1,0:T(8,128)S(1)}, bf16[256,512]{1,0:T(8,128)(2,1)S(1)}, bf16[256,512]{1,0:T(8,128)(2,1)S(1)}, bf...) custom-call(f32[512,512]{1,0:T(8,128)S(1)} %get-tuple-element.132.total_up, ...), custom_call_target="tpu_custom_call" | custom-call | flops 1000 | bytes 1000 | tf_op jit(solution)/shard_map/pallas_call | solution.py:24
  48.3 0.4 collective-permute-start.17
  48.9 1.8 %collective-permute-start.16 = (bf16[256,512]{1,0:T(8,128)(2,1)S(1)}, bf16[256,512]{1,0:T(8,128)(2,1)S(1)}, u32[]{:S(2)}, u32[]{:S(2)}) collective-permute-start(bf16[256,512]{1,0:T(8,128)(2,1)S(1)} %slice.123), channel_id=1, source_target_pairs={{0,2},{1,3},{2,0},{3,1},{4,6},{5,7},{6,4},{7,5},{8,10},{9,11},{10,... | collective-permute-start | bytes 786440 | tf_op jit(solution)/shard_map/ppermute | solution.py:440
  50.8 2.2 %collective-permute-start.20 = (bf16[256,512]{1,0:T(8,128)(2,1)S(1)}, bf16[256,512]{1,0:T(8,128)(2,1)S(1)}, u32[]{:S(2)}, u32[]{:S(2)}) collective-permute-start(bf16[256,512]{1,0:T(8,128)(2,1)S(1)} %get-tuple-element.149), channel_id=1, source_target_pairs={{0,4},{1,5},{2,6},{3,7},{4,8},{5,9},{6,10},{7,11},{8,12},{9,13},{1... | collective-permute-start | bytes 786440 | tf_op jit(solution)/shard_map/ppermute | solution.py:446
  53.0 1.7 %collective-permute-start.21 = (bf16[256,512]{1,0:T(8,128)(2,1)S(1)}, bf16[256,512]{1,0:T(8,128)(2,1)S(1)}, u32[]{:S(2)}, u32[]{:S(2)}) collective-permute-start(bf16[256,512]{1,0:T(8,128)(2,1)S(1)} %get-tuple-element.150), channel_id=1, source_target_pairs={{0,12},{1,13},{2,14},{3,15},{4,0},{5,1},{6,2},{7,3},{8,4},{9,5},{1... | collective-permute-start | bytes 786440 | tf_op jit(solution)/shard_map/ppermute | solution.py:446
  54.7 2.7 %collective-permute-done.16.refs_1_ = bf16[256,512]{1,0:T(8,128)(2,1)S(1)} collective-permute-done((bf16[256,512]{1,0:T(8,128)(2,1)S(1)}, bf16[256,512]{1,0:T(8,128)(2,1)S(1)}, u32[]{:S(2)}, u32[]{:S(2)}) %collective-permute-start.16) | collective-permute-done | bytes 262176 | tf_op jit(solution)/shard_map/ppermute | solution.py:440
  57.6 1.8 %collective-permute-start.19 = (bf16[256,512]{1,0:T(8,128)(2,1)S(1)}, bf16[256,512]{1,0:T(8,128)(2,1)S(1)}, u32[]{:S(2)}, u32[]{:S(2)}) collective-permute-start(bf16[256,512]{1,0:T(8,128)(2,1)S(1)} %slice.122), channel_id=1, source_target_pairs={{0,2},{1,3},{2,0},{3,1},{4,6},{5,7},{6,4},{7,5},{8,10},{9,11},{10,... | collective-permute-start | bytes 786440 | tf_op jit(solution)/shard_map/ppermute | solution.py:440
  59.7 2.8 %shard_map.183 = f32[4,64,128]{2,1,0:T(8,128)S(1)} custom-call(bf16[4,64,512]{2,1,0:T(8,128)(2,1)S(1)} %get-tuple-element.155.dconv, bf16[4,64,512]{2,1,0:T(8,128)(2,1)S(1)} %copy-done.1, bf16[4,64,512]{2,1,0:T(8,128)(2,1)S(1)} %collective-permute-done.outer, bf16[4,64,512]{2,1,0:T(8,128)(2,1)S(1)} %collective-permute-done.1.inner, ...), custom_call_target="tpu_custom_call" | custom-call | flops 1000 | bytes 1000 | tf_op jit(solution)/shard_map/pallas_call | solution.py:24
  62.6 0.7 collective-permute-start.23
  63.3 0.7 collective-permute-done.18
  64.0 2.4 %collective-permute-done.21.refs_4_ = bf16[256,512]{1,0:T(8,128)(2,1)S(1)} collective-permute-done((bf16[256,512]{1,0:T(8,128)(2,1)S(1)}, bf16[256,512]{1,0:T(8,128)(2,1)S(1)}, u32[]{:S(2)}, u32[]{:S(2)}) %collective-permute-start.21) | collective-permute-done | bytes 262176 | tf_op jit(solution)/shard_map/ppermute | solution.py:446
  66.4 0.7 collective-permute-start.26
  67.1 3.4 %collective-permute-start.22 = (f32[4,64,128]{2,1,0:T(8,128)S(1)}, f32[4,64,128]{2,1,0:T(8,128)S(1)}, u32[]{:S(2)}, u32[]{:S(2)}) collective-permute-start(f32[4,64,128]{2,1,0:T(8,128)S(1)} %add.40), channel_id=1, source_target_pairs={{0,2},{1,3},{2,0},{3,1},{4,6},{5,7},{6,4},{7,5},{8,10},{9,11},{10,... | collective-permute-start | bytes 393224 | tf_op jit(solution)/shard_map/ppermute | solution.py:440
  70.6 0.8 add_convert_fusion
  71.4 6.2 %collective-permute-done.22 = f32[4,64,128]{2,1,0:T(8,128)S(1)} collective-permute-done((f32[4,64,128]{2,1,0:T(8,128)S(1)}, f32[4,64,128]{2,1,0:T(8,128)S(1)}, u32[]{:S(2)}, u32[]{:S(2)}) %collective-permute-start.22) | collective-permute-done | bytes 131104 | tf_op jit(solution)/shard_map/ppermute | solution.py:440
  77.6 0.4 collective-permute-done.23.refs_3_
  78.0 1.2 %collective-permute-start.25 = (f32[2,64,128]{2,1,0:T(8,128)S(1)}, f32[2,64,128]{2,1,0:T(8,128)S(1)}, u32[]{:S(2)}, u32[]{:S(2)}) collective-permute-start(f32[2,64,128]{2,1,0:T(8,128)S(1)} %slice.89), channel_id=1, source_target_pairs={{0,8},{1,9},{2,10},{3,11},{4,12},{5,13},{6,14},{7,15},{8,0},{9,1},... | collective-permute-start | bytes 196616 | tf_op jit(solution)/shard_map/ppermute | solution.py:454
  79.2 0.8 shard_map.185
  79.9 2.5 %collective-permute-start.27 = (bf16[64,512]{1,0:T(8,128)(2,1)S(1)}, bf16[64,512]{1,0:T(8,128)(2,1)S(1)}, u32[]{:S(2)}, u32[]{:S(2)}) collective-permute-start(bf16[64,512]{1,0:T(8,128)(2,1)S(1)} %pad_maximum_fusion.2), channel_id=1, source_target_pairs={{0,2},{1,3},{2,0},{3,1},{4,6},{5,7},{6,4},{7,5},{8,10},{9,11},{10,... | collective-permute-start | bytes 196616 | tf_op jit(solution)/shard_map/ppermute | solution.py:440
  82.4 3.7 %shard_map.184 = bf16[4,64,512]{2,1,0:T(8,128)(2,1)} custom-call(bf16[4,64,512]{2,1,0:T(8,128)(2,1)S(1)} %get-tuple-element.155.dconv, bf16[4,64,512]{2,1,0:T(8,128)(2,1)S(1)} %collective-permute-done.26.outer, bf16[4,64,512]{2,1,0:T(8,128)(2,1)S(1)} %collective-permute-done.24.inner, bf16[4,64,512]{2,1,0:T(8,128)(2,1)S(1)} %copy-done, ...), custom_call_target="tpu_custom_call" | custom-call | flops 1000 | bytes 1000 | tf_op jit(solution)/shard_map/pallas_call | solution.py:24
  86.3 2.8 %collective-permute-start.29 = (f32[64,128]{1,0:T(8,128)S(1)}, f32[64,128]{1,0:T(8,128)S(1)}, u32[]{:S(2)}, u32[]{:S(2)}) collective-permute-start(f32[64,128]{1,0:T(8,128)S(1)} %get-tuple-element.188), channel_id=1, source_target_pairs={{0,4},{1,5},{2,6},{3,7},{4,0},{5,1},{6,2},{7,3},{8,12},{9,13},{10,... | collective-permute-start | bytes 98312 | tf_op jit(solution)/shard_map/ppermute | solution.py:454
  89.1 0.8 shard_map.186
  89.8 1.2 %collective-permute-done.29.refs_1_ = f32[64,128]{1,0:T(8,128)S(1)} collective-permute-done((f32[64,128]{1,0:T(8,128)S(1)}, f32[64,128]{1,0:T(8,128)S(1)}, u32[]{:S(2)}, u32[]{:S(2)}) %collective-permute-start.29) | collective-permute-done | bytes 32800 | tf_op jit(solution)/shard_map/ppermute | solution.py:454
  91.1 0.9 shard_map.187
  (60 shorter events, 1.7 us)
Async XLA Ops:
  2.5 5.7 %copy-start.5 = (bf16[64,128]{1,0:T(8,128)(2,1)S(1)}, bf16[64,128]{1,0:T(8,128)(2,1)}, u32[]{:S(2)}) copy-start(bf16[64,128]{1,0:T(8,128)(2,1)} %get-tuple-element.97) | copy-start | bytes 49156
  2.5 5.7 %collective-permute-start.2 = (bf16[320,128]{1,0:T(8,128)(2,1)}, bf16[320,128]{1,0:T(8,128)(2,1)S(1)}, u32[]{:S(2)}, u32[]{:S(2)}) collective-permute-start(bf16[320,128]{1,0:T(8,128)(2,1)} %get-tuple-element.99), channel_id=1, source_target_pairs={{0,2},{1,3},{2,0},{3,1},{4,6},{5,7},{6,4},{7,5},{8,10},{9,11},{10,... | collective-permute-start | bytes 245768 | tf_op jit(solution)/shard_map/ppermute | solution.py:440
  8.2 0.8 copy-start.4
  9.0 3.5 %copy-start.2 = (bf16[128,512]{1,0:T(8,128)(2,1)S(1)}, bf16[128,512]{1,0:T(8,128)(2,1)}, u32[]{:S(2)}) copy-start(bf16[128,512]{1,0:T(8,128)(2,1)} %down) | copy-start | bytes 393220
  9.0 1.3 %collective-permute-start.3 = (bf16[320,128]{1,0:T(8,128)(2,1)S(1)}, bf16[320,128]{1,0:T(8,128)(2,1)S(1)}, u32[]{:S(2)}, u32[]{:S(2)}) collective-permute-start(bf16[320,128]{1,0:T(8,128)(2,1)S(1)} %pad_maximum_fusion), channel_id=1, source_target_pairs={{0,1},{1,0},{2,3},{3,2},{4,5},{5,4},{6,7},{7,6},{8,9},{9,8},{10,11... | collective-permute-start | bytes 245768 | tf_op jit(solution)/shard_map/ppermute | solution.py:440
  10.4 2.2 %copy-start.3 = (bf16[128,128]{1,0:T(8,128)(2,1)S(1)}, bf16[128,128]{1,0:T(8,128)(2,1)}, u32[]{:S(2)}) copy-start(bf16[128,128]{1,0:T(8,128)(2,1)} %get-tuple-element.109.refs_0_) | copy-start | bytes 98308
  10.4 6.9 %copy-start.1 = (bf16[4,64,512]{2,1,0:T(8,128)(2,1)S(1)}, bf16[4,64,512]{2,1,0:T(8,128)(2,1)}, u32[]{:S(2)}) copy-start(bf16[4,64,512]{2,1,0:T(8,128)(2,1)} %features.1) | copy-start | bytes 786436
  10.4 10.5 %copy-start = (bf16[4,64,512]{2,1,0:T(8,128)(2,1)S(1)}, bf16[4,64,512]{2,1,0:T(8,128)(2,1)}, u32[]{:S(2)}) copy-start(bf16[4,64,512]{2,1,0:T(8,128)(2,1)} %cotangent.1) | copy-start | bytes 786436
  10.4 3.8 %collective-permute-start.4 = (bf16[64,128]{1,0:T(8,128)(2,1)S(1)}, bf16[64,128]{1,0:T(8,128)(2,1)S(1)}, u32[]{:S(2)}, u32[]{:S(2)}) collective-permute-start(bf16[64,128]{1,0:T(8,128)(2,1)S(1)} %slice_add_fusion.2), channel_id=1, source_target_pairs={{0,4},{1,5},{2,6},{3,7},{4,0},{5,1},{6,2},{7,3},{8,12},{9,13},{10,... | collective-permute-start | bytes 49160 | tf_op jit(solution)/shard_map/ppermute | solution.py:454
  12.6 11.4 %collective-permute-start.6 = (bf16[256,512]{1,0:T(8,128)(2,1)S(1)}, bf16[256,512]{1,0:T(8,128)(2,1)S(1)}, u32[]{:S(2)}, u32[]{:S(2)}) collective-permute-start(bf16[256,512]{1,0:T(8,128)(2,1)S(1)} %bitcast.24), channel_id=1, source_target_pairs={{0,4},{1,5},{2,6},{3,7},{4,8},{5,9},{6,10},{7,11},{8,12},{9,13},{1... | collective-permute-start | bytes 786440 | tf_op jit(solution)/shard_map/ppermute | solution.py:446
  14.2 9.7 %collective-permute-start.5 = (bf16[128,128]{1,0:T(8,128)(2,1)S(1)}, bf16[128,128]{1,0:T(8,128)(2,1)S(1)}, u32[]{:S(2)}, u32[]{:S(2)}) collective-permute-start(bf16[128,128]{1,0:T(8,128)(2,1)S(1)} %pad_maximum_fusion.4), channel_id=1, source_target_pairs={{0,8},{1,9},{2,10},{3,11},{4,12},{5,13},{6,14},{7,15},{8,0},{9,1},... | collective-permute-start | bytes 98312 | tf_op jit(solution)/shard_map/ppermute | solution.py:454
  17.3 9.0 %collective-permute-start = (bf16[4,64,512]{2,1,0:T(8,128)(2,1)S(1)}, bf16[4,64,512]{2,1,0:T(8,128)(2,1)S(1)}, u32[]{:S(2)}, u32[]{:S(2)}) collective-permute-start(bf16[4,64,512]{2,1,0:T(8,128)(2,1)S(1)} %copy-done.1), channel_id=1, source_target_pairs={{1,2},{3,4},{5,6},{7,8},{9,10},{11,12},{13,14},{2,1},{4,3},{6,5},{... | collective-permute-start | bytes 786440 | tf_op jit(solution)/shard_map/ppermute | solution.py:451
  17.9 8.4 %collective-permute-start.1 = (bf16[4,64,512]{2,1,0:T(8,128)(2,1)S(1)}, bf16[4,64,512]{2,1,0:T(8,128)(2,1)S(1)}, u32[]{:S(2)}, u32[]{:S(2)}) collective-permute-start(bf16[4,64,512]{2,1,0:T(8,128)(2,1)S(1)} %copy-done.1), channel_id=1, source_target_pairs={{0,1},{1,0},{2,3},{3,2},{4,5},{5,4},{6,7},{7,6},{8,9},{9,8},{10,11... | collective-permute-start | bytes 786440 | tf_op jit(solution)/shard_map/ppermute | solution.py:440
  20.9 10.2 %collective-permute-start.7 = (bf16[256,512]{1,0:T(8,128)(2,1)S(1)}, bf16[256,512]{1,0:T(8,128)(2,1)S(1)}, u32[]{:S(2)}, u32[]{:S(2)}) collective-permute-start(bf16[256,512]{1,0:T(8,128)(2,1)S(1)} %bitcast.20), channel_id=1, source_target_pairs={{0,2},{1,3},{2,0},{3,1},{4,6},{5,7},{6,4},{7,5},{8,10},{9,11},{10,... | collective-permute-start | bytes 786440 | tf_op jit(solution)/shard_map/ppermute | solution.py:440
  23.9 14.6 %collective-permute-start.9 = (bf16[256,512]{1,0:T(8,128)(2,1)S(1)}, bf16[256,512]{1,0:T(8,128)(2,1)S(1)}, u32[]{:S(2)}, u32[]{:S(2)}) collective-permute-start(bf16[256,512]{1,0:T(8,128)(2,1)S(1)} %bitcast.25), channel_id=1, source_target_pairs={{0,8},{1,9},{2,10},{3,11},{4,12},{5,13},{6,14},{7,15},{8,0},{9,1},... | collective-permute-start | bytes 786440 | tf_op jit(solution)/shard_map/ppermute | solution.py:446
  23.9 14.6 %collective-permute-start.10 = (bf16[256,512]{1,0:T(8,128)(2,1)S(1)}, bf16[256,512]{1,0:T(8,128)(2,1)S(1)}, u32[]{:S(2)}, u32[]{:S(2)}) collective-permute-start(bf16[256,512]{1,0:T(8,128)(2,1)S(1)} %bitcast.26), channel_id=1, source_target_pairs={{0,12},{1,13},{2,14},{3,15},{4,0},{5,1},{6,2},{7,3},{8,4},{9,5},{1... | collective-permute-start | bytes 786440 | tf_op jit(solution)/shard_map/ppermute | solution.py:446
  31.1 10.4 %collective-permute-start.8 = (bf16[256,512]{1,0:T(8,128)(2,1)S(1)}, bf16[256,512]{1,0:T(8,128)(2,1)S(1)}, u32[]{:S(2)}, u32[]{:S(2)}) collective-permute-start(bf16[256,512]{1,0:T(8,128)(2,1)S(1)} %get-tuple-element.122.refs_0_), channel_id=1, source_target_pairs={{0,2},{1,3},{2,0},{3,1},{4,6},{5,7},{6,4},{7,5},{8,10},{9,11},{10,... | collective-permute-start | bytes 786440 | tf_op jit(solution)/shard_map/ppermute | solution.py:440
  34.4 7.6 %collective-permute-start.13 = (bf16[256,512]{1,0:T(8,128)(2,1)S(1)}, bf16[256,512]{1,0:T(8,128)(2,1)S(1)}, u32[]{:S(2)}, u32[]{:S(2)}) collective-permute-start(bf16[256,512]{1,0:T(8,128)(2,1)S(1)} %bitcast.21), channel_id=1, source_target_pairs={{0,1},{1,0},{2,3},{3,2},{4,5},{5,4},{6,7},{7,6},{8,9},{9,8},{10,11... | collective-permute-start | bytes 786440 | tf_op jit(solution)/shard_map/ppermute | solution.py:440
  34.7 7.3 %collective-permute-start.14 = (bf16[256,512]{1,0:T(8,128)(2,1)S(1)}, bf16[256,512]{1,0:T(8,128)(2,1)S(1)}, u32[]{:S(2)}, u32[]{:S(2)}) collective-permute-start(bf16[256,512]{1,0:T(8,128)(2,1)S(1)} %collective-permute-done.7.refs_6_.refs_2_), channel_id=1, source_target_pairs={{0,1},{1,0},{2,3},{3,2},{4,5},{5,4},{6,7},{7,6},{8,9},{9,8},{10,11... | collective-permute-start | bytes 786440 | tf_op jit(solution)/shard_map/ppermute | solution.py:440
  41.5 1.5 %collective-permute-start.11 = (bf16[256,512]{1,0:T(8,128)(2,1)S(1)}, bf16[256,512]{1,0:T(8,128)(2,1)S(1)}, u32[]{:S(2)}, u32[]{:S(2)}) collective-permute-start(bf16[256,512]{1,0:T(8,128)(2,1)S(1)} %get-tuple-element.122.refs_0_), channel_id=1, source_target_pairs={{0,1},{1,0},{2,3},{3,2},{4,5},{5,4},{6,7},{7,6},{8,9},{9,8},{10,11... | collective-permute-start | bytes 786440 | tf_op jit(solution)/shard_map/ppermute | solution.py:440
  41.5 1.9 %collective-permute-start.12 = (bf16[256,512]{1,0:T(8,128)(2,1)S(1)}, bf16[256,512]{1,0:T(8,128)(2,1)S(1)}, u32[]{:S(2)}, u32[]{:S(2)}) collective-permute-start(bf16[256,512]{1,0:T(8,128)(2,1)S(1)} %collective-permute-done.8.refs_2_), channel_id=1, source_target_pairs={{0,1},{1,0},{2,3},{3,2},{4,5},{5,4},{6,7},{7,6},{8,9},{9,8},{10,11... | collective-permute-start | bytes 786440 | tf_op jit(solution)/shard_map/ppermute | solution.py:440
  46.7 2.1 %collective-permute-start.15 = (bf16[512,512]{1,0:T(8,128)(2,1)S(1)}, bf16[512,512]{1,0:T(8,128)(2,1)S(1)}, u32[]{:S(2)}, u32[]{:S(2)}) collective-permute-start(bf16[512,512]{1,0:T(8,128)(2,1)S(1)} %get-tuple-element.131), channel_id=1, source_target_pairs={{0,1},{1,0},{2,3},{3,2},{4,5},{5,4},{6,7},{7,6},{8,9},{9,8},{10,11... | collective-permute-start | bytes 1572872 | tf_op jit(solution)/shard_map/ppermute | solution.py:440
  48.3 6.4 %collective-permute-start.17 = (bf16[512,512]{1,0:T(8,128)(2,1)S(1)}, bf16[512,512]{1,0:T(8,128)(2,1)S(1)}, u32[]{:S(2)}, u32[]{:S(2)}) collective-permute-start(bf16[512,512]{1,0:T(8,128)(2,1)S(1)} %get-tuple-element.141), channel_id=1, source_target_pairs={{0,1},{1,0},{2,3},{3,2},{4,5},{5,4},{6,7},{7,6},{8,9},{9,8},{10,11... | collective-permute-start | bytes 1572872 | tf_op jit(solution)/shard_map/ppermute | solution.py:440
  48.9 8.4 %collective-permute-start.16 = (bf16[256,512]{1,0:T(8,128)(2,1)S(1)}, bf16[256,512]{1,0:T(8,128)(2,1)S(1)}, u32[]{:S(2)}, u32[]{:S(2)}) collective-permute-start(bf16[256,512]{1,0:T(8,128)(2,1)S(1)} %slice.123), channel_id=1, source_target_pairs={{0,2},{1,3},{2,0},{3,1},{4,6},{5,7},{6,4},{7,5},{8,10},{9,11},{10,... | collective-permute-start | bytes 786440 | tf_op jit(solution)/shard_map/ppermute | solution.py:440
  50.8 13.2 %collective-permute-start.20 = (bf16[256,512]{1,0:T(8,128)(2,1)S(1)}, bf16[256,512]{1,0:T(8,128)(2,1)S(1)}, u32[]{:S(2)}, u32[]{:S(2)}) collective-permute-start(bf16[256,512]{1,0:T(8,128)(2,1)S(1)} %get-tuple-element.149), channel_id=1, source_target_pairs={{0,4},{1,5},{2,6},{3,7},{4,8},{5,9},{6,10},{7,11},{8,12},{9,13},{1... | collective-permute-start | bytes 786440 | tf_op jit(solution)/shard_map/ppermute | solution.py:446
  53.0 13.4 %collective-permute-start.21 = (bf16[256,512]{1,0:T(8,128)(2,1)S(1)}, bf16[256,512]{1,0:T(8,128)(2,1)S(1)}, u32[]{:S(2)}, u32[]{:S(2)}) collective-permute-start(bf16[256,512]{1,0:T(8,128)(2,1)S(1)} %get-tuple-element.150), channel_id=1, source_target_pairs={{0,12},{1,13},{2,14},{3,15},{4,0},{5,1},{6,2},{7,3},{8,4},{9,5},{1... | collective-permute-start | bytes 786440 | tf_op jit(solution)/shard_map/ppermute | solution.py:446
  57.6 8.8 %collective-permute-start.19 = (bf16[256,512]{1,0:T(8,128)(2,1)S(1)}, bf16[256,512]{1,0:T(8,128)(2,1)S(1)}, u32[]{:S(2)}, u32[]{:S(2)}) collective-permute-start(bf16[256,512]{1,0:T(8,128)(2,1)S(1)} %slice.122), channel_id=1, source_target_pairs={{0,2},{1,3},{2,0},{3,1},{4,6},{5,7},{6,4},{7,5},{8,10},{9,11},{10,... | collective-permute-start | bytes 786440 | tf_op jit(solution)/shard_map/ppermute | solution.py:440
  62.5 1.4 %collective-permute-start.18 = (f32[4,64,128]{2,1,0:T(8,128)S(1)}, f32[4,64,128]{2,1,0:T(8,128)S(1)}, u32[]{:S(2)}, u32[]{:S(2)}) collective-permute-start(f32[4,64,128]{2,1,0:T(8,128)S(1)} %shard_map.183), channel_id=1, source_target_pairs={{0,1},{1,0},{2,3},{3,2},{4,5},{5,4},{6,7},{7,6},{8,9},{9,8},{10,11... | collective-permute-start | bytes 393224 | tf_op jit(solution)/shard_map/ppermute | solution.py:440
  62.6 15.3 %collective-permute-start.23 = (bf16[256,512]{1,0:T(8,128)(2,1)S(1)}, bf16[256,512]{1,0:T(8,128)(2,1)S(1)}, u32[]{:S(2)}, u32[]{:S(2)}) collective-permute-start(bf16[256,512]{1,0:T(8,128)(2,1)S(1)} %get-tuple-element.153), channel_id=1, source_target_pairs={{0,8},{1,9},{2,10},{3,11},{4,12},{5,13},{6,14},{7,15},{8,0},{9,1},... | collective-permute-start | bytes 786440 | tf_op jit(solution)/shard_map/ppermute | solution.py:446
  66.4 11.6 %collective-permute-start.24 = (bf16[4,64,512]{2,1,0:T(8,128)(2,1)S(1)}, bf16[4,64,512]{2,1,0:T(8,128)(2,1)S(1)}, u32[]{:S(2)}, u32[]{:S(2)}) collective-permute-start(bf16[4,64,512]{2,1,0:T(8,128)(2,1)S(1)} %get-tuple-element.155.dconv), channel_id=1, source_target_pairs={{0,1},{1,0},{2,3},{3,2},{4,5},{5,4},{6,7},{7,6},{8,9},{9,8},{10,11... | collective-permute-start | bytes 786440 | tf_op jit(solution)/shard_map/ppermute | solution.py:440
  66.4 16.0 %collective-permute-start.26 = (bf16[4,64,512]{2,1,0:T(8,128)(2,1)S(1)}, bf16[4,64,512]{2,1,0:T(8,128)(2,1)S(1)}, u32[]{:S(2)}, u32[]{:S(2)}) collective-permute-start(bf16[4,64,512]{2,1,0:T(8,128)(2,1)S(1)} %get-tuple-element.155.dconv), channel_id=1, source_target_pairs={{1,2},{3,4},{5,6},{7,8},{9,10},{11,12},{13,14},{2,1},{4,3},{6,5},{... | collective-permute-start | bytes 786440 | tf_op jit(solution)/shard_map/ppermute | solution.py:451
  67.1 10.5 %collective-permute-start.22 = (f32[4,64,128]{2,1,0:T(8,128)S(1)}, f32[4,64,128]{2,1,0:T(8,128)S(1)}, u32[]{:S(2)}, u32[]{:S(2)}) collective-permute-start(f32[4,64,128]{2,1,0:T(8,128)S(1)} %add.40), channel_id=1, source_target_pairs={{0,2},{1,3},{2,0},{3,1},{4,6},{5,7},{6,4},{7,5},{8,10},{9,11},{10,... | collective-permute-start | bytes 393224 | tf_op jit(solution)/shard_map/ppermute | solution.py:440
  78.0 8.1 %collective-permute-start.25 = (f32[2,64,128]{2,1,0:T(8,128)S(1)}, f32[2,64,128]{2,1,0:T(8,128)S(1)}, u32[]{:S(2)}, u32[]{:S(2)}) collective-permute-start(f32[2,64,128]{2,1,0:T(8,128)S(1)} %slice.89), channel_id=1, source_target_pairs={{0,8},{1,9},{2,10},{3,11},{4,12},{5,13},{6,14},{7,15},{8,0},{9,1},... | collective-permute-start | bytes 196616 | tf_op jit(solution)/shard_map/ppermute | solution.py:454
  79.9 6.2 %collective-permute-start.27 = (bf16[64,512]{1,0:T(8,128)(2,1)S(1)}, bf16[64,512]{1,0:T(8,128)(2,1)S(1)}, u32[]{:S(2)}, u32[]{:S(2)}) collective-permute-start(bf16[64,512]{1,0:T(8,128)(2,1)S(1)} %pad_maximum_fusion.2), channel_id=1, source_target_pairs={{0,2},{1,3},{2,0},{3,1},{4,6},{5,7},{6,4},{7,5},{8,10},{9,11},{10,... | collective-permute-start | bytes 196616 | tf_op jit(solution)/shard_map/ppermute | solution.py:440
  86.2 2.9 %collective-permute-start.28 = (bf16[64,512]{1,0:T(8,128)(2,1)S(1)}, bf16[64,512]{1,0:T(8,128)(2,1)S(1)}, u32[]{:S(2)}, u32[]{:S(2)}) collective-permute-start(bf16[64,512]{1,0:T(8,128)(2,1)S(1)} %pad_maximum_fusion.3), channel_id=1, source_target_pairs={{0,1},{1,0},{2,3},{3,2},{4,5},{5,4},{6,7},{7,6},{8,9},{9,8},{10,11... | collective-permute-start | bytes 196616 | tf_op jit(solution)/shard_map/ppermute | solution.py:440
  86.3 4.8 %collective-permute-start.29 = (f32[64,128]{1,0:T(8,128)S(1)}, f32[64,128]{1,0:T(8,128)S(1)}, u32[]{:S(2)}, u32[]{:S(2)}) collective-permute-start(f32[64,128]{1,0:T(8,128)S(1)} %get-tuple-element.188), channel_id=1, source_target_pairs={{0,4},{1,5},{2,6},{3,7},{4,0},{5,1},{6,2},{7,3},{8,12},{9,13},{10,... | collective-permute-start | bytes 98312 | tf_op jit(solution)/shard_map/ppermute | solution.py:454

commit v5 on v4

--- a/solution.py
+++ b/solution.py
@@ -167,7 +167,7 @@
             )
         return carry
 
-    lax.fori_loop(0, chans // lanes, chunk, 0)
+    lax.fori_loop(0, chans // lanes, chunk, 0, unroll=True)
 
     def norm(i, carry):
         at = pl.ds(pl.multiple_of(i * width, width), width)
@@ -184,7 +184,7 @@
         ).astype(bf16)
         return carry
 
-    lax.fori_loop(0, height, norm, 0)
+    lax.fori_loop(0, height, norm, 0, unroll=True)
 
 
 def back_kernel(dconv, outer, inner, cotangent, params, out, padded):
@@ -198,7 +198,7 @@
             out[row, :, at] = (cotangent[row, :, at].astype(f32) + sums[row]).astype(bf16)
         return carry
 
-    lax.fori_loop(0, chans // lanes, chunk, 0)
+    lax.fori_loop(0, chans // lanes, chunk, 0, unroll=True)
 
 
 def taps_kernel(
@@ -241,7 +241,7 @@
         grads[row_shift : row_shift + 1, at] = norms[1:2, at] * scale
         return carry
 
-    lax.fori_loop(0, chans // lanes, chunk, 0)
+    lax.fori_loop(0, chans // lanes, chunk, 0, unroll=True)
     part = upb.shape[1] // layers
     for z in range(layers):
         bias = upb[0:1, z * part : (z + 1) * part] * scale

time: 92.2 us -> 90.6 us (0.983)
  Pallas kernels: 19.6 us -> 18.6 us
    pallas_call x11, Pallas kernels: 19.6 us -> 18.6 us  [call(): pl.pallas_call(kernel, out_shape=[jax.ShapeDtypeStruct(shape, dtype) for...]
    ppermute x4, starting transfers between devices: 9.18 us -> 8.26 us  [cross(): lax.ppermute(value, 'row', [(i, (i // quads ^ other) * quads + i % quads)...]
  transfers between devices with their start and end apart: 30 -> 30, of which waited for: 15 -> 15; matrix products, arithmetic and copies ran while one was open for 1% -> 1% of each run, Pallas kernels for 15% -> 14%
where the time goes in v5:
time: 90.6 us; the launch traced here: 90.3 us
  starting transfers between devices  40 us (44%)
  waiting for transfers between devices  28.7 us (32%)
  Pallas kernels  18.6 us (21%)
  other arithmetic  1.23 us (1%)
  between operations  0.94 us (1%)
    ppermute x18, starting transfers between devices, swap(): return lax.ppermute(value, 'row', [(i, i ^ other) for i in range(devices)])  22.7 us
    ppermute x18, waiting for transfers between devices, swap(): return lax.ppermute(value, 'row', [(i, i ^ other) for i in range(devices)])  18.7 us
    pallas_call x11, Pallas kernels, call(): pl.pallas_call(kernel, out_shape=[jax.ShapeDtypeStruct(shape, dtype) for...  18.6 us
    ppermute x4, starting transfers between devices, cross(): lax.ppermute(value, 'row', [(i, (i // quads ^ other) * quads + i % quads)...  8.26 us
    ppermute x6, starting transfers between devices, turn(): return lax.ppermute(value, 'row', pairs)  7.69 us
    ppermute x6, waiting for transfers between devices, turn(): return lax.ppermute(value, 'row', pairs)  6.53 us
    ppermute x4, waiting for transfers between devices, cross(): lax.ppermute(value, 'row', [(i, (i // quads ^ other) * quads + i % quads)...  3.51 us
  transfers between devices with their start and end apart: 30, of which 15 were waited for; matrix products, arithmetic and copies ran while one was open for 1% of the time, Pallas kernels for 14%

profile of v5, /device:TPU:0, one launch (start us, length us, event | category | flops | bytes accessed | tf_op | source)
XLA Modules:
  0.0 90.3 jit_solution(6830034473733712096)
XLA Ops:
  0.6 1.9 %shard_map.177 = (bf16[128,128]{1,0:T(8,128)(2,1)}, bf16[128,128]{1,0:T(8,128)(2,1)}, bf16[64,128]{1,0:T(8,128)(2,1)}, bf16[320,128]{1,0:T(8,128)(2,1)}) custom-call(bf16[32,49]{1,0:T(8,128)(2,1)} %bitcast.30, bf16[1,32]{1,0:T(2,128)(2,1)} %bitcast.31, bf16[1,32]{1,0:T(2,128)(2,1)} %bitcast.32, bf16[1,32]{1,0:T(2,128)(2,1)} %bitcast.33, ...), custom_call_target="tpu_custom_call" | custom-call | flops 1000 | bytes 1000 | tf_op jit(solution)/shard_map/pallas_call | solution.py:24
  2.5 3.0 %collective-permute-start.2 = (bf16[320,128]{1,0:T(8,128)(2,1)}, bf16[320,128]{1,0:T(8,128)(2,1)S(1)}, u32[]{:S(2)}, u32[]{:S(2)}) collective-permute-start(bf16[320,128]{1,0:T(8,128)(2,1)} %get-tuple-element.99), channel_id=1, source_target_pairs={{0,2},{1,3},{2,0},{3,1},{4,6},{5,7},{6,4},{7,5},{8,10},{9,11},{10,... | collective-permute-start | bytes 245768 | tf_op jit(solution)/shard_map/ppermute | solution.py:440
  5.6 2.7 %collective-permute-done.2 = bf16[320,128]{1,0:T(8,128)(2,1)S(1)} collective-permute-done((bf16[320,128]{1,0:T(8,128)(2,1)}, bf16[320,128]{1,0:T(8,128)(2,1)S(1)}, u32[]{:S(2)}, u32[]{:S(2)}) %collective-permute-start.2) | collective-permute-done | bytes 81952 | tf_op jit(solution)/shard_map/ppermute | solution.py:440
  8.3 0.7 copy-done.4
  9.1 1.3 %collective-permute-done.3 = bf16[320,128]{1,0:T(8,128)(2,1)S(1)} collective-permute-done((bf16[320,128]{1,0:T(8,128)(2,1)S(1)}, bf16[320,128]{1,0:T(8,128)(2,1)S(1)}, u32[]{:S(2)}, u32[]{:S(2)}) %collective-permute-start.3) | collective-permute-done | bytes 81952 | tf_op jit(solution)/shard_map/ppermute | solution.py:440
  10.4 2.1 %collective-permute-start.4 = (bf16[64,128]{1,0:T(8,128)(2,1)S(1)}, bf16[64,128]{1,0:T(8,128)(2,1)S(1)}, u32[]{:S(2)}, u32[]{:S(2)}) collective-permute-start(bf16[64,128]{1,0:T(8,128)(2,1)S(1)} %slice_add_fusion.2), channel_id=1, source_target_pairs={{0,4},{1,5},{2,6},{3,7},{4,0},{5,1},{6,2},{7,3},{8,12},{9,13},{10,... | collective-permute-start | bytes 49160 | tf_op jit(solution)/shard_map/ppermute | solution.py:454
  12.6 0.7 collective-permute-start.6
  13.3 1.0 %collective-permute-done.4 = bf16[64,128]{1,0:T(8,128)(2,1)S(1)} collective-permute-done((bf16[64,128]{1,0:T(8,128)(2,1)S(1)}, bf16[64,128]{1,0:T(8,128)(2,1)S(1)}, u32[]{:S(2)}, u32[]{:S(2)}) %collective-permute-start.4) | collective-permute-done | bytes 16416 | tf_op jit(solution)/shard_map/ppermute | solution.py:454
  14.2 3.0 %collective-permute-start.5 = (bf16[128,128]{1,0:T(8,128)(2,1)S(1)}, bf16[128,128]{1,0:T(8,128)(2,1)S(1)}, u32[]{:S(2)}, u32[]{:S(2)}) collective-permute-start(bf16[128,128]{1,0:T(8,128)(2,1)S(1)} %pad_maximum_fusion.4), channel_id=1, source_target_pairs={{0,8},{1,9},{2,10},{3,11},{4,12},{5,13},{6,14},{7,15},{8,0},{9,1},... | collective-permute-start | bytes 98312 | tf_op jit(solution)/shard_map/ppermute | solution.py:454
  17.3 0.7 collective-permute-start
  17.9 2.9 %collective-permute-start.1 = (bf16[4,64,512]{2,1,0:T(8,128)(2,1)S(1)}, bf16[4,64,512]{2,1,0:T(8,128)(2,1)S(1)}, u32[]{:S(2)}, u32[]{:S(2)}) collective-permute-start(bf16[4,64,512]{2,1,0:T(8,128)(2,1)S(1)} %copy-done.1), channel_id=1, source_target_pairs={{0,1},{1,0},{2,3},{3,2},{4,5},{5,4},{6,7},{7,6},{8,9},{9,8},{10,11... | collective-permute-start | bytes 786440 | tf_op jit(solution)/shard_map/ppermute | solution.py:440
  20.9 1.7 %collective-permute-start.7 = (bf16[256,512]{1,0:T(8,128)(2,1)S(1)}, bf16[256,512]{1,0:T(8,128)(2,1)S(1)}, u32[]{:S(2)}, u32[]{:S(2)}) collective-permute-start(bf16[256,512]{1,0:T(8,128)(2,1)S(1)} %bitcast.20), channel_id=1, source_target_pairs={{0,2},{1,3},{2,0},{3,1},{4,6},{5,7},{6,4},{7,5},{8,10},{9,11},{10,... | collective-permute-start | bytes 786440 | tf_op jit(solution)/shard_map/ppermute | solution.py:440
  22.6 1.3 %collective-permute-done.5 = bf16[128,128]{1,0:T(8,128)(2,1)S(1)} collective-permute-done((bf16[128,128]{1,0:T(8,128)(2,1)S(1)}, bf16[128,128]{1,0:T(8,128)(2,1)S(1)}, u32[]{:S(2)}, u32[]{:S(2)}) %collective-permute-start.5) | collective-permute-done | bytes 32800 | tf_op jit(solution)/shard_map/ppermute | solution.py:454
  23.9 2.4 %collective-permute-start.10 = (bf16[256,512]{1,0:T(8,128)(2,1)S(1)}, bf16[256,512]{1,0:T(8,128)(2,1)S(1)}, u32[]{:S(2)}, u32[]{:S(2)}) collective-permute-start(bf16[256,512]{1,0:T(8,128)(2,1)S(1)} %bitcast.26), channel_id=1, source_target_pairs={{0,12},{1,13},{2,14},{3,15},{4,0},{5,1},{6,2},{7,3},{8,4},{9,5},{1... | collective-permute-start | bytes 786440 | tf_op jit(solution)/shard_map/ppermute | solution.py:446
  26.3 3.4 %shard_map.179 = (bf16[256,512]{1,0:T(8,128)(2,1)S(1)}, f32[256,512]{1,0:T(8,128)S(1)}, f32[256,128]{1,0:T(8,128)S(1)}, f32[64,512]{1,0:T(8,128)S(1)}, f32[8,512]{1,0:T(8,128)S(1)}) custom-call(bf16[4,64,512]{2,1,0:T(8,128)(2,1)S(1)} %copy-done.1, bf16[4,64,512]{2,1,0:T(8,128)(2,1)S(1)} %collective-permute-done.outer, ...), custom_call_target="tpu_custom_call" | custom-call | flops 1000 | bytes 1000 | tf_op jit(solution)/shard_map/pallas_call | solution.py:24
  29.7 1.4 %collective-permute-done.7.refs_6_.refs_2_ = bf16[256,512]{1,0:T(8,128)(2,1)S(1)} collective-permute-done((bf16[256,512]{1,0:T(8,128)(2,1)S(1)}, bf16[256,512]{1,0:T(8,128)(2,1)S(1)}, u32[]{:S(2)}, u32[]{:S(2)}) %collective-permute-start.7) | collective-permute-done | bytes 262176 | tf_op jit(solution)/shard_map/ppermute | solution.py:440
  31.1 2.9 %collective-permute-start.8 = (bf16[256,512]{1,0:T(8,128)(2,1)S(1)}, bf16[256,512]{1,0:T(8,128)(2,1)S(1)}, u32[]{:S(2)}, u32[]{:S(2)}) collective-permute-start(bf16[256,512]{1,0:T(8,128)(2,1)S(1)} %get-tuple-element.122.refs_0_), channel_id=1, source_target_pairs={{0,2},{1,3},{2,0},{3,1},{4,6},{5,7},{6,4},{7,5},{8,10},{9,11},{10,... | collective-permute-start | bytes 786440 | tf_op jit(solution)/shard_map/ppermute | solution.py:440
  34.0 0.7 collective-permute-start.13
  34.7 3.7 %collective-permute-done.9.refs_10_ = bf16[256,512]{1,0:T(8,128)(2,1)S(1)} collective-permute-done((bf16[256,512]{1,0:T(8,128)(2,1)S(1)}, bf16[256,512]{1,0:T(8,128)(2,1)S(1)}, u32[]{:S(2)}, u32[]{:S(2)}) %collective-permute-start.9) | collective-permute-done | bytes 262176 | tf_op jit(solution)/shard_map/ppermute | solution.py:446
  38.5 2.4 %collective-permute-done.8.refs_2_ = bf16[256,512]{1,0:T(8,128)(2,1)S(1)} collective-permute-done((bf16[256,512]{1,0:T(8,128)(2,1)S(1)}, bf16[256,512]{1,0:T(8,128)(2,1)S(1)}, u32[]{:S(2)}, u32[]{:S(2)}) %collective-permute-start.8) | collective-permute-done | bytes 262176 | tf_op jit(solution)/shard_map/ppermute | solution.py:440
  41.0 0.4 collective-permute-start.12
  41.4 1.0 %collective-permute-done.11.refs_1_ = bf16[256,512]{1,0:T(8,128)(2,1)S(1)} collective-permute-done((bf16[256,512]{1,0:T(8,128)(2,1)S(1)}, bf16[256,512]{1,0:T(8,128)(2,1)S(1)}, u32[]{:S(2)}, u32[]{:S(2)}) %collective-permute-start.11) | collective-permute-done | bytes 262176 | tf_op jit(solution)/shard_map/ppermute | solution.py:440
  42.5 0.4 collective-permute-done.12.refs_3_
  42.8 3.3 %shard_map.180 = (f32[512,512]{1,0:T(8,128)S(1)}, f32[512,512]{1,0:T(8,128)S(1)}, bf16[512,512]{1,0:T(8,128)(2,1)S(1)}, bf16[1024,512]{1,0:T(8,128)(2,1)S(1)}, f...) custom-call(f32[8,512]{1,0:T(8,128)S(1)} %get-tuple-element.117.bias_row, ...), custom_call_target="tpu_custom_call" | custom-call | flops 1000 | bytes 1000 | tf_op jit(solution)/shard_map/pallas_call | solution.py:24
  46.3 1.4 %shard_map.181 = (f32[128,512]{1,0:T(8,128)S(1)}, f32[128,512]{1,0:T(8,128)S(1)}, bf16[256,512]{1,0:T(8,128)(2,1)S(1)}, bf16[256,512]{1,0:T(8,128)(2,1)S(1)}, bf...) custom-call(f32[512,512]{1,0:T(8,128)S(1)} %get-tuple-element.132.total_up, ...), custom_call_target="tpu_custom_call" | custom-call | flops 1000 | bytes 1000 | tf_op jit(solution)/shard_map/pallas_call | solution.py:24
  47.7 0.4 collective-permute-start.17
  48.4 2.3 %collective-permute-start.16 = (bf16[256,512]{1,0:T(8,128)(2,1)S(1)}, bf16[256,512]{1,0:T(8,128)(2,1)S(1)}, u32[]{:S(2)}, u32[]{:S(2)}) collective-permute-start(bf16[256,512]{1,0:T(8,128)(2,1)S(1)} %slice.123), channel_id=1, source_target_pairs={{0,2},{1,3},{2,0},{3,1},{4,6},{5,7},{6,4},{7,5},{8,10},{9,11},{10,... | collective-permute-start | bytes 786440 | tf_op jit(solution)/shard_map/ppermute | solution.py:440
  50.8 1.9 %collective-permute-start.20 = (bf16[256,512]{1,0:T(8,128)(2,1)S(1)}, bf16[256,512]{1,0:T(8,128)(2,1)S(1)}, u32[]{:S(2)}, u32[]{:S(2)}) collective-permute-start(bf16[256,512]{1,0:T(8,128)(2,1)S(1)} %get-tuple-element.149), channel_id=1, source_target_pairs={{0,4},{1,5},{2,6},{3,7},{4,8},{5,9},{6,10},{7,11},{8,12},{9,13},{1... | collective-permute-start | bytes 786440 | tf_op jit(solution)/shard_map/ppermute | solution.py:446
  52.7 2.0 %collective-permute-start.21 = (bf16[256,512]{1,0:T(8,128)(2,1)S(1)}, bf16[256,512]{1,0:T(8,128)(2,1)S(1)}, u32[]{:S(2)}, u32[]{:S(2)}) collective-permute-start(bf16[256,512]{1,0:T(8,128)(2,1)S(1)} %get-tuple-element.150), channel_id=1, source_target_pairs={{0,12},{1,13},{2,14},{3,15},{4,0},{5,1},{6,2},{7,3},{8,4},{9,5},{1... | collective-permute-start | bytes 786440 | tf_op jit(solution)/shard_map/ppermute | solution.py:446
  54.7 2.6 %collective-permute-done.16.refs_1_ = bf16[256,512]{1,0:T(8,128)(2,1)S(1)} collective-permute-done((bf16[256,512]{1,0:T(8,128)(2,1)S(1)}, bf16[256,512]{1,0:T(8,128)(2,1)S(1)}, u32[]{:S(2)}, u32[]{:S(2)}) %collective-permute-start.16) | collective-permute-done | bytes 262176 | tf_op jit(solution)/shard_map/ppermute | solution.py:440
  57.5 1.8 %collective-permute-start.19 = (bf16[256,512]{1,0:T(8,128)(2,1)S(1)}, bf16[256,512]{1,0:T(8,128)(2,1)S(1)}, u32[]{:S(2)}, u32[]{:S(2)}) collective-permute-start(bf16[256,512]{1,0:T(8,128)(2,1)S(1)} %slice.122), channel_id=1, source_target_pairs={{0,2},{1,3},{2,0},{3,1},{4,6},{5,7},{6,4},{7,5},{8,10},{9,11},{10,... | collective-permute-start | bytes 786440 | tf_op jit(solution)/shard_map/ppermute | solution.py:440
  59.7 2.7 %shard_map.183 = f32[4,64,128]{2,1,0:T(8,128)S(1)} custom-call(bf16[4,64,512]{2,1,0:T(8,128)(2,1)S(1)} %get-tuple-element.155.dconv, bf16[4,64,512]{2,1,0:T(8,128)(2,1)S(1)} %copy-done.1, bf16[4,64,512]{2,1,0:T(8,128)(2,1)S(1)} %collective-permute-done.outer, bf16[4,64,512]{2,1,0:T(8,128)(2,1)S(1)} %collective-permute-done.1.inner, ...), custom_call_target="tpu_custom_call" | custom-call | flops 1000 | bytes 1000 | tf_op jit(solution)/shard_map/pallas_call | solution.py:24
  62.5 0.7 collective-permute-start.23
  63.2 0.6 collective-permute-done.18
  63.9 2.4 %collective-permute-done.21.refs_4_ = bf16[256,512]{1,0:T(8,128)(2,1)S(1)} collective-permute-done((bf16[256,512]{1,0:T(8,128)(2,1)S(1)}, bf16[256,512]{1,0:T(8,128)(2,1)S(1)}, u32[]{:S(2)}, u32[]{:S(2)}) %collective-permute-start.21) | collective-permute-done | bytes 262176 | tf_op jit(solution)/shard_map/ppermute | solution.py:446
  66.3 0.7 collective-permute-start.26
  66.9 3.4 %collective-permute-start.22 = (f32[4,64,128]{2,1,0:T(8,128)S(1)}, f32[4,64,128]{2,1,0:T(8,128)S(1)}, u32[]{:S(2)}, u32[]{:S(2)}) collective-permute-start(f32[4,64,128]{2,1,0:T(8,128)S(1)} %add.40), channel_id=1, source_target_pairs={{0,2},{1,3},{2,0},{3,1},{4,6},{5,7},{6,4},{7,5},{8,10},{9,11},{10,... | collective-permute-start | bytes 393224 | tf_op jit(solution)/shard_map/ppermute | solution.py:440
  70.5 0.8 add_convert_fusion
  71.2 6.2 %collective-permute-done.22 = f32[4,64,128]{2,1,0:T(8,128)S(1)} collective-permute-done((f32[4,64,128]{2,1,0:T(8,128)S(1)}, f32[4,64,128]{2,1,0:T(8,128)S(1)}, u32[]{:S(2)}, u32[]{:S(2)}) %collective-permute-start.22) | collective-permute-done | bytes 131104 | tf_op jit(solution)/shard_map/ppermute | solution.py:440
  77.5 0.4 collective-permute-done.23.refs_3_
  77.8 1.1 %collective-permute-start.25 = (f32[2,64,128]{2,1,0:T(8,128)S(1)}, f32[2,64,128]{2,1,0:T(8,128)S(1)}, u32[]{:S(2)}, u32[]{:S(2)}) collective-permute-start(f32[2,64,128]{2,1,0:T(8,128)S(1)} %slice.89), channel_id=1, source_target_pairs={{0,8},{1,9},{2,10},{3,11},{4,12},{5,13},{6,14},{7,15},{8,0},{9,1},... | collective-permute-start | bytes 196616 | tf_op jit(solution)/shard_map/ppermute | solution.py:454
  78.9 0.8 shard_map.185
  79.7 2.5 %collective-permute-start.27 = (bf16[64,512]{1,0:T(8,128)(2,1)S(1)}, bf16[64,512]{1,0:T(8,128)(2,1)S(1)}, u32[]{:S(2)}, u32[]{:S(2)}) collective-permute-start(bf16[64,512]{1,0:T(8,128)(2,1)S(1)} %pad_maximum_fusion.2), channel_id=1, source_target_pairs={{0,2},{1,3},{2,0},{3,1},{4,6},{5,7},{6,4},{7,5},{8,10},{9,11},{10,... | collective-permute-start | bytes 196616 | tf_op jit(solution)/shard_map/ppermute | solution.py:440
  82.2 3.1 %shard_map.184 = bf16[4,64,512]{2,1,0:T(8,128)(2,1)} custom-call(bf16[4,64,512]{2,1,0:T(8,128)(2,1)S(1)} %get-tuple-element.155.dconv, bf16[4,64,512]{2,1,0:T(8,128)(2,1)S(1)} %collective-permute-done.26.outer, bf16[4,64,512]{2,1,0:T(8,128)(2,1)S(1)} %collective-permute-done.24.inner, bf16[4,64,512]{2,1,0:T(8,128)(2,1)S(1)} %copy-done, ...), custom_call_target="tpu_custom_call" | custom-call | flops 1000 | bytes 1000 | tf_op jit(solution)/shard_map/pallas_call | solution.py:24
  85.4 2.0 %collective-permute-start.29 = (f32[64,128]{1,0:T(8,128)S(1)}, f32[64,128]{1,0:T(8,128)S(1)}, u32[]{:S(2)}, u32[]{:S(2)}) collective-permute-start(f32[64,128]{1,0:T(8,128)S(1)} %get-tuple-element.188), channel_id=1, source_target_pairs={{0,4},{1,5},{2,6},{3,7},{4,0},{5,1},{6,2},{7,3},{8,12},{9,13},{10,... | collective-permute-start | bytes 98312 | tf_op jit(solution)/shard_map/ppermute | solution.py:454
  87.5 0.8 shard_map.186
  88.2 1.2 %collective-permute-done.29.refs_1_ = f32[64,128]{1,0:T(8,128)S(1)} collective-permute-done((f32[64,128]{1,0:T(8,128)S(1)}, f32[64,128]{1,0:T(8,128)S(1)}, u32[]{:S(2)}, u32[]{:S(2)}) %collective-permute-start.29) | collective-permute-done | bytes 32800 | tf_op jit(solution)/shard_map/ppermute | solution.py:454
  89.5 0.9 shard_map.187
  (60 shorter events, 1.6 us)
Async XLA Ops:
  2.5 5.7 %copy-start.5 = (bf16[64,128]{1,0:T(8,128)(2,1)S(1)}, bf16[64,128]{1,0:T(8,128)(2,1)}, u32[]{:S(2)}) copy-start(bf16[64,128]{1,0:T(8,128)(2,1)} %get-tuple-element.97) | copy-start | bytes 49156
  2.5 5.7 %collective-permute-start.2 = (bf16[320,128]{1,0:T(8,128)(2,1)}, bf16[320,128]{1,0:T(8,128)(2,1)S(1)}, u32[]{:S(2)}, u32[]{:S(2)}) collective-permute-start(bf16[320,128]{1,0:T(8,128)(2,1)} %get-tuple-element.99), channel_id=1, source_target_pairs={{0,2},{1,3},{2,0},{3,1},{4,6},{5,7},{6,4},{7,5},{8,10},{9,11},{10,... | collective-permute-start | bytes 245768 | tf_op jit(solution)/shard_map/ppermute | solution.py:440
  8.2 0.8 copy-start.4
  9.0 3.5 %copy-start.2 = (bf16[128,512]{1,0:T(8,128)(2,1)S(1)}, bf16[128,512]{1,0:T(8,128)(2,1)}, u32[]{:S(2)}) copy-start(bf16[128,512]{1,0:T(8,128)(2,1)} %down) | copy-start | bytes 393220
  9.0 1.3 %collective-permute-start.3 = (bf16[320,128]{1,0:T(8,128)(2,1)S(1)}, bf16[320,128]{1,0:T(8,128)(2,1)S(1)}, u32[]{:S(2)}, u32[]{:S(2)}) collective-permute-start(bf16[320,128]{1,0:T(8,128)(2,1)S(1)} %pad_maximum_fusion), channel_id=1, source_target_pairs={{0,1},{1,0},{2,3},{3,2},{4,5},{5,4},{6,7},{7,6},{8,9},{9,8},{10,11... | collective-permute-start | bytes 245768 | tf_op jit(solution)/shard_map/ppermute | solution.py:440
  10.4 2.2 %copy-start.3 = (bf16[128,128]{1,0:T(8,128)(2,1)S(1)}, bf16[128,128]{1,0:T(8,128)(2,1)}, u32[]{:S(2)}) copy-start(bf16[128,128]{1,0:T(8,128)(2,1)} %get-tuple-element.109.refs_0_) | copy-start | bytes 98308
  10.4 6.9 %copy-start.1 = (bf16[4,64,512]{2,1,0:T(8,128)(2,1)S(1)}, bf16[4,64,512]{2,1,0:T(8,128)(2,1)}, u32[]{:S(2)}) copy-start(bf16[4,64,512]{2,1,0:T(8,128)(2,1)} %features.1) | copy-start | bytes 786436
  10.4 10.5 %copy-start = (bf16[4,64,512]{2,1,0:T(8,128)(2,1)S(1)}, bf16[4,64,512]{2,1,0:T(8,128)(2,1)}, u32[]{:S(2)}) copy-start(bf16[4,64,512]{2,1,0:T(8,128)(2,1)} %cotangent.1) | copy-start | bytes 786436
  10.4 3.8 %collective-permute-start.4 = (bf16[64,128]{1,0:T(8,128)(2,1)S(1)}, bf16[64,128]{1,0:T(8,128)(2,1)S(1)}, u32[]{:S(2)}, u32[]{:S(2)}) collective-permute-start(bf16[64,128]{1,0:T(8,128)(2,1)S(1)} %slice_add_fusion.2), channel_id=1, source_target_pairs={{0,4},{1,5},{2,6},{3,7},{4,0},{5,1},{6,2},{7,3},{8,12},{9,13},{10,... | collective-permute-start | bytes 49160 | tf_op jit(solution)/shard_map/ppermute | solution.py:454
  12.6 11.4 %collective-permute-start.6 = (bf16[256,512]{1,0:T(8,128)(2,1)S(1)}, bf16[256,512]{1,0:T(8,128)(2,1)S(1)}, u32[]{:S(2)}, u32[]{:S(2)}) collective-permute-start(bf16[256,512]{1,0:T(8,128)(2,1)S(1)} %bitcast.24), channel_id=1, source_target_pairs={{0,4},{1,5},{2,6},{3,7},{4,8},{5,9},{6,10},{7,11},{8,12},{9,13},{1... | collective-permute-start | bytes 786440 | tf_op jit(solution)/shard_map/ppermute | solution.py:446
  14.2 9.7 %collective-permute-start.5 = (bf16[128,128]{1,0:T(8,128)(2,1)S(1)}, bf16[128,128]{1,0:T(8,128)(2,1)S(1)}, u32[]{:S(2)}, u32[]{:S(2)}) collective-permute-start(bf16[128,128]{1,0:T(8,128)(2,1)S(1)} %pad_maximum_fusion.4), channel_id=1, source_target_pairs={{0,8},{1,9},{2,10},{3,11},{4,12},{5,13},{6,14},{7,15},{8,0},{9,1},... | collective-permute-start | bytes 98312 | tf_op jit(solution)/shard_map/ppermute | solution.py:454
  17.3 9.0 %collective-permute-start = (bf16[4,64,512]{2,1,0:T(8,128)(2,1)S(1)}, bf16[4,64,512]{2,1,0:T(8,128)(2,1)S(1)}, u32[]{:S(2)}, u32[]{:S(2)}) collective-permute-start(bf16[4,64,512]{2,1,0:T(8,128)(2,1)S(1)} %copy-done.1), channel_id=1, source_target_pairs={{1,2},{3,4},{5,6},{7,8},{9,10},{11,12},{13,14},{2,1},{4,3},{6,5},{... | collective-permute-start | bytes 786440 | tf_op jit(solution)/shard_map/ppermute | solution.py:451
  17.9 8.4 %collective-permute-start.1 = (bf16[4,64,512]{2,1,0:T(8,128)(2,1)S(1)}, bf16[4,64,512]{2,1,0:T(8,128)(2,1)S(1)}, u32[]{:S(2)}, u32[]{:S(2)}) collective-permute-start(bf16[4,64,512]{2,1,0:T(8,128)(2,1)S(1)} %copy-done.1), channel_id=1, source_target_pairs={{0,1},{1,0},{2,3},{3,2},{4,5},{5,4},{6,7},{7,6},{8,9},{9,8},{10,11... | collective-permute-start | bytes 786440 | tf_op jit(solution)/shard_map/ppermute | solution.py:440
  20.9 10.2 %collective-permute-start.7 = (bf16[256,512]{1,0:T(8,128)(2,1)S(1)}, bf16[256,512]{1,0:T(8,128)(2,1)S(1)}, u32[]{:S(2)}, u32[]{:S(2)}) collective-permute-start(bf16[256,512]{1,0:T(8,128)(2,1)S(1)} %bitcast.20), channel_id=1, source_target_pairs={{0,2},{1,3},{2,0},{3,1},{4,6},{5,7},{6,4},{7,5},{8,10},{9,11},{10,... | collective-permute-start | bytes 786440 | tf_op jit(solution)/shard_map/ppermute | solution.py:440
  23.9 14.6 %collective-permute-start.9 = (bf16[256,512]{1,0:T(8,128)(2,1)S(1)}, bf16[256,512]{1,0:T(8,128)(2,1)S(1)}, u32[]{:S(2)}, u32[]{:S(2)}) collective-permute-start(bf16[256,512]{1,0:T(8,128)(2,1)S(1)} %bitcast.25), channel_id=1, source_target_pairs={{0,8},{1,9},{2,10},{3,11},{4,12},{5,13},{6,14},{7,15},{8,0},{9,1},... | collective-permute-start | bytes 786440 | tf_op jit(solution)/shard_map/ppermute | solution.py:446
  23.9 14.6 %collective-permute-start.10 = (bf16[256,512]{1,0:T(8,128)(2,1)S(1)}, bf16[256,512]{1,0:T(8,128)(2,1)S(1)}, u32[]{:S(2)}, u32[]{:S(2)}) collective-permute-start(bf16[256,512]{1,0:T(8,128)(2,1)S(1)} %bitcast.26), channel_id=1, source_target_pairs={{0,12},{1,13},{2,14},{3,15},{4,0},{5,1},{6,2},{7,3},{8,4},{9,5},{1... | collective-permute-start | bytes 786440 | tf_op jit(solution)/shard_map/ppermute | solution.py:446
  31.1 9.8 %collective-permute-start.8 = (bf16[256,512]{1,0:T(8,128)(2,1)S(1)}, bf16[256,512]{1,0:T(8,128)(2,1)S(1)}, u32[]{:S(2)}, u32[]{:S(2)}) collective-permute-start(bf16[256,512]{1,0:T(8,128)(2,1)S(1)} %get-tuple-element.122.refs_0_), channel_id=1, source_target_pairs={{0,2},{1,3},{2,0},{3,1},{4,6},{5,7},{6,4},{7,5},{8,10},{9,11},{10,... | collective-permute-start | bytes 786440 | tf_op jit(solution)/shard_map/ppermute | solution.py:440
  34.0 7.4 %collective-permute-start.13 = (bf16[256,512]{1,0:T(8,128)(2,1)S(1)}, bf16[256,512]{1,0:T(8,128)(2,1)S(1)}, u32[]{:S(2)}, u32[]{:S(2)}) collective-permute-start(bf16[256,512]{1,0:T(8,128)(2,1)S(1)} %bitcast.21), channel_id=1, source_target_pairs={{0,1},{1,0},{2,3},{3,2},{4,5},{5,4},{6,7},{7,6},{8,9},{9,8},{10,11... | collective-permute-start | bytes 786440 | tf_op jit(solution)/shard_map/ppermute | solution.py:440
  34.7 6.7 %collective-permute-start.14 = (bf16[256,512]{1,0:T(8,128)(2,1)S(1)}, bf16[256,512]{1,0:T(8,128)(2,1)S(1)}, u32[]{:S(2)}, u32[]{:S(2)}) collective-permute-start(bf16[256,512]{1,0:T(8,128)(2,1)S(1)} %collective-permute-done.7.refs_6_.refs_2_), channel_id=1, source_target_pairs={{0,1},{1,0},{2,3},{3,2},{4,5},{5,4},{6,7},{7,6},{8,9},{9,8},{10,11... | collective-permute-start | bytes 786440 | tf_op jit(solution)/shard_map/ppermute | solution.py:440
  40.9 1.5 %collective-permute-start.11 = (bf16[256,512]{1,0:T(8,128)(2,1)S(1)}, bf16[256,512]{1,0:T(8,128)(2,1)S(1)}, u32[]{:S(2)}, u32[]{:S(2)}) collective-permute-start(bf16[256,512]{1,0:T(8,128)(2,1)S(1)} %get-tuple-element.122.refs_0_), channel_id=1, source_target_pairs={{0,1},{1,0},{2,3},{3,2},{4,5},{5,4},{6,7},{7,6},{8,9},{9,8},{10,11... | collective-permute-start | bytes 786440 | tf_op jit(solution)/shard_map/ppermute | solution.py:440
  41.0 1.8 %collective-permute-start.12 = (bf16[256,512]{1,0:T(8,128)(2,1)S(1)}, bf16[256,512]{1,0:T(8,128)(2,1)S(1)}, u32[]{:S(2)}, u32[]{:S(2)}) collective-permute-start(bf16[256,512]{1,0:T(8,128)(2,1)S(1)} %collective-permute-done.8.refs_2_), channel_id=1, source_target_pairs={{0,1},{1,0},{2,3},{3,2},{4,5},{5,4},{6,7},{7,6},{8,9},{9,8},{10,11... | collective-permute-start | bytes 786440 | tf_op jit(solution)/shard_map/ppermute | solution.py:440
  46.1 2.1 %collective-permute-start.15 = (bf16[512,512]{1,0:T(8,128)(2,1)S(1)}, bf16[512,512]{1,0:T(8,128)(2,1)S(1)}, u32[]{:S(2)}, u32[]{:S(2)}) collective-permute-start(bf16[512,512]{1,0:T(8,128)(2,1)S(1)} %get-tuple-element.131), channel_id=1, source_target_pairs={{0,1},{1,0},{2,3},{3,2},{4,5},{5,4},{6,7},{7,6},{8,9},{9,8},{10,11... | collective-permute-start | bytes 1572872 | tf_op jit(solution)/shard_map/ppermute | solution.py:440
  47.7 7.0 %collective-permute-start.17 = (bf16[512,512]{1,0:T(8,128)(2,1)S(1)}, bf16[512,512]{1,0:T(8,128)(2,1)S(1)}, u32[]{:S(2)}, u32[]{:S(2)}) collective-permute-start(bf16[512,512]{1,0:T(8,128)(2,1)S(1)} %get-tuple-element.141), channel_id=1, source_target_pairs={{0,1},{1,0},{2,3},{3,2},{4,5},{5,4},{6,7},{7,6},{8,9},{9,8},{10,11... | collective-permute-start | bytes 1572872 | tf_op jit(solution)/shard_map/ppermute | solution.py:440
  48.4 8.9 %collective-permute-start.16 = (bf16[256,512]{1,0:T(8,128)(2,1)S(1)}, bf16[256,512]{1,0:T(8,128)(2,1)S(1)}, u32[]{:S(2)}, u32[]{:S(2)}) collective-permute-start(bf16[256,512]{1,0:T(8,128)(2,1)S(1)} %slice.123), channel_id=1, source_target_pairs={{0,2},{1,3},{2,0},{3,1},{4,6},{5,7},{6,4},{7,5},{8,10},{9,11},{10,... | collective-permute-start | bytes 786440 | tf_op jit(solution)/shard_map/ppermute | solution.py:440
  50.8 13.1 %collective-permute-start.20 = (bf16[256,512]{1,0:T(8,128)(2,1)S(1)}, bf16[256,512]{1,0:T(8,128)(2,1)S(1)}, u32[]{:S(2)}, u32[]{:S(2)}) collective-permute-start(bf16[256,512]{1,0:T(8,128)(2,1)S(1)} %get-tuple-element.149), channel_id=1, source_target_pairs={{0,4},{1,5},{2,6},{3,7},{4,8},{5,9},{6,10},{7,11},{8,12},{9,13},{1... | collective-permute-start | bytes 786440 | tf_op jit(solution)/shard_map/ppermute | solution.py:446
  52.7 13.6 %collective-permute-start.21 = (bf16[256,512]{1,0:T(8,128)(2,1)S(1)}, bf16[256,512]{1,0:T(8,128)(2,1)S(1)}, u32[]{:S(2)}, u32[]{:S(2)}) collective-permute-start(bf16[256,512]{1,0:T(8,128)(2,1)S(1)} %get-tuple-element.150), channel_id=1, source_target_pairs={{0,12},{1,13},{2,14},{3,15},{4,0},{5,1},{6,2},{7,3},{8,4},{9,5},{1... | collective-permute-start | bytes 786440 | tf_op jit(solution)/shard_map/ppermute | solution.py:446
  57.5 8.7 %collective-permute-start.19 = (bf16[256,512]{1,0:T(8,128)(2,1)S(1)}, bf16[256,512]{1,0:T(8,128)(2,1)S(1)}, u32[]{:S(2)}, u32[]{:S(2)}) collective-permute-start(bf16[256,512]{1,0:T(8,128)(2,1)S(1)} %slice.122), channel_id=1, source_target_pairs={{0,2},{1,3},{2,0},{3,1},{4,6},{5,7},{6,4},{7,5},{8,10},{9,11},{10,... | collective-permute-start | bytes 786440 | tf_op jit(solution)/shard_map/ppermute | solution.py:440
  62.4 1.4 %collective-permute-start.18 = (f32[4,64,128]{2,1,0:T(8,128)S(1)}, f32[4,64,128]{2,1,0:T(8,128)S(1)}, u32[]{:S(2)}, u32[]{:S(2)}) collective-permute-start(f32[4,64,128]{2,1,0:T(8,128)S(1)} %shard_map.183), channel_id=1, source_target_pairs={{0,1},{1,0},{2,3},{3,2},{4,5},{5,4},{6,7},{7,6},{8,9},{9,8},{10,11... | collective-permute-start | bytes 393224 | tf_op jit(solution)/shard_map/ppermute | solution.py:440
  62.5 15.3 %collective-permute-start.23 = (bf16[256,512]{1,0:T(8,128)(2,1)S(1)}, bf16[256,512]{1,0:T(8,128)(2,1)S(1)}, u32[]{:S(2)}, u32[]{:S(2)}) collective-permute-start(bf16[256,512]{1,0:T(8,128)(2,1)S(1)} %get-tuple-element.153), channel_id=1, source_target_pairs={{0,8},{1,9},{2,10},{3,11},{4,12},{5,13},{6,14},{7,15},{8,0},{9,1},... | collective-permute-start | bytes 786440 | tf_op jit(solution)/shard_map/ppermute | solution.py:446
  66.3 11.6 %collective-permute-start.24 = (bf16[4,64,512]{2,1,0:T(8,128)(2,1)S(1)}, bf16[4,64,512]{2,1,0:T(8,128)(2,1)S(1)}, u32[]{:S(2)}, u32[]{:S(2)}) collective-permute-start(bf16[4,64,512]{2,1,0:T(8,128)(2,1)S(1)} %get-tuple-element.155.dconv), channel_id=1, source_target_pairs={{0,1},{1,0},{2,3},{3,2},{4,5},{5,4},{6,7},{7,6},{8,9},{9,8},{10,11... | collective-permute-start | bytes 786440 | tf_op jit(solution)/shard_map/ppermute | solution.py:440
  66.3 15.9 %collective-permute-start.26 = (bf16[4,64,512]{2,1,0:T(8,128)(2,1)S(1)}, bf16[4,64,512]{2,1,0:T(8,128)(2,1)S(1)}, u32[]{:S(2)}, u32[]{:S(2)}) collective-permute-start(bf16[4,64,512]{2,1,0:T(8,128)(2,1)S(1)} %get-tuple-element.155.dconv), channel_id=1, source_target_pairs={{1,2},{3,4},{5,6},{7,8},{9,10},{11,12},{13,14},{2,1},{4,3},{6,5},{... | collective-permute-start | bytes 786440 | tf_op jit(solution)/shard_map/ppermute | solution.py:451
  66.9 10.5 %collective-permute-start.22 = (f32[4,64,128]{2,1,0:T(8,128)S(1)}, f32[4,64,128]{2,1,0:T(8,128)S(1)}, u32[]{:S(2)}, u32[]{:S(2)}) collective-permute-start(f32[4,64,128]{2,1,0:T(8,128)S(1)} %add.40), channel_id=1, source_target_pairs={{0,2},{1,3},{2,0},{3,1},{4,6},{5,7},{6,4},{7,5},{8,10},{9,11},{10,... | collective-permute-start | bytes 393224 | tf_op jit(solution)/shard_map/ppermute | solution.py:440
  77.8 7.4 %collective-permute-start.25 = (f32[2,64,128]{2,1,0:T(8,128)S(1)}, f32[2,64,128]{2,1,0:T(8,128)S(1)}, u32[]{:S(2)}, u32[]{:S(2)}) collective-permute-start(f32[2,64,128]{2,1,0:T(8,128)S(1)} %slice.89), channel_id=1, source_target_pairs={{0,8},{1,9},{2,10},{3,11},{4,12},{5,13},{6,14},{7,15},{8,0},{9,1},... | collective-permute-start | bytes 196616 | tf_op jit(solution)/shard_map/ppermute | solution.py:454
  79.7 5.6 %collective-permute-start.27 = (bf16[64,512]{1,0:T(8,128)(2,1)S(1)}, bf16[64,512]{1,0:T(8,128)(2,1)S(1)}, u32[]{:S(2)}, u32[]{:S(2)}) collective-permute-start(bf16[64,512]{1,0:T(8,128)(2,1)S(1)} %pad_maximum_fusion.2), channel_id=1, source_target_pairs={{0,2},{1,3},{2,0},{3,1},{4,6},{5,7},{6,4},{7,5},{8,10},{9,11},{10,... | collective-permute-start | bytes 196616 | tf_op jit(solution)/shard_map/ppermute | solution.py:440
  85.3 2.1 %collective-permute-start.28 = (bf16[64,512]{1,0:T(8,128)(2,1)S(1)}, bf16[64,512]{1,0:T(8,128)(2,1)S(1)}, u32[]{:S(2)}, u32[]{:S(2)}) collective-permute-start(bf16[64,512]{1,0:T(8,128)(2,1)S(1)} %pad_maximum_fusion.3), channel_id=1, source_target_pairs={{0,1},{1,0},{2,3},{3,2},{4,5},{5,4},{6,7},{7,6},{8,9},{9,8},{10,11... | collective-permute-start | bytes 196616 | tf_op jit(solution)/shard_map/ppermute | solution.py:440
  85.4 4.0 %collective-permute-start.29 = (f32[64,128]{1,0:T(8,128)S(1)}, f32[64,128]{1,0:T(8,128)S(1)}, u32[]{:S(2)}, u32[]{:S(2)}) collective-permute-start(f32[64,128]{1,0:T(8,128)S(1)} %get-tuple-element.188), channel_id=1, source_target_pairs={{0,4},{1,5},{2,6},{3,7},{4,0},{5,1},{6,2},{7,3},{8,12},{9,13},{10,... | collective-permute-start | bytes 98312 | tf_op jit(solution)/shard_map/ppermute | solution.py:454

commit v6 on v5

--- a/solution.py
+++ b/solution.py
@@ -257,7 +257,7 @@
 def mlp_kernel(quads, layers, bias_row, *refs):
     normals, refs = refs[:quads], refs[quads:]
     cots, refs = refs[:quads], refs[quads:]
-    weights, (total, even, odd, act, upb, down, up) = refs[:-7], refs[-7:]
+    weights, (total, even, odd, act, upb, down, up, cells_in, slopes) = refs[:-9], refs[-9:]
     layer, _ = place(quads)
     cells, chans = normals[0].shape
     hidden_units = act.shape[1]
@@ -290,26 +290,26 @@
             odd[at, :] = dnorm.astype(bf16)
         else:
             even[at, :] = dnorm
-        grad = lax.dot_general(
-            normals[i][...], dhidden, (((0,), (0,)), ((), ())), preferred_element_type=f32
-        )
-        total[...] = grad if i == 0 else total[...] + grad
+        cells_in[i * cells : (i + 1) * cells, :] = normals[i][...]
+        slopes[i * cells : (i + 1) * cells, :] = dhidden
+    total[...] = lax.dot_general(
+        cells_in[...], slopes[...], (((0,), (0,)), ((), ())), preferred_element_type=f32
+    )
     upb[...] = jnp.broadcast_to(bias_sum, upb.shape)
 
 
 def out_kernel(quads, layers, scale, total_up, act, down, *refs):
     cots, refs = refs[:quads], refs[quads:]
     own_down, own_up, refs = refs[0], refs[1], refs[2:]
-    sends, (even, odd, total) = refs[:-3], refs[-3:]
+    sends, (even, odd, total, held) = refs[:-4], refs[-4:]
     layer, _ = place(quads)
     cells = cots[0].shape[0]
     part = down.shape[0] // layers
     for i in range(quads):
-        block = act[i * cells : (i + 1) * cells, :]
-        grad = lax.dot_general(
-            block, cots[i][...], (((0,), (0,)), ((), ())), preferred_element_type=f32
-        )
-        total[...] = grad if i == 0 else total[...] + grad
+        held[i * cells : (i + 1) * cells, :] = cots[i][...]
+    total[...] = lax.dot_general(
+        act[...], held[...], (((0,), (0,)), ((), ())), preferred_element_type=f32
+    )
     for step in range(layers):
         if step == 0:
             one, two = own_down, own_up
@@ -580,7 +580,11 @@
         [((chans, share), f32), ((half, chans), f32), ((half, chans), bf16)]
         + [((quads * cells, share), bf16), ((8, share), f32), ((share, chans), bf16)],
         (bias, *normals, *cots, *(block for held in weights for block in held)),
-        [pltpu.VMEM((chans, share), bf16)],
+        [
+            pltpu.VMEM((chans, share), bf16),
+            pltpu.VMEM((quads * cells, chans), bf16),
+            pltpu.VMEM((quads * cells, share), bf16),
+        ],
         mib=40,
     )
     sums = near(even, odd)
@@ -594,7 +598,7 @@
         + [(shape, bf16) for shape in shapes]
         + [((half, chans), f32), ((half, chans), bf16)],
         (total_up, act, down_full, *cots),
-        [pltpu.VMEM((share, chans), f32)],
+        [pltpu.VMEM((share, chans), f32), pltpu.VMEM((quads * cells, chans), bf16)],
         mib=40,
     )
     sums, sends = lax.optimization_barrier((sums, sends))

time: 90.6 us -> 90.6 us (level)
  no operation moved by 1% of the time
where the time goes in v6:
time: 90.6 us; the launch traced here: 90.3 us
  starting transfers between devices  40 us (44%)
  waiting for transfers between devices  28.7 us (32%)
  Pallas kernels  18.6 us (21%)
  other arithmetic  1.23 us (1%)
  between operations  0.94 us (1%)
    ppermute x18, starting transfers between devices, swap(): return lax.ppermute(value, 'row', [(i, i ^ other) for i in range(devices)])  22.7 us
    ppermute x18, waiting for transfers between devices, swap(): return lax.ppermute(value, 'row', [(i, i ^ other) for i in range(devices)])  18.7 us
    pallas_call x11, Pallas kernels, call(): pl.pallas_call(kernel, out_shape=[jax.ShapeDtypeStruct(shape, dtype) for...  18.6 us
    ppermute x4, starting transfers between devices, cross(): lax.ppermute(value, 'row', [(i, (i // quads ^ other) * quads + i % quads)...  8.25 us
    ppermute x6, starting transfers between devices, turn(): return lax.ppermute(value, 'row', pairs)  7.68 us
    ppermute x6, waiting for transfers between devices, turn(): return lax.ppermute(value, 'row', pairs)  6.53 us
    ppermute x4, waiting for transfers between devices, cross(): lax.ppermute(value, 'row', [(i, (i // quads ^ other) * quads + i % quads)...  3.51 us
  transfers between devices with their start and end apart: 30, of which 15 were waited for; matrix products, arithmetic and copies ran while one was open for 1% of the time, Pallas kernels for 14%

profile of v6, /device:TPU:0, one launch (start us, length us, event | category | flops | bytes accessed | tf_op | source)
XLA Modules:
  0.0 90.3 jit_solution(15453221556915964095)
XLA Ops:
  0.6 1.9 %shard_map.177 = (bf16[128,128]{1,0:T(8,128)(2,1)}, bf16[128,128]{1,0:T(8,128)(2,1)}, bf16[64,128]{1,0:T(8,128)(2,1)}, bf16[320,128]{1,0:T(8,128)(2,1)}) custom-call(bf16[32,49]{1,0:T(8,128)(2,1)} %bitcast.30, bf16[1,32]{1,0:T(2,128)(2,1)} %bitcast.31, bf16[1,32]{1,0:T(2,128)(2,1)} %bitcast.32, bf16[1,32]{1,0:T(2,128)(2,1)} %bitcast.33, ...), custom_call_target="tpu_custom_call" | custom-call | flops 1000 | bytes 1000 | tf_op jit(solution)/shard_map/pallas_call | solution.py:24
  2.5 3.0 %collective-permute-start.2 = (bf16[320,128]{1,0:T(8,128)(2,1)}, bf16[320,128]{1,0:T(8,128)(2,1)S(1)}, u32[]{:S(2)}, u32[]{:S(2)}) collective-permute-start(bf16[320,128]{1,0:T(8,128)(2,1)} %get-tuple-element.99), channel_id=1, source_target_pairs={{0,2},{1,3},{2,0},{3,1},{4,6},{5,7},{6,4},{7,5},{8,10},{9,11},{10,... | collective-permute-start | bytes 245768 | tf_op jit(solution)/shard_map/ppermute | solution.py:440
  5.6 2.7 %collective-permute-done.2 = bf16[320,128]{1,0:T(8,128)(2,1)S(1)} collective-permute-done((bf16[320,128]{1,0:T(8,128)(2,1)}, bf16[320,128]{1,0:T(8,128)(2,1)S(1)}, u32[]{:S(2)}, u32[]{:S(2)}) %collective-permute-start.2) | collective-permute-done | bytes 81952 | tf_op jit(solution)/shard_map/ppermute | solution.py:440
  8.3 0.7 copy-done.4
  9.1 1.3 %collective-permute-done.3 = bf16[320,128]{1,0:T(8,128)(2,1)S(1)} collective-permute-done((bf16[320,128]{1,0:T(8,128)(2,1)S(1)}, bf16[320,128]{1,0:T(8,128)(2,1)S(1)}, u32[]{:S(2)}, u32[]{:S(2)}) %collective-permute-start.3) | collective-permute-done | bytes 81952 | tf_op jit(solution)/shard_map/ppermute | solution.py:440
  10.4 2.1 %collective-permute-start.4 = (bf16[64,128]{1,0:T(8,128)(2,1)S(1)}, bf16[64,128]{1,0:T(8,128)(2,1)S(1)}, u32[]{:S(2)}, u32[]{:S(2)}) collective-permute-start(bf16[64,128]{1,0:T(8,128)(2,1)S(1)} %slice_add_fusion.2), channel_id=1, source_target_pairs={{0,4},{1,5},{2,6},{3,7},{4,0},{5,1},{6,2},{7,3},{8,12},{9,13},{10,... | collective-permute-start | bytes 49160 | tf_op jit(solution)/shard_map/ppermute | solution.py:454
  12.6 0.7 collective-permute-start.6
  13.3 1.0 %collective-permute-done.4 = bf16[64,128]{1,0:T(8,128)(2,1)S(1)} collective-permute-done((bf16[64,128]{1,0:T(8,128)(2,1)S(1)}, bf16[64,128]{1,0:T(8,128)(2,1)S(1)}, u32[]{:S(2)}, u32[]{:S(2)}) %collective-permute-start.4) | collective-permute-done | bytes 16416 | tf_op jit(solution)/shard_map/ppermute | solution.py:454
  14.2 3.0 %collective-permute-start.5 = (bf16[128,128]{1,0:T(8,128)(2,1)S(1)}, bf16[128,128]{1,0:T(8,128)(2,1)S(1)}, u32[]{:S(2)}, u32[]{:S(2)}) collective-permute-start(bf16[128,128]{1,0:T(8,128)(2,1)S(1)} %pad_maximum_fusion.4), channel_id=1, source_target_pairs={{0,8},{1,9},{2,10},{3,11},{4,12},{5,13},{6,14},{7,15},{8,0},{9,1},... | collective-permute-start | bytes 98312 | tf_op jit(solution)/shard_map/ppermute | solution.py:454
  17.3 0.7 collective-permute-start
  17.9 2.9 %collective-permute-start.1 = (bf16[4,64,512]{2,1,0:T(8,128)(2,1)S(1)}, bf16[4,64,512]{2,1,0:T(8,128)(2,1)S(1)}, u32[]{:S(2)}, u32[]{:S(2)}) collective-permute-start(bf16[4,64,512]{2,1,0:T(8,128)(2,1)S(1)} %copy-done.1), channel_id=1, source_target_pairs={{0,1},{1,0},{2,3},{3,2},{4,5},{5,4},{6,7},{7,6},{8,9},{9,8},{10,11... | collective-permute-start | bytes 786440 | tf_op jit(solution)/shard_map/ppermute | solution.py:440
  20.9 1.7 %collective-permute-start.7 = (bf16[256,512]{1,0:T(8,128)(2,1)S(1)}, bf16[256,512]{1,0:T(8,128)(2,1)S(1)}, u32[]{:S(2)}, u32[]{:S(2)}) collective-permute-start(bf16[256,512]{1,0:T(8,128)(2,1)S(1)} %bitcast.20), channel_id=1, source_target_pairs={{0,2},{1,3},{2,0},{3,1},{4,6},{5,7},{6,4},{7,5},{8,10},{9,11},{10,... | collective-permute-start | bytes 786440 | tf_op jit(solution)/shard_map/ppermute | solution.py:440
  22.6 1.3 %collective-permute-done.5 = bf16[128,128]{1,0:T(8,128)(2,1)S(1)} collective-permute-done((bf16[128,128]{1,0:T(8,128)(2,1)S(1)}, bf16[128,128]{1,0:T(8,128)(2,1)S(1)}, u32[]{:S(2)}, u32[]{:S(2)}) %collective-permute-start.5) | collective-permute-done | bytes 32800 | tf_op jit(solution)/shard_map/ppermute | solution.py:454
  23.9 2.4 %collective-permute-start.10 = (bf16[256,512]{1,0:T(8,128)(2,1)S(1)}, bf16[256,512]{1,0:T(8,128)(2,1)S(1)}, u32[]{:S(2)}, u32[]{:S(2)}) collective-permute-start(bf16[256,512]{1,0:T(8,128)(2,1)S(1)} %bitcast.26), channel_id=1, source_target_pairs={{0,12},{1,13},{2,14},{3,15},{4,0},{5,1},{6,2},{7,3},{8,4},{9,5},{1... | collective-permute-start | bytes 786440 | tf_op jit(solution)/shard_map/ppermute | solution.py:446
  26.3 3.4 %shard_map.179 = (bf16[256,512]{1,0:T(8,128)(2,1)S(1)}, f32[256,512]{1,0:T(8,128)S(1)}, f32[256,128]{1,0:T(8,128)S(1)}, f32[64,512]{1,0:T(8,128)S(1)}, f32[8,512]{1,0:T(8,128)S(1)}) custom-call(bf16[4,64,512]{2,1,0:T(8,128)(2,1)S(1)} %copy-done.1, bf16[4,64,512]{2,1,0:T(8,128)(2,1)S(1)} %collective-permute-done.outer, ...), custom_call_target="tpu_custom_call" | custom-call | flops 1000 | bytes 1000 | tf_op jit(solution)/shard_map/pallas_call | solution.py:24
  29.7 1.4 %collective-permute-done.7.refs_6_.refs_2_ = bf16[256,512]{1,0:T(8,128)(2,1)S(1)} collective-permute-done((bf16[256,512]{1,0:T(8,128)(2,1)S(1)}, bf16[256,512]{1,0:T(8,128)(2,1)S(1)}, u32[]{:S(2)}, u32[]{:S(2)}) %collective-permute-start.7) | collective-permute-done | bytes 262176 | tf_op jit(solution)/shard_map/ppermute | solution.py:440
  31.1 2.9 %collective-permute-start.8 = (bf16[256,512]{1,0:T(8,128)(2,1)S(1)}, bf16[256,512]{1,0:T(8,128)(2,1)S(1)}, u32[]{:S(2)}, u32[]{:S(2)}) collective-permute-start(bf16[256,512]{1,0:T(8,128)(2,1)S(1)} %get-tuple-element.122.refs_0_), channel_id=1, source_target_pairs={{0,2},{1,3},{2,0},{3,1},{4,6},{5,7},{6,4},{7,5},{8,10},{9,11},{10,... | collective-permute-start | bytes 786440 | tf_op jit(solution)/shard_map/ppermute | solution.py:440
  34.0 0.7 collective-permute-start.13
  34.7 3.7 %collective-permute-done.9.refs_10_ = bf16[256,512]{1,0:T(8,128)(2,1)S(1)} collective-permute-done((bf16[256,512]{1,0:T(8,128)(2,1)S(1)}, bf16[256,512]{1,0:T(8,128)(2,1)S(1)}, u32[]{:S(2)}, u32[]{:S(2)}) %collective-permute-start.9) | collective-permute-done | bytes 262176 | tf_op jit(solution)/shard_map/ppermute | solution.py:446
  38.5 2.4 %collective-permute-done.8.refs_2_ = bf16[256,512]{1,0:T(8,128)(2,1)S(1)} collective-permute-done((bf16[256,512]{1,0:T(8,128)(2,1)S(1)}, bf16[256,512]{1,0:T(8,128)(2,1)S(1)}, u32[]{:S(2)}, u32[]{:S(2)}) %collective-permute-start.8) | collective-permute-done | bytes 262176 | tf_op jit(solution)/shard_map/ppermute | solution.py:440
  41.0 0.4 collective-permute-start.12
  41.4 1.0 %collective-permute-done.11.refs_1_ = bf16[256,512]{1,0:T(8,128)(2,1)S(1)} collective-permute-done((bf16[256,512]{1,0:T(8,128)(2,1)S(1)}, bf16[256,512]{1,0:T(8,128)(2,1)S(1)}, u32[]{:S(2)}, u32[]{:S(2)}) %collective-permute-start.11) | collective-permute-done | bytes 262176 | tf_op jit(solution)/shard_map/ppermute | solution.py:440
  42.5 0.4 collective-permute-done.12.refs_3_
  42.8 3.3 %shard_map.180 = (f32[512,512]{1,0:T(8,128)S(1)}, f32[512,512]{1,0:T(8,128)S(1)}, bf16[512,512]{1,0:T(8,128)(2,1)S(1)}, bf16[1024,512]{1,0:T(8,128)(2,1)S(1)}, f...) custom-call(f32[8,512]{1,0:T(8,128)S(1)} %get-tuple-element.117.bias_row, ...), custom_call_target="tpu_custom_call" | custom-call | flops 1000 | bytes 1000 | tf_op jit(solution)/shard_map/pallas_call | solution.py:24
  46.3 1.4 %shard_map.181 = (f32[128,512]{1,0:T(8,128)S(1)}, f32[128,512]{1,0:T(8,128)S(1)}, bf16[256,512]{1,0:T(8,128)(2,1)S(1)}, bf16[256,512]{1,0:T(8,128)(2,1)S(1)}, bf...) custom-call(f32[512,512]{1,0:T(8,128)S(1)} %get-tuple-element.132.total_up, ...), custom_call_target="tpu_custom_call" | custom-call | flops 1000 | bytes 1000 | tf_op jit(solution)/shard_map/pallas_call | solution.py:24
  47.7 0.4 collective-permute-start.17
  48.4 2.4 %collective-permute-start.16 = (bf16[256,512]{1,0:T(8,128)(2,1)S(1)}, bf16[256,512]{1,0:T(8,128)(2,1)S(1)}, u32[]{:S(2)}, u32[]{:S(2)}) collective-permute-start(bf16[256,512]{1,0:T(8,128)(2,1)S(1)} %slice.123), channel_id=1, source_target_pairs={{0,2},{1,3},{2,0},{3,1},{4,6},{5,7},{6,4},{7,5},{8,10},{9,11},{10,... | collective-permute-start | bytes 786440 | tf_op jit(solution)/shard_map/ppermute | solution.py:440
  50.8 1.9 %collective-permute-start.20 = (bf16[256,512]{1,0:T(8,128)(2,1)S(1)}, bf16[256,512]{1,0:T(8,128)(2,1)S(1)}, u32[]{:S(2)}, u32[]{:S(2)}) collective-permute-start(bf16[256,512]{1,0:T(8,128)(2,1)S(1)} %get-tuple-element.149), channel_id=1, source_target_pairs={{0,4},{1,5},{2,6},{3,7},{4,8},{5,9},{6,10},{7,11},{8,12},{9,13},{1... | collective-permute-start | bytes 786440 | tf_op jit(solution)/shard_map/ppermute | solution.py:446
  52.7 2.0 %collective-permute-start.21 = (bf16[256,512]{1,0:T(8,128)(2,1)S(1)}, bf16[256,512]{1,0:T(8,128)(2,1)S(1)}, u32[]{:S(2)}, u32[]{:S(2)}) collective-permute-start(bf16[256,512]{1,0:T(8,128)(2,1)S(1)} %get-tuple-element.150), channel_id=1, source_target_pairs={{0,12},{1,13},{2,14},{3,15},{4,0},{5,1},{6,2},{7,3},{8,4},{9,5},{1... | collective-permute-start | bytes 786440 | tf_op jit(solution)/shard_map/ppermute | solution.py:446
  54.7 2.6 %collective-permute-done.16.refs_1_ = bf16[256,512]{1,0:T(8,128)(2,1)S(1)} collective-permute-done((bf16[256,512]{1,0:T(8,128)(2,1)S(1)}, bf16[256,512]{1,0:T(8,128)(2,1)S(1)}, u32[]{:S(2)}, u32[]{:S(2)}) %collective-permute-start.16) | collective-permute-done | bytes 262176 | tf_op jit(solution)/shard_map/ppermute | solution.py:440
  57.5 1.8 %collective-permute-start.19 = (bf16[256,512]{1,0:T(8,128)(2,1)S(1)}, bf16[256,512]{1,0:T(8,128)(2,1)S(1)}, u32[]{:S(2)}, u32[]{:S(2)}) collective-permute-start(bf16[256,512]{1,0:T(8,128)(2,1)S(1)} %slice.122), channel_id=1, source_target_pairs={{0,2},{1,3},{2,0},{3,1},{4,6},{5,7},{6,4},{7,5},{8,10},{9,11},{10,... | collective-permute-start | bytes 786440 | tf_op jit(solution)/shard_map/ppermute | solution.py:440
  59.7 2.7 %shard_map.183 = f32[4,64,128]{2,1,0:T(8,128)S(1)} custom-call(bf16[4,64,512]{2,1,0:T(8,128)(2,1)S(1)} %get-tuple-element.155.dconv, bf16[4,64,512]{2,1,0:T(8,128)(2,1)S(1)} %copy-done.1, bf16[4,64,512]{2,1,0:T(8,128)(2,1)S(1)} %collective-permute-done.outer, bf16[4,64,512]{2,1,0:T(8,128)(2,1)S(1)} %collective-permute-done.1.inner, ...), custom_call_target="tpu_custom_call" | custom-call | flops 1000 | bytes 1000 | tf_op jit(solution)/shard_map/pallas_call | solution.py:24
  62.5 0.7 collective-permute-start.23
  63.2 0.6 collective-permute-done.18
  63.9 2.4 %collective-permute-done.21.refs_4_ = bf16[256,512]{1,0:T(8,128)(2,1)S(1)} collective-permute-done((bf16[256,512]{1,0:T(8,128)(2,1)S(1)}, bf16[256,512]{1,0:T(8,128)(2,1)S(1)}, u32[]{:S(2)}, u32[]{:S(2)}) %collective-permute-start.21) | collective-permute-done | bytes 262176 | tf_op jit(solution)/shard_map/ppermute | solution.py:446
  66.3 0.7 collective-permute-start.26
  66.9 3.4 %collective-permute-start.22 = (f32[4,64,128]{2,1,0:T(8,128)S(1)}, f32[4,64,128]{2,1,0:T(8,128)S(1)}, u32[]{:S(2)}, u32[]{:S(2)}) collective-permute-start(f32[4,64,128]{2,1,0:T(8,128)S(1)} %add.40), channel_id=1, source_target_pairs={{0,2},{1,3},{2,0},{3,1},{4,6},{5,7},{6,4},{7,5},{8,10},{9,11},{10,... | collective-permute-start | bytes 393224 | tf_op jit(solution)/shard_map/ppermute | solution.py:440
  70.5 0.8 add_convert_fusion
  71.2 6.2 %collective-permute-done.22 = f32[4,64,128]{2,1,0:T(8,128)S(1)} collective-permute-done((f32[4,64,128]{2,1,0:T(8,128)S(1)}, f32[4,64,128]{2,1,0:T(8,128)S(1)}, u32[]{:S(2)}, u32[]{:S(2)}) %collective-permute-start.22) | collective-permute-done | bytes 131104 | tf_op jit(solution)/shard_map/ppermute | solution.py:440
  77.5 0.4 collective-permute-done.23.refs_3_
  77.8 1.1 %collective-permute-start.25 = (f32[2,64,128]{2,1,0:T(8,128)S(1)}, f32[2,64,128]{2,1,0:T(8,128)S(1)}, u32[]{:S(2)}, u32[]{:S(2)}) collective-permute-start(f32[2,64,128]{2,1,0:T(8,128)S(1)} %slice.89), channel_id=1, source_target_pairs={{0,8},{1,9},{2,10},{3,11},{4,12},{5,13},{6,14},{7,15},{8,0},{9,1},... | collective-permute-start | bytes 196616 | tf_op jit(solution)/shard_map/ppermute | solution.py:454
  78.9 0.8 shard_map.185
  79.7 2.5 %collective-permute-start.27 = (bf16[64,512]{1,0:T(8,128)(2,1)S(1)}, bf16[64,512]{1,0:T(8,128)(2,1)S(1)}, u32[]{:S(2)}, u32[]{:S(2)}) collective-permute-start(bf16[64,512]{1,0:T(8,128)(2,1)S(1)} %pad_maximum_fusion.2), channel_id=1, source_target_pairs={{0,2},{1,3},{2,0},{3,1},{4,6},{5,7},{6,4},{7,5},{8,10},{9,11},{10,... | collective-permute-start | bytes 196616 | tf_op jit(solution)/shard_map/ppermute | solution.py:440
  82.2 3.1 %shard_map.184 = bf16[4,64,512]{2,1,0:T(8,128)(2,1)} custom-call(bf16[4,64,512]{2,1,0:T(8,128)(2,1)S(1)} %get-tuple-element.155.dconv, bf16[4,64,512]{2,1,0:T(8,128)(2,1)S(1)} %collective-permute-done.26.outer, bf16[4,64,512]{2,1,0:T(8,128)(2,1)S(1)} %collective-permute-done.24.inner, bf16[4,64,512]{2,1,0:T(8,128)(2,1)S(1)} %copy-done, ...), custom_call_target="tpu_custom_call" | custom-call | flops 1000 | bytes 1000 | tf_op jit(solution)/shard_map/pallas_call | solution.py:24
  85.4 2.0 %collective-permute-start.29 = (f32[64,128]{1,0:T(8,128)S(1)}, f32[64,128]{1,0:T(8,128)S(1)}, u32[]{:S(2)}, u32[]{:S(2)}) collective-permute-start(f32[64,128]{1,0:T(8,128)S(1)} %get-tuple-element.188), channel_id=1, source_target_pairs={{0,4},{1,5},{2,6},{3,7},{4,0},{5,1},{6,2},{7,3},{8,12},{9,13},{10,... | collective-permute-start | bytes 98312 | tf_op jit(solution)/shard_map/ppermute | solution.py:454
  87.5 0.8 shard_map.186
  88.2 1.2 %collective-permute-done.29.refs_1_ = f32[64,128]{1,0:T(8,128)S(1)} collective-permute-done((f32[64,128]{1,0:T(8,128)S(1)}, f32[64,128]{1,0:T(8,128)S(1)}, u32[]{:S(2)}, u32[]{:S(2)}) %collective-permute-start.29) | collective-permute-done | bytes 32800 | tf_op jit(solution)/shard_map/ppermute | solution.py:454
  89.4 0.9 shard_map.187
  (60 shorter events, 1.6 us)
Async XLA Ops:
  2.5 5.7 %copy-start.5 = (bf16[64,128]{1,0:T(8,128)(2,1)S(1)}, bf16[64,128]{1,0:T(8,128)(2,1)}, u32[]{:S(2)}) copy-start(bf16[64,128]{1,0:T(8,128)(2,1)} %get-tuple-element.97) | copy-start | bytes 49156
  2.5 5.7 %collective-permute-start.2 = (bf16[320,128]{1,0:T(8,128)(2,1)}, bf16[320,128]{1,0:T(8,128)(2,1)S(1)}, u32[]{:S(2)}, u32[]{:S(2)}) collective-permute-start(bf16[320,128]{1,0:T(8,128)(2,1)} %get-tuple-element.99), channel_id=1, source_target_pairs={{0,2},{1,3},{2,0},{3,1},{4,6},{5,7},{6,4},{7,5},{8,10},{9,11},{10,... | collective-permute-start | bytes 245768 | tf_op jit(solution)/shard_map/ppermute | solution.py:440
  8.2 0.8 copy-start.4
  9.0 3.5 %copy-start.2 = (bf16[128,512]{1,0:T(8,128)(2,1)S(1)}, bf16[128,512]{1,0:T(8,128)(2,1)}, u32[]{:S(2)}) copy-start(bf16[128,512]{1,0:T(8,128)(2,1)} %down) | copy-start | bytes 393220
  9.0 1.3 %collective-permute-start.3 = (bf16[320,128]{1,0:T(8,128)(2,1)S(1)}, bf16[320,128]{1,0:T(8,128)(2,1)S(1)}, u32[]{:S(2)}, u32[]{:S(2)}) collective-permute-start(bf16[320,128]{1,0:T(8,128)(2,1)S(1)} %pad_maximum_fusion), channel_id=1, source_target_pairs={{0,1},{1,0},{2,3},{3,2},{4,5},{5,4},{6,7},{7,6},{8,9},{9,8},{10,11... | collective-permute-start | bytes 245768 | tf_op jit(solution)/shard_map/ppermute | solution.py:440
  10.4 2.2 %copy-start.3 = (bf16[128,128]{1,0:T(8,128)(2,1)S(1)}, bf16[128,128]{1,0:T(8,128)(2,1)}, u32[]{:S(2)}) copy-start(bf16[128,128]{1,0:T(8,128)(2,1)} %get-tuple-element.109.refs_0_) | copy-start | bytes 98308
  10.4 6.9 %copy-start.1 = (bf16[4,64,512]{2,1,0:T(8,128)(2,1)S(1)}, bf16[4,64,512]{2,1,0:T(8,128)(2,1)}, u32[]{:S(2)}) copy-start(bf16[4,64,512]{2,1,0:T(8,128)(2,1)} %features.1) | copy-start | bytes 786436
  10.4 10.5 %copy-start = (bf16[4,64,512]{2,1,0:T(8,128)(2,1)S(1)}, bf16[4,64,512]{2,1,0:T(8,128)(2,1)}, u32[]{:S(2)}) copy-start(bf16[4,64,512]{2,1,0:T(8,128)(2,1)} %cotangent.1) | copy-start | bytes 786436
  10.4 3.8 %collective-permute-start.4 = (bf16[64,128]{1,0:T(8,128)(2,1)S(1)}, bf16[64,128]{1,0:T(8,128)(2,1)S(1)}, u32[]{:S(2)}, u32[]{:S(2)}) collective-permute-start(bf16[64,128]{1,0:T(8,128)(2,1)S(1)} %slice_add_fusion.2), channel_id=1, source_target_pairs={{0,4},{1,5},{2,6},{3,7},{4,0},{5,1},{6,2},{7,3},{8,12},{9,13},{10,... | collective-permute-start | bytes 49160 | tf_op jit(solution)/shard_map/ppermute | solution.py:454
  12.6 11.4 %collective-permute-start.6 = (bf16[256,512]{1,0:T(8,128)(2,1)S(1)}, bf16[256,512]{1,0:T(8,128)(2,1)S(1)}, u32[]{:S(2)}, u32[]{:S(2)}) collective-permute-start(bf16[256,512]{1,0:T(8,128)(2,1)S(1)} %bitcast.24), channel_id=1, source_target_pairs={{0,4},{1,5},{2,6},{3,7},{4,8},{5,9},{6,10},{7,11},{8,12},{9,13},{1... | collective-permute-start | bytes 786440 | tf_op jit(solution)/shard_map/ppermute | solution.py:446
  14.2 9.7 %collective-permute-start.5 = (bf16[128,128]{1,0:T(8,128)(2,1)S(1)}, bf16[128,128]{1,0:T(8,128)(2,1)S(1)}, u32[]{:S(2)}, u32[]{:S(2)}) collective-permute-start(bf16[128,128]{1,0:T(8,128)(2,1)S(1)} %pad_maximum_fusion.4), channel_id=1, source_target_pairs={{0,8},{1,9},{2,10},{3,11},{4,12},{5,13},{6,14},{7,15},{8,0},{9,1},... | collective-permute-start | bytes 98312 | tf_op jit(solution)/shard_map/ppermute | solution.py:454
  17.3 9.0 %collective-permute-start = (bf16[4,64,512]{2,1,0:T(8,128)(2,1)S(1)}, bf16[4,64,512]{2,1,0:T(8,128)(2,1)S(1)}, u32[]{:S(2)}, u32[]{:S(2)}) collective-permute-start(bf16[4,64,512]{2,1,0:T(8,128)(2,1)S(1)} %copy-done.1), channel_id=1, source_target_pairs={{1,2},{3,4},{5,6},{7,8},{9,10},{11,12},{13,14},{2,1},{4,3},{6,5},{... | collective-permute-start | bytes 786440 | tf_op jit(solution)/shard_map/ppermute | solution.py:451
  17.9 8.4 %collective-permute-start.1 = (bf16[4,64,512]{2,1,0:T(8,128)(2,1)S(1)}, bf16[4,64,512]{2,1,0:T(8,128)(2,1)S(1)}, u32[]{:S(2)}, u32[]{:S(2)}) collective-permute-start(bf16[4,64,512]{2,1,0:T(8,128)(2,1)S(1)} %copy-done.1), channel_id=1, source_target_pairs={{0,1},{1,0},{2,3},{3,2},{4,5},{5,4},{6,7},{7,6},{8,9},{9,8},{10,11... | collective-permute-start | bytes 786440 | tf_op jit(solution)/shard_map/ppermute | solution.py:440
  20.9 10.2 %collective-permute-start.7 = (bf16[256,512]{1,0:T(8,128)(2,1)S(1)}, bf16[256,512]{1,0:T(8,128)(2,1)S(1)}, u32[]{:S(2)}, u32[]{:S(2)}) collective-permute-start(bf16[256,512]{1,0:T(8,128)(2,1)S(1)} %bitcast.20), channel_id=1, source_target_pairs={{0,2},{1,3},{2,0},{3,1},{4,6},{5,7},{6,4},{7,5},{8,10},{9,11},{10,... | collective-permute-start | bytes 786440 | tf_op jit(solution)/shard_map/ppermute | solution.py:440
  23.9 14.6 %collective-permute-start.9 = (bf16[256,512]{1,0:T(8,128)(2,1)S(1)}, bf16[256,512]{1,0:T(8,128)(2,1)S(1)}, u32[]{:S(2)}, u32[]{:S(2)}) collective-permute-start(bf16[256,512]{1,0:T(8,128)(2,1)S(1)} %bitcast.25), channel_id=1, source_target_pairs={{0,8},{1,9},{2,10},{3,11},{4,12},{5,13},{6,14},{7,15},{8,0},{9,1},... | collective-permute-start | bytes 786440 | tf_op jit(solution)/shard_map/ppermute | solution.py:446
  23.9 14.6 %collective-permute-start.10 = (bf16[256,512]{1,0:T(8,128)(2,1)S(1)}, bf16[256,512]{1,0:T(8,128)(2,1)S(1)}, u32[]{:S(2)}, u32[]{:S(2)}) collective-permute-start(bf16[256,512]{1,0:T(8,128)(2,1)S(1)} %bitcast.26), channel_id=1, source_target_pairs={{0,12},{1,13},{2,14},{3,15},{4,0},{5,1},{6,2},{7,3},{8,4},{9,5},{1... | collective-permute-start | bytes 786440 | tf_op jit(solution)/shard_map/ppermute | solution.py:446
  31.1 9.8 %collective-permute-start.8 = (bf16[256,512]{1,0:T(8,128)(2,1)S(1)}, bf16[256,512]{1,0:T(8,128)(2,1)S(1)}, u32[]{:S(2)}, u32[]{:S(2)}) collective-permute-start(bf16[256,512]{1,0:T(8,128)(2,1)S(1)} %get-tuple-element.122.refs_0_), channel_id=1, source_target_pairs={{0,2},{1,3},{2,0},{3,1},{4,6},{5,7},{6,4},{7,5},{8,10},{9,11},{10,... | collective-permute-start | bytes 786440 | tf_op jit(solution)/shard_map/ppermute | solution.py:440
  34.0 7.4 %collective-permute-start.13 = (bf16[256,512]{1,0:T(8,128)(2,1)S(1)}, bf16[256,512]{1,0:T(8,128)(2,1)S(1)}, u32[]{:S(2)}, u32[]{:S(2)}) collective-permute-start(bf16[256,512]{1,0:T(8,128)(2,1)S(1)} %bitcast.21), channel_id=1, source_target_pairs={{0,1},{1,0},{2,3},{3,2},{4,5},{5,4},{6,7},{7,6},{8,9},{9,8},{10,11... | collective-permute-start | bytes 786440 | tf_op jit(solution)/shard_map/ppermute | solution.py:440
  34.7 6.7 %collective-permute-start.14 = (bf16[256,512]{1,0:T(8,128)(2,1)S(1)}, bf16[256,512]{1,0:T(8,128)(2,1)S(1)}, u32[]{:S(2)}, u32[]{:S(2)}) collective-permute-start(bf16[256,512]{1,0:T(8,128)(2,1)S(1)} %collective-permute-done.7.refs_6_.refs_2_), channel_id=1, source_target_pairs={{0,1},{1,0},{2,3},{3,2},{4,5},{5,4},{6,7},{7,6},{8,9},{9,8},{10,11... | collective-permute-start | bytes 786440 | tf_op jit(solution)/shard_map/ppermute | solution.py:440
  40.9 1.5 %collective-permute-start.11 = (bf16[256,512]{1,0:T(8,128)(2,1)S(1)}, bf16[256,512]{1,0:T(8,128)(2,1)S(1)}, u32[]{:S(2)}, u32[]{:S(2)}) collective-permute-start(bf16[256,512]{1,0:T(8,128)(2,1)S(1)} %get-tuple-element.122.refs_0_), channel_id=1, source_target_pairs={{0,1},{1,0},{2,3},{3,2},{4,5},{5,4},{6,7},{7,6},{8,9},{9,8},{10,11... | collective-permute-start | bytes 786440 | tf_op jit(solution)/shard_map/ppermute | solution.py:440
  41.0 1.8 %collective-permute-start.12 = (bf16[256,512]{1,0:T(8,128)(2,1)S(1)}, bf16[256,512]{1,0:T(8,128)(2,1)S(1)}, u32[]{:S(2)}, u32[]{:S(2)}) collective-permute-start(bf16[256,512]{1,0:T(8,128)(2,1)S(1)} %collective-permute-done.8.refs_2_), channel_id=1, source_target_pairs={{0,1},{1,0},{2,3},{3,2},{4,5},{5,4},{6,7},{7,6},{8,9},{9,8},{10,11... | collective-permute-start | bytes 786440 | tf_op jit(solution)/shard_map/ppermute | solution.py:440
  46.1 2.1 %collective-permute-start.15 = (bf16[512,512]{1,0:T(8,128)(2,1)S(1)}, bf16[512,512]{1,0:T(8,128)(2,1)S(1)}, u32[]{:S(2)}, u32[]{:S(2)}) collective-permute-start(bf16[512,512]{1,0:T(8,128)(2,1)S(1)} %get-tuple-element.131), channel_id=1, source_target_pairs={{0,1},{1,0},{2,3},{3,2},{4,5},{5,4},{6,7},{7,6},{8,9},{9,8},{10,11... | collective-permute-start | bytes 1572872 | tf_op jit(solution)/shard_map/ppermute | solution.py:440
  47.7 7.0 %collective-permute-start.17 = (bf16[512,512]{1,0:T(8,128)(2,1)S(1)}, bf16[512,512]{1,0:T(8,128)(2,1)S(1)}, u32[]{:S(2)}, u32[]{:S(2)}) collective-permute-start(bf16[512,512]{1,0:T(8,128)(2,1)S(1)} %get-tuple-element.141), channel_id=1, source_target_pairs={{0,1},{1,0},{2,3},{3,2},{4,5},{5,4},{6,7},{7,6},{8,9},{9,8},{10,11... | collective-permute-start | bytes 1572872 | tf_op jit(solution)/shard_map/ppermute | solution.py:440
  48.4 9.0 %collective-permute-start.16 = (bf16[256,512]{1,0:T(8,128)(2,1)S(1)}, bf16[256,512]{1,0:T(8,128)(2,1)S(1)}, u32[]{:S(2)}, u32[]{:S(2)}) collective-permute-start(bf16[256,512]{1,0:T(8,128)(2,1)S(1)} %slice.123), channel_id=1, source_target_pairs={{0,2},{1,3},{2,0},{3,1},{4,6},{5,7},{6,4},{7,5},{8,10},{9,11},{10,... | collective-permute-start | bytes 786440 | tf_op jit(solution)/shard_map/ppermute | solution.py:440
  50.8 13.1 %collective-permute-start.20 = (bf16[256,512]{1,0:T(8,128)(2,1)S(1)}, bf16[256,512]{1,0:T(8,128)(2,1)S(1)}, u32[]{:S(2)}, u32[]{:S(2)}) collective-permute-start(bf16[256,512]{1,0:T(8,128)(2,1)S(1)} %get-tuple-element.149), channel_id=1, source_target_pairs={{0,4},{1,5},{2,6},{3,7},{4,8},{5,9},{6,10},{7,11},{8,12},{9,13},{1... | collective-permute-start | bytes 786440 | tf_op jit(solution)/shard_map/ppermute | solution.py:446
  52.7 13.6 %collective-permute-start.21 = (bf16[256,512]{1,0:T(8,128)(2,1)S(1)}, bf16[256,512]{1,0:T(8,128)(2,1)S(1)}, u32[]{:S(2)}, u32[]{:S(2)}) collective-permute-start(bf16[256,512]{1,0:T(8,128)(2,1)S(1)} %get-tuple-element.150), channel_id=1, source_target_pairs={{0,12},{1,13},{2,14},{3,15},{4,0},{5,1},{6,2},{7,3},{8,4},{9,5},{1... | collective-permute-start | bytes 786440 | tf_op jit(solution)/shard_map/ppermute | solution.py:446
  57.5 8.7 %collective-permute-start.19 = (bf16[256,512]{1,0:T(8,128)(2,1)S(1)}, bf16[256,512]{1,0:T(8,128)(2,1)S(1)}, u32[]{:S(2)}, u32[]{:S(2)}) collective-permute-start(bf16[256,512]{1,0:T(8,128)(2,1)S(1)} %slice.122), channel_id=1, source_target_pairs={{0,2},{1,3},{2,0},{3,1},{4,6},{5,7},{6,4},{7,5},{8,10},{9,11},{10,... | collective-permute-start | bytes 786440 | tf_op jit(solution)/shard_map/ppermute | solution.py:440
  62.4 1.4 %collective-permute-start.18 = (f32[4,64,128]{2,1,0:T(8,128)S(1)}, f32[4,64,128]{2,1,0:T(8,128)S(1)}, u32[]{:S(2)}, u32[]{:S(2)}) collective-permute-start(f32[4,64,128]{2,1,0:T(8,128)S(1)} %shard_map.183), channel_id=1, source_target_pairs={{0,1},{1,0},{2,3},{3,2},{4,5},{5,4},{6,7},{7,6},{8,9},{9,8},{10,11... | collective-permute-start | bytes 393224 | tf_op jit(solution)/shard_map/ppermute | solution.py:440
  62.5 15.3 %collective-permute-start.23 = (bf16[256,512]{1,0:T(8,128)(2,1)S(1)}, bf16[256,512]{1,0:T(8,128)(2,1)S(1)}, u32[]{:S(2)}, u32[]{:S(2)}) collective-permute-start(bf16[256,512]{1,0:T(8,128)(2,1)S(1)} %get-tuple-element.153), channel_id=1, source_target_pairs={{0,8},{1,9},{2,10},{3,11},{4,12},{5,13},{6,14},{7,15},{8,0},{9,1},... | collective-permute-start | bytes 786440 | tf_op jit(solution)/shard_map/ppermute | solution.py:446
  66.3 11.6 %collective-permute-start.24 = (bf16[4,64,512]{2,1,0:T(8,128)(2,1)S(1)}, bf16[4,64,512]{2,1,0:T(8,128)(2,1)S(1)}, u32[]{:S(2)}, u32[]{:S(2)}) collective-permute-start(bf16[4,64,512]{2,1,0:T(8,128)(2,1)S(1)} %get-tuple-element.155.dconv), channel_id=1, source_target_pairs={{0,1},{1,0},{2,3},{3,2},{4,5},{5,4},{6,7},{7,6},{8,9},{9,8},{10,11... | collective-permute-start | bytes 786440 | tf_op jit(solution)/shard_map/ppermute | solution.py:440
  66.3 15.9 %collective-permute-start.26 = (bf16[4,64,512]{2,1,0:T(8,128)(2,1)S(1)}, bf16[4,64,512]{2,1,0:T(8,128)(2,1)S(1)}, u32[]{:S(2)}, u32[]{:S(2)}) collective-permute-start(bf16[4,64,512]{2,1,0:T(8,128)(2,1)S(1)} %get-tuple-element.155.dconv), channel_id=1, source_target_pairs={{1,2},{3,4},{5,6},{7,8},{9,10},{11,12},{13,14},{2,1},{4,3},{6,5},{... | collective-permute-start | bytes 786440 | tf_op jit(solution)/shard_map/ppermute | solution.py:451
  66.9 10.5 %collective-permute-start.22 = (f32[4,64,128]{2,1,0:T(8,128)S(1)}, f32[4,64,128]{2,1,0:T(8,128)S(1)}, u32[]{:S(2)}, u32[]{:S(2)}) collective-permute-start(f32[4,64,128]{2,1,0:T(8,128)S(1)} %add.40), channel_id=1, source_target_pairs={{0,2},{1,3},{2,0},{3,1},{4,6},{5,7},{6,4},{7,5},{8,10},{9,11},{10,... | collective-permute-start | bytes 393224 | tf_op jit(solution)/shard_map/ppermute | solution.py:440
  77.8 7.4 %collective-permute-start.25 = (f32[2,64,128]{2,1,0:T(8,128)S(1)}, f32[2,64,128]{2,1,0:T(8,128)S(1)}, u32[]{:S(2)}, u32[]{:S(2)}) collective-permute-start(f32[2,64,128]{2,1,0:T(8,128)S(1)} %slice.89), channel_id=1, source_target_pairs={{0,8},{1,9},{2,10},{3,11},{4,12},{5,13},{6,14},{7,15},{8,0},{9,1},... | collective-permute-start | bytes 196616 | tf_op jit(solution)/shard_map/ppermute | solution.py:454
  79.7 5.6 %collective-permute-start.27 = (bf16[64,512]{1,0:T(8,128)(2,1)S(1)}, bf16[64,512]{1,0:T(8,128)(2,1)S(1)}, u32[]{:S(2)}, u32[]{:S(2)}) collective-permute-start(bf16[64,512]{1,0:T(8,128)(2,1)S(1)} %pad_maximum_fusion.2), channel_id=1, source_target_pairs={{0,2},{1,3},{2,0},{3,1},{4,6},{5,7},{6,4},{7,5},{8,10},{9,11},{10,... | collective-permute-start | bytes 196616 | tf_op jit(solution)/shard_map/ppermute | solution.py:440
  85.3 2.1 %collective-permute-start.28 = (bf16[64,512]{1,0:T(8,128)(2,1)S(1)}, bf16[64,512]{1,0:T(8,128)(2,1)S(1)}, u32[]{:S(2)}, u32[]{:S(2)}) collective-permute-start(bf16[64,512]{1,0:T(8,128)(2,1)S(1)} %pad_maximum_fusion.3), channel_id=1, source_target_pairs={{0,1},{1,0},{2,3},{3,2},{4,5},{5,4},{6,7},{7,6},{8,9},{9,8},{10,11... | collective-permute-start | bytes 196616 | tf_op jit(solution)/shard_map/ppermute | solution.py:440
  85.4 4.0 %collective-permute-start.29 = (f32[64,128]{1,0:T(8,128)S(1)}, f32[64,128]{1,0:T(8,128)S(1)}, u32[]{:S(2)}, u32[]{:S(2)}) collective-permute-start(f32[64,128]{1,0:T(8,128)S(1)} %get-tuple-element.188), channel_id=1, source_target_pairs={{0,4},{1,5},{2,6},{3,7},{4,0},{5,1},{6,2},{7,3},{8,12},{9,13},{10,... | collective-permute-start | bytes 98312 | tf_op jit(solution)/shard_map/ppermute | solution.py:454
